TPU v7x, 32 devices: a whole 2x2x4 slice. The times are simulated.
32 devices in a mesh: groups: 2 (over y), gx: 4 (over x, core), gy: 4 (over z).
Axes of the slice: x: 2, y: 2, z: 4, core: 2. Of those that a mesh axis runs over, the one named last changes fastest.
Arguments:
- tokens: bfloat16 [2048, 16384], P(('groups', 'gy'), 'gx'), parts along dimension 0, may hold values from -1000 to 1000
- norm_gain: float32 [16384], P('gx'), may hold values from 0.1 to 1.9
- qkv_weight: bfloat16 [16384, 18432], P('gx', 'gy'), may hold values from -0.046875 to 0.046875
- out_weight: bfloat16 [16384, 16384], P('gy', 'gx'), may hold values from -1.5 to 1.5
- key_cache: bfloat16 [4, 3072, 1024], P('groups', None, 'gy'), parts along dimension 0, may hold values from -400 to 400
- value_cache: bfloat16 [4, 3072, 1024], P('groups', None, 'gy'), parts along dimension 0, may hold values from -6 to 6
- prefix_len: int32 [4], P('groups'), parts along dimension 0, may hold values from 512 to 3072, as said below
- stretch_len: int32 [4], P('groups'), parts along dimension 0, may hold values from 128 to 512, as said below
Outputs:
- block_output: bfloat16 [2048, 16384], P(('groups', 'gy'), 'gx'), parts along dimension 0
There are 2 independent parts, one for each index of `groups`. A program takes and returns all parts, laid end to end along the dimension named above; an argument that names none is the same for every part. Nothing has to cross between parts.
Inputs may be any that keep to these rules, and one draw needn't show every extreme that they name: `prefix_len`: one request in every draw has exactly 3072 cached positions. `stretch_len`: one request in every draw has all 512 tokens live.
All inputs are finite; a program needn't handle non-finite values.
Results may differ from a plain program's by a relative error of at most 0.012.
The roundings to bfloat16 on the way count: a program that leaves them out, or rounds other values in their place, can miss the bound.
Values may be sent and summed in bfloat16 or wider, within the bound.
No kernel may reach another device: no remote copies, remote signals or barrier semaphores. Data moves between devices by JAX's collectives and lax.ppermute only.
A program may use at most 448 MiB of HBM per device.

v0:
```python
import jax
import jax.numpy as jnp
from jax import lax
from jax.sharding import PartitionSpec as P

D = 16384
QH = 128
KVH = 8
HD = 128
STRETCH = 512


THETA = 500000.0
EPSILON = 1e-05


def rotate(values, positions):
    half = values.shape[-1] // 2
    freq = THETA ** (-(jnp.arange(half, dtype=jnp.float32) * 2.0) / values.shape[-1])
    angles = positions.astype(jnp.float32)[:, None] * freq[None, :]
    cosine = jnp.concatenate([jnp.cos(angles), jnp.cos(angles)], -1)[:, None, :]
    sine = jnp.concatenate([jnp.sin(angles), jnp.sin(angles)], -1)[:, None, :]
    turned = jnp.concatenate([-values[..., half:], values[..., :half]], -1)
    return values * cosine + turned * sine


def row_positions(row_ids, prefix_len):
    request = row_ids // STRETCH
    match = request[:, None] == jnp.arange(prefix_len.shape[0], dtype=jnp.int32)[None, :]
    start = jnp.sum(jnp.where(match, prefix_len[None, :], 0), axis=1)
    return start + row_ids % STRETCH


def attend(queries, offsets, cached_keys, cached_values, fresh_keys, fresh_values, prefix, live):
    keys = jnp.concatenate([cached_keys, fresh_keys], 0)
    values = jnp.concatenate([cached_values, fresh_values], 0)
    scores = jnp.dot(queries, keys.T, preferred_element_type=jnp.float32) * queries.shape[-1] ** (
        -0.5
    )
    span = cached_keys.shape[0]
    places = jnp.arange(keys.shape[0], dtype=jnp.int32)
    shifted = places - span
    allowed = jnp.where(
        (places < span)[None, :],
        (places < prefix)[None, :],
        (shifted[None, :] < live) & (shifted[None, :] <= offsets[:, None]),
    )
    scores = jnp.where(allowed, scores, -1e30)
    highest = jnp.max(scores, axis=1, keepdims=True)
    weights = jnp.where(allowed, jnp.exp(scores - highest), 0.0)
    total = jnp.sum(weights, axis=1, keepdims=True)
    probs = (weights / total).astype(jnp.bfloat16)
    return jnp.dot(probs, values, preferred_element_type=jnp.float32).astype(jnp.bfloat16)


def body(
    tokens, norm_gain, qkv_weight, out_weight, key_cache, value_cache, prefix_len, stretch_len
):
    group = QH // KVH
    index_gx = lax.axis_index("gx")
    whole = lax.all_gather(tokens, "gy", axis=0, tiled=True)
    widened = whole.astype(jnp.float32)
    squares = lax.psum(jnp.sum(widened * widened, axis=1), "gx")
    normed_all = (widened * lax.rsqrt(squares / D + EPSILON)[:, None] * norm_gain[None, :]).astype(
        jnp.bfloat16
    )
    total_rows = normed_all.shape[0]
    local_groups = qkv_weight.shape[1] // ((group + 2) * HD)
    requests = prefix_len.shape[0]
    projected = jnp.dot(normed_all, qkv_weight, preferred_element_type=jnp.float32)
    blocks = projected.reshape(total_rows, local_groups, group + 2, HD)
    query_part = blocks[:, :, :group].reshape(total_rows, local_groups * group * HD)
    pair_part = blocks[:, :, group:].reshape(total_rows, local_groups * 2 * HD)
    query_mine = lax.psum_scatter(query_part, "gx", scatter_dimension=1, tiled=True)
    pair_sums = lax.psum(pair_part, "gx")
    positions = row_positions(jnp.arange(total_rows, dtype=jnp.int32), prefix_len)
    pairs = pair_sums.reshape(total_rows, local_groups, 2, HD)
    fresh_keys = rotate(pairs[:, :, 0], positions).astype(jnp.bfloat16)
    fresh_values = pairs[:, :, 1].astype(jnp.bfloat16)
    heads_here = query_mine.shape[1] // HD
    queries = rotate(query_mine.reshape(total_rows, heads_here, HD), positions).astype(jnp.bfloat16)
    offsets = jnp.arange(STRETCH, dtype=jnp.int32)
    head_columns = []
    for head in range(heads_here):
        group_index = (index_gx * heads_here + head) // group
        request_rows = []
        for request in range(requests):
            lower = request * STRETCH
            upper = lower + STRETCH
            result = attend(
                queries[lower:upper, head],
                offsets,
                lax.dynamic_slice_in_dim(key_cache[request], group_index * HD, HD, 1),
                lax.dynamic_slice_in_dim(value_cache[request], group_index * HD, HD, 1),
                lax.dynamic_index_in_dim(fresh_keys[lower:upper], group_index, 1, keepdims=False),
                lax.dynamic_index_in_dim(fresh_values[lower:upper], group_index, 1, keepdims=False),
                prefix_len[request],
                stretch_len[request],
            )
            request_rows.append(result)
        head_columns.append(jnp.concatenate(request_rows, 0))
    local_out = jnp.concatenate(head_columns, 1)
    gathered_out = lax.all_gather(local_out, "gx", axis=1, tiled=True)
    summed = lax.psum_scatter(
        jnp.dot(gathered_out, out_weight, preferred_element_type=jnp.float32),
        "gy",
        scatter_dimension=0,
        tiled=True,
    )
    return summed.astype(jnp.bfloat16)


def solution(mesh):
    placed = (
        P(("groups", "gy"), "gx"),
        P("gx"),
        P("gx", "gy"),
        P("gy", "gx"),
        P("groups", None, "gy"),
        P("groups", None, "gy"),
        P("groups"),
        P("groups"),
    )
    return jax.shard_map(
        body, mesh=mesh, in_specs=placed, out_specs=P(("groups", "gy"), "gx"), check_vma=False
    )
```

profile of v0, /device:TPU:28, one launch (start us, length us, event | category | flops | bytes accessed | tf_op | source)
XLA Modules:
  0.0 986.1 jit_solution(7366145797393599078)
XLA Ops:
  7.3 149.4 %all-gather.3.cloned.1.call-done = bf16[1024,4096]{1,0:T(8,128)(2,1)} async-done(((bf16[256,4096]{1,0:T(8,128)(2,1)}), bf16[1024,4096]{1,0:T(8,128)(2,1)}) %all-gather.3.cloned.1.call-update) | async-done | bytes 8388624 | tf_op jit(solution)/shard_map/all_gather | solution.py:61
  156.7 5.1 fusion
  161.8 6.8 psum.14
  168.7 48.1 %fusion.3 = f32[1024,4608]{0,1:T(8,128)} fusion(bf16[4096,4608]{1,0:T(8,128)(2,1)} %param.10, bf16[1024,4096]{1,0:T(8,128)(2,1)} %all-gather.3.cloned.1.call-done, f32[4096]{0:T(1024)S(1)} %copy-done.108, f32[1024]{0:T(1024)S(1)} %add_rsqrt_fusion), kind=kOutput, calls=%fused_computation.5 | convolution fusion | flops 38671482880 | bytes 65032192 | tf_op jit(solution)/shard_map/dot_general | solution.py:70
  216.8 3.2 slice.114
  220.0 12.0 %slice.110 = f32[1024,2,16,128]{0,3,2,1:T(8,128)} slice(f32[1024,2,18,128]{0,3,2,1:T(8,128)} %bitcast.208), slice={[0:1024], [0:2], [0:16], [0:128]} | slice | bytes 33554432 | tf_op jit(solution)/shard_map/slice | solution.py:72
  241.5 5.4 dynamic-slice_bitcast_fusion
  247.1 5.0 dynamic-slice_bitcast_fusion.5
  252.1 19.5 %all-reduce.2.cloned.1.call-done = f32[1024,2,2,128]{0,3,2,1:T(8,128)} async-done(((f32[1024,2,2,128]{0,3,2,1:T(8,128)}), f32[1024,2,2,128]{0,3,2,1:T(8,128)}) %all-reduce.2.cloned.1.call-update) | async-done | bytes 2097168 | tf_op jit(solution)/shard_map/psum | solution.py:75
  311.7 88.9 %reduce-scatter.3.cloned.1.call-done = f32[1024,1024]{0,1:T(8,128)} async-done(((f32[1024,4096]{0,1:T(8,128)}), f32[1024,1024]{0,1:T(8,128)}) %reduce-scatter.3.cloned.1.call-update) | async-done | bytes 4194320 | tf_op jit(solution)/shard_map/reduce_scatter | solution.py:74
  400.6 2.9 slice_negate_fusion
  405.4 2.5 fusion.241
  408.0 6.5 fusion.256
  419.6 5.7 fusion.247
  425.3 5.7 fusion.254
  431.1 5.8 fusion.246
  436.9 6.0 fusion.253
  442.9 5.8 fusion.245
  448.7 5.8 fusion.252
  454.6 5.8 fusion.244
  460.3 5.8 fusion.251
  466.2 5.8 fusion.243
  471.9 6.2 fusion.250
  478.1 5.7 fusion.242
  483.8 5.8 fusion.249
  489.6 18.8 %fusion.26 = (f32[512]{0:T(512)}, f32[512]{0:T(512)S(1)}, f32[512]{0:T(512)}, f32[512]{0:T(512)S(1)}, f32[512]{0:T(512)S(1)}, /*index=5*/f32[512]{0:T(512)S(1)}, f32[512]{0:T(512)S(1)}) fusion(f32[512,3584]{1,0:T(8,128)S(1)} %get-tuple-element.104, f32[512]{0:T(512)S(1)} %get-tuple-element.103, s32[3584]{0:T(1024)S(1)} %iota_add_fusion, ...), kind=kLoop, calls=%fused_computation.76 | loop fusion | flops 44036608 | bytes 51433984 | tf_op jit(solution)/shard_map/reduce_sum | solution.py:51
  508.4 6.1 fusion.59
  514.7 17.3 %fusion.25 = (f32[512]{0:T(512)}, f32[512]{0:T(512)S(1)}, f32[512]{0:T(512)}, f32[512]{0:T(512)}, f32[512]{0:T(512)}, /*index=5*/f32[512]{0:T(512)}, f32[512]{0:T(512)}) fusion(f32[512,3584]{1,0:T(8,128)S(1)} %get-tuple-element.118, f32[512]{0:T(512)S(1)} %get-tuple-element.117, s32[3584]{0:T(1024)S(1)} %iota_add_fusion, pred[3584]{0:T(1024)(128)(4,1)S(1)} %copy-done.77, ...), kind=kLoop, calls=%fused_computation.75 | loop fusion | flops 44036608 | bytes 51433984 | tf_op jit(solution)/shard_map/reduce_sum | solution.py:51
  532.0 6.1 fusion.60
  538.9 6.4 fusion.23
  545.3 3.6 fusion.47
  548.9 3.6 fusion.48
  552.5 3.6 fusion.49
  556.2 3.7 fusion.51
  560.0 3.6 fusion.53
  563.6 2.9 fusion.55
  566.7 2.9 fusion.57
  569.7 3.1 fusion.45
  573.0 2.9 fusion.50
  576.1 2.9 fusion.52
  579.1 2.9 fusion.54
  582.2 3.3 fusion.56
  585.6 2.9 fusion.58
  588.7 2.9 fusion.46
  593.8 58.4 %all-gather.5.cloned.1.call-done = bf16[1024,4096]{1,0:T(8,128)(2,1)} async-done(((bf16[1024,1024]{1,0:T(8,128)(2,1)}), bf16[1024,4096]{1,0:T(8,128)(2,1)}) %all-gather.5.cloned.1.call-update) | async-done | bytes 8388624 | tf_op jit(solution)/shard_map/all_gather | solution.py:103
  652.2 43.2 %fusion.257 = f32[1024,4096]{1,0:T(8,128)} fusion(bf16[1024,4096]{1,0:T(8,128)(2,1)} %all-gather.5.cloned.1.call-done, bf16[4096,4096]{1,0:T(8,128)(2,1)} %param.11), kind=kOutput, calls=%fused_computation.399 | convolution fusion | flops 34359738368 | bytes 58720256 | tf_op jit(solution)/shard_map/dot_general | solution.py:105
  695.4 280.2 %reduce-scatter.5.cloned.1.call-done = f32[256,4096]{1,0:T(8,128)} async-done(((f32[1024,4096]{1,0:T(8,128)}), f32[256,4096]{1,0:T(8,128)}) %reduce-scatter.5.cloned.1.call-update) | async-done | bytes 4194320 | tf_op jit(solution)/shard_map/reduce_scatter | solution.py:104
  975.6 3.8 convert_element_type.158
  (365 shorter events, 60.5 us)
Async XLA Ops:
  6.5 150.2 %all-gather.3.cloned.1.call-start = ((), (), s32[]{:S(2)}) async-start(), calls=%async_computation.2 | async-start | bytes 10485760 | tf_op jit(solution)/shard_map/all_gather | solution.py:61
  7.3 161.4 %copy-start.108 = (f32[4096]{0:T(1024)S(1)}, f32[4096]{0:T(1024)}, u32[]{:S(2)}) copy-start(f32[4096]{0:T(1024)} %param.9) | copy-start | bytes 49156
  7.3 264.3 %all-reduce.2.cloned.1.call-start = ((), (), s32[]{:S(2)}) async-start(), calls=%async_computation.4 | async-start | bytes 4194304 | tf_op jit(solution)/shard_map/psum | solution.py:75
  219.9 180.7 %reduce-scatter.3.cloned.1.call-start = ((), (), s32[]{:S(2)}) async-start(), calls=%async_computation.3 | async-start | bytes 20971520 | tf_op jit(solution)/shard_map/reduce_scatter | solution.py:74
  232.0 420.2 %all-gather.5.cloned.1.call-start = ((), (), s32[]{:S(2)}) async-start(), calls=%async_computation.5 | async-start | bytes 10485760 | tf_op jit(solution)/shard_map/all_gather | solution.py:103
  407.9 81.7 %copy-start.3 = (f32[512,3584]{1,0:T(8,128)}, f32[512,3584]{1,0:T(8,128)S(1)}, u32[]{:S(2)}) copy-start(f32[512,3584]{1,0:T(8,128)S(1)} %get-tuple-element.104) | copy-start | bytes 22020100
  407.9 81.7 %copy-start.84 = (f32[512]{0:T(512)}, f32[512]{0:T(512)S(1)}, u32[]{:S(2)}) copy-start(f32[512]{0:T(512)S(1)} %get-tuple-element.103) | copy-start | bytes 6148
  407.9 6.5 copy-start.36
  407.9 6.5 copy-start.63
  407.9 6.5 copy-start.75
  407.9 6.5 copy-start.77
  417.0 97.6 %copy-start.2 = (f32[512,3584]{1,0:T(8,128)}, f32[512,3584]{1,0:T(8,128)S(1)}, u32[]{:S(2)}) copy-start(f32[512,3584]{1,0:T(8,128)S(1)} %get-tuple-element.118) | copy-start | bytes 22020100
  417.0 97.6 %copy-start.82 = (f32[512]{0:T(512)}, f32[512]{0:T(512)S(1)}, u32[]{:S(2)}) copy-start(f32[512]{0:T(512)S(1)} %get-tuple-element.117) | copy-start | bytes 6148
  431.1 83.5 %copy-start.86 = (f32[512]{0:T(512)}, f32[512]{0:T(512)S(1)}, u32[]{:S(2)}) copy-start(f32[512]{0:T(512)S(1)} %get-tuple-element.129) | copy-start | bytes 6148
  436.9 6.0 copy-start.30
  436.9 6.0 copy-start.64
  442.9 71.7 %copy-start.88 = (f32[512]{0:T(512)}, f32[512]{0:T(512)S(1)}, u32[]{:S(2)}) copy-start(f32[512]{0:T(512)S(1)} %get-tuple-element.127) | copy-start | bytes 6148
  442.9 5.8 copy-start.29
  454.5 60.1 %copy-start.90 = (f32[512]{0:T(512)}, f32[512]{0:T(512)S(1)}, u32[]{:S(2)}) copy-start(f32[512]{0:T(512)S(1)} %get-tuple-element.125) | copy-start | bytes 6148
  460.3 5.8 copy-start.26
  460.3 5.8 copy-start.60
  466.1 48.5 %copy-start.92 = (f32[512]{0:T(512)}, f32[512]{0:T(512)S(1)}, u32[]{:S(2)}) copy-start(f32[512]{0:T(512)S(1)} %get-tuple-element.123) | copy-start | bytes 6148
  471.9 17.7 %copy-start.96 = (f32[512]{0:T(512)}, f32[512]{0:T(512)S(1)}, u32[]{:S(2)}) copy-start(f32[512]{0:T(512)S(1)} %get-tuple-element.107) | copy-start | bytes 6148
  471.9 6.2 copy-start.24
  478.1 36.5 %copy-start.94 = (f32[512]{0:T(512)}, f32[512]{0:T(512)S(1)}, u32[]{:S(2)}) copy-start(f32[512]{0:T(512)S(1)} %get-tuple-element.121) | copy-start | bytes 6148
  489.6 18.8 %copy-start.22 = (bf16[3072,128]{1,0:T(8,128)(2,1)S(1)}, bf16[3072,128]{1,0:T(8,128)(2,1)}, u32[]{:S(2)}) copy-start(bf16[3072,128]{1,0:T(8,128)(2,1)} %get-tuple-element.42) | copy-start | bytes 2359300
  508.4 6.2 slice-start.6
  508.4 6.2 slice-start.7
  514.7 17.3 %copy-start.21 = (bf16[3072,128]{1,0:T(8,128)(2,1)S(1)}, bf16[3072,128]{1,0:T(8,128)(2,1)}, u32[]{:S(2)}) copy-start(bf16[3072,128]{1,0:T(8,128)(2,1)} %get-tuple-element.153) | copy-start | bytes 2359300
  514.7 17.3 %copy-start.59 = (bf16[512,1,1,128]{3,0,2,1:T(8,128)(2,1)S(1)}, bf16[512,1,1,128]{3,0,2,1:T(8,128)(2,1)}, u32[]{:S(2)}) copy-start(bf16[512,1,1,128]{3,0,2,1:T(8,128)(2,1)} %copy.96) | copy-start | bytes 393220
  532.0 6.9 slice-start
  532.0 6.9 slice-start.1
  532.0 6.9 copy-start.107
  538.9 6.4 copy-start.20
  538.9 6.4 copy-start.53
  545.3 7.2 slice-start.18
  548.9 7.2 slice-start.20
  552.5 7.4 slice-start.22
  556.2 7.4 slice-start.24
  560.0 6.6 slice-start.26
  563.6 6.0 slice-start.4
  566.7 6.2 slice-start.8
  569.7 6.2 slice-start.10
  573.0 6.0 slice-start.12
  576.0 6.0 slice-start.14
  579.1 6.4 slice-start.16
  582.2 6.4 slice-start.2
  593.7 381.8 %reduce-scatter.5.cloned.1.call-start = ((), (), s32[]{:S(2)}) async-start(), calls=%async_computation.6 | async-start | bytes 20971520 | tf_op jit(solution)/shard_map/reduce_scatter | solution.py:104
  (94 other events, 323.9 us)
Sparse Core Ops, SparseCore 0:
  8.9 147.7 all-gather.2
  220.1 51.4 all-reduce.1
  274.3 126.2 reduce-scatter.2
  593.8 58.2 all-gather.4
  695.5 280.0 reduce-scatter.4
where the time goes:
time: 995 us; the launch traced here: 986 us
  waiting for transfers between devices  597 us (60%)
  matrix products  232 us (23%)
  local copies, waits for them, and re-layouts  71.4 us (7%)
  other arithmetic  62.9 us (6%)
  between operations  15.4 us (2%)
    reduce_scatter x1, waiting for transfers between devices, body(): lax.psum_scatter(jnp.dot(gathered_out, out_weight, preferred_element_type...  280 us
    all_gather x1, waiting for transfers between devices, body(): whole = lax.all_gather(tokens, 'gy', axis=0, tiled=True)  149 us
    reduce_scatter x1, waiting for transfers between devices, body(): lax.psum_scatter(query_part, 'gx', scatter_dimension=1, tiled=True)  88.9 us
    dot_general x16, matrix products, attend(): jnp.dot(queries, keys.T, preferred_element_type=jnp.float32)  83.8 us
    all_gather x1, waiting for transfers between devices, body(): gathered_out = lax.all_gather(local_out, 'gx', axis=1, tiled=True)  58.4 us
    dot_general x16, matrix products, attend(): jnp.dot(probs, values, preferred_element_type=jnp.float32)  57.1 us
    dot_general x1, matrix products, body(): jnp.dot(normed_all, qkv_weight, preferred_element_type=jnp.float32)  48.1 us
    dot_general x1, matrix products, body(): jnp.dot(gathered_out, out_weight, preferred_element_type=jnp.float32)  43.2 us
  transfers between devices with their start and end apart: 5, of which 5 were waited for; matrix products, arithmetic and copies ran while one was open for 7% of the time, Pallas kernels for 0%

commit v1 on v0

--- a/solution.py
+++ b/solution.py
@@ -1,6 +1,10 @@
+import math
+
 import jax
 import jax.numpy as jnp
 from jax import lax
+from jax.experimental import pallas as pl
+from jax.experimental.pallas import tpu as pltpu
 from jax.sharding import PartitionSpec as P
 
 D = 16384
@@ -8,10 +12,735 @@
 KVH = 8
 HD = 128
 STRETCH = 512
-
+G = QH // KVH
 
 THETA = 500000.0
 EPSILON = 1e-05
+QSCALE = HD ** (-0.5) * math.log2(math.e)
+
+F32 = jnp.float32
+BF16 = jnp.bfloat16
+TILE = 256
+VMEM_LIMIT = 56 * 1024 * 1024
+
+
+HINT = pl.CostEstimate(flops=1024, bytes_accessed=1024, transcendentals=0)
+
+LONGER = pl.CostEstimate(flops=1024, bytes_accessed=2**25, transcendentals=0)
+
+
+def params(**kw):
+    return pltpu.CompilerParams(vmem_limit_bytes=VMEM_LIMIT, **kw)
+
+
+def sds(shape, dtype):
+    return jax.ShapeDtypeStruct(shape, dtype)
+
+
+def whole(*_):
+    return (0, 0)
+
+
+PER = 2
+
+
+def project_kernel(s_ref, *refs, sources):
+    x_refs, refs = refs[:sources], refs[sources:]
+    w_refs, (*peer_refs, own_ref, x_ref, sem) = refs[:PER], refs[PER:]
+    step = pl.program_id(0)
+    half = x_refs[0].shape[0]
+
+    def fetch(pair):
+        for i, ref in enumerate(pair):
+            pltpu.make_async_copy(ref, x_ref.at[pl.ds(i * half, half)], sem.at[i]).start()
+        for i, ref in enumerate(pair):
+            pltpu.make_async_copy(ref, x_ref.at[pl.ds(i * half, half)], sem.at[i]).wait()
+
+    @pl.when(step == 0)
+    def _():
+        if sources == 2:
+            fetch(x_refs)
+        else:
+
+            @pl.when(s_ref[0] == 1)
+            def _():
+                fetch(x_refs[:2])
+
+            @pl.when(s_ref[0] == 0)
+            def _():
+                fetch(x_refs[2:])
+
+    peer_steps = 10 // PER
+    products = [jnp.dot(x_ref[...], w[...], preferred_element_type=F32) for w in w_refs]
+
+    @pl.when(step < peer_steps)
+    def _():
+        for v, o_ref in zip(products, peer_refs):
+            o_ref[...] = v.astype(BF16)
+
+    @pl.when(step >= peer_steps)
+    def _():
+        for i, v in enumerate(products):
+            own_ref[:, i * TILE : (i + 1) * TILE] = v
+
+
+def project(info, xs, w):
+    half, depth = xs[0].shape
+    peer_steps = 10 // PER
+    steps = 18 // PER
+    weights = [
+        pl.BlockSpec((depth, TILE), lambda j, s, i=i: (0, s[1 + j * PER + i])) for i in range(PER)
+    ]
+    rows = 2 * half
+    return pl.pallas_call(
+        lambda *refs: project_kernel(*refs, sources=len(xs)),
+        grid_spec=pltpu.PrefetchScalarGridSpec(
+            num_scalar_prefetch=1,
+            grid=(steps,),
+            in_specs=[pl.BlockSpec(memory_space=pl.ANY)] * len(xs) + weights,
+            out_specs=[
+                pl.BlockSpec((rows, TILE), lambda j, s: (0, jnp.minimum(j, peer_steps - 1))),
+                pl.BlockSpec((rows, TILE), lambda j, s: (0, jnp.minimum(j, peer_steps - 1))),
+                pl.BlockSpec((rows, PER * TILE), lambda j, s: (0, jnp.maximum(j - peer_steps, 0))),
+            ],
+            scratch_shapes=[pltpu.VMEM((rows, depth), BF16), pltpu.SemaphoreType.DMA((2,))],
+        ),
+        out_shape=[sds((rows, 5 * TILE), BF16)] * 2 + [sds((rows, 8 * TILE), F32)],
+        compiler_params=params(),
+        cost_estimate=HINT,
+        name="project",
+    )(info, *xs, *([w] * PER))
+
+
+def core_sums(s_ref, own_ref, kv_refs, recv_refs):
+    n = recv_refs[0].shape[1]
+    first = s_ref[0] == 0
+    mine = jnp.where(first, kv_refs[0][...].astype(F32), kv_refs[1][...].astype(F32))
+    theirs = jnp.where(first, kv_refs[2][...].astype(F32), kv_refs[3][...].astype(F32))
+    halves = [
+        own_ref[:, i * n : (i + 1) * n] + r[...].astype(F32) for i, r in enumerate(recv_refs)
+    ]
+    return halves, mine + theirs
+
+
+def combine_kernel(s_ref, own_ref, kva_ref, kvb_ref, ra_ref, rb_ref, rka_ref, rkb_ref, o_ref):
+    halves, kv = core_sums(s_ref, own_ref, (kva_ref, kvb_ref, rka_ref, rkb_ref), (ra_ref, rb_ref))
+    n = ra_ref.shape[1]
+    for i, v in enumerate(halves):
+        o_ref[:, i * n : (i + 1) * n] = v.astype(BF16)
+    o_ref[:, 2 * n :] = kv.astype(BF16)
+
+
+def sums_specs(rows, n):
+    kv = pl.BlockSpec((rows, TILE), lambda i, s: (i, 4))
+    half = pl.BlockSpec((rows, n // 2), lambda i, s: (i, s[0]))
+    return [pl.BlockSpec((rows, n), lambda i, s: (i, s[0])), kv, kv, half, half, kv, kv]
+
+
+def combine(chip, own, mine, recv):
+    rows = own.shape[0]
+    n = own.shape[1] // 2
+    part = rows // 2
+    other = jnp.reshape(1 - chip, (1,)).astype(jnp.int32)
+    return pl.pallas_call(
+        combine_kernel,
+        grid_spec=pltpu.PrefetchScalarGridSpec(
+            num_scalar_prefetch=1,
+            grid=(rows // part,),
+            in_specs=sums_specs(part, n),
+            out_specs=pl.BlockSpec((part, n + TILE), lambda i, s: (i, 0)),
+        ),
+        out_shape=sds((rows, n + TILE), BF16),
+        compiler_params=params(),
+        cost_estimate=HINT,
+        name="combine",
+    )(other, own, *mine, *recv, *recv)
+
+
+def finish_kernel(s_ref, own_ref, kva_ref, kvb_ref, ra_ref, rb_ref, rka_ref, rkb_ref, *rest):
+    x_ref, cos_ref, sin_ref, q_ref, k_ref, v_ref = rest
+    halves, kv = core_sums(s_ref, own_ref, (kva_ref, kvb_ref, rka_ref, rkb_ref), (ra_ref, rb_ref))
+    n = ra_ref.shape[1]
+    cos, sin = cos_ref[...], sin_ref[...]
+
+    def turn(v):
+        return v * cos + pltpu.roll(v, HD // 2, 1) * sin
+
+    for i, half in enumerate(halves):
+        v = half + x_ref[:, i * n : (i + 1) * n].astype(F32)
+        for h in range(n // HD):
+            at = i * (n // HD) + h
+            q_ref[at] = (turn(v[:, h * HD : (h + 1) * HD]) * QSCALE).astype(BF16)
+    kv += x_ref[:, 2 * n :].astype(F32)
+    k_ref[...] = turn(kv[:, :HD]).astype(BF16)
+    v_ref[...] = kv[:, HD:].astype(BF16)
+
+
+def finish(chip, own, mine, recv, cross, cos, sin, slot):
+    rows = own.shape[0]
+    n = own.shape[1] // 2
+    part = rows // 2
+    here = jnp.reshape(chip, (1,)).astype(jnp.int32)
+    row = lambda i, s: (i, 0)
+    table = lambda i, s: (slot * (rows // part) + i, 0)
+    return pl.pallas_call(
+        finish_kernel,
+        grid_spec=pltpu.PrefetchScalarGridSpec(
+            num_scalar_prefetch=1,
+            grid=(rows // part,),
+            in_specs=sums_specs(part, n)
+            + [
+                pl.BlockSpec((part, n + TILE), row),
+                pl.BlockSpec((part, HD), table),
+                pl.BlockSpec((part, HD), table),
+            ],
+            out_specs=[
+                pl.BlockSpec((n // HD, part, HD), lambda i, s: (0, i, 0)),
+                pl.BlockSpec((part, HD), row),
+                pl.BlockSpec((part, HD), row),
+            ],
+        ),
+        out_shape=[sds((n // HD, rows, HD), BF16), sds((rows, HD), BF16), sds((rows, HD), BF16)],
+        compiler_params=params(),
+        cost_estimate=HINT,
+        name="finish",
+    )(here, own, *mine, *recv, *recv, cross, cos, sin)
+
+
+KB = 512
+CHUNK = 1024
+PIECE = 512
+LARGE = 2.0**100
+
+
+def attend_kernel(
+    s_ref, q_ref, k_ref, v_ref, ka_ref, kb_ref, va_ref, vb_ref, o_ref, vx_ref, acc_ref, top_ref
+):
+    prefix, live, half = s_ref[2], s_ref[3], s_ref[4]
+    rows = ka_ref.shape[0]
+    m_rows = q_ref.shape[0]
+    span = k_ref.shape[1]
+    fresh = 2 * rows
+    vx_ref[:span, :HD] = v_ref[0]
+    vx_ref[span : span + rows, :HD] = va_ref[...]
+    vx_ref[span + rows :, :HD] = vb_ref[...]
+    vx_ref[:, HD:] = jnp.ones((span + fresh, HD), BF16)
+    nt = (((1,), (1,)), ((), ()))
+    count = prefix // KB
+    rest = prefix - count * KB
+
+    def product(a, b):
+        return lax.dot_general(a, b, nt, preferred_element_type=F32)
+
+    def scores(cut, at):
+        return product(q_ref[cut, :], k_ref[0, pl.ds(at, KB), :])
+
+    def fresh_scores(cut):
+        row = lax.broadcasted_iota(jnp.int32, (rows, fresh), 0) + half * rows
+        place = lax.broadcasted_iota(jnp.int32, (rows, fresh), 1)
+        ok = (place <= row) & (place < live)
+        q = q_ref[cut, :]
+        s = jnp.concatenate([product(q, ka_ref[...]), product(q, kb_ref[...])], 1)
+        s = s.reshape(PIECE // rows, rows, fresh)
+        return jnp.where(ok[None], s, -1e30).reshape(PIECE, fresh)
+
+    def rest_scores(cut, at):
+        place = lax.broadcasted_iota(jnp.int32, (PIECE, KB), 1)
+        return jnp.where(place < rest, scores(cut, at), -1e30)
+
+    def add(s, cut, at):
+        p = jnp.exp2(s - top_ref[cut, :1]).astype(BF16)
+        acc_ref[cut, :] += jnp.dot(p, vx_ref[pl.ds(at, KB), :], preferred_element_type=F32)
+
+    def raise_top(s, cut):
+        top_ref[cut, :] = jnp.maximum(top_ref[cut, :], jnp.max(s, axis=1, keepdims=True))
+
+    def block(i):
+        return pl.multiple_of(i * KB, KB)
+
+    def cuts(size, visit):
+        def step(i, carry):
+            visit(pl.ds(pl.multiple_of(i * size, size), size))
+            return carry
+
+        lax.fori_loop(0, m_rows // size, step, 0)
+
+    def blocks(stop, visit):
+        def step(i, carry):
+            visit(block(i))
+            return carry
+
+        lax.fori_loop(0, stop, step, 0)
+
+    def sweep():
+        acc_ref[...] = jnp.zeros_like(acc_ref)
+        cuts(PIECE, lambda cut: add(fresh_scores(cut), cut, span))
+
+        @pl.when(rest > 0)
+        def _():
+            at = block(count)
+            cuts(PIECE, lambda cut: add(rest_scores(cut, at), cut, at))
+
+        cuts(CHUNK, lambda cut: blocks(count, lambda at: add(scores(cut, at), cut, at)))
+
+    top_ref[...] = jnp.full(top_ref.shape, -1e30, F32)
+    cuts(PIECE, lambda cut: raise_top(scores(cut, 0), cut))
+
+    def attempt(i):
+        @pl.when(i > 0)
+        def _():
+            cuts(PIECE, lambda cut: raise_top(fresh_scores(cut), cut))
+            cuts(PIECE, lambda cut: blocks(count, lambda at: raise_top(scores(cut, at), cut)))
+
+            @pl.when(rest > 0)
+            def _():
+                at = block(count)
+                cuts(PIECE, lambda cut: raise_top(rest_scores(cut, at), cut))
+
+        sweep()
+        return jnp.max(jnp.where(acc_ref[:, HD:] < LARGE, 0.0, 1.0))
+
+    def more(state):
+        return (state[0] == 0) | ((state[0] == 1) & (state[1] > 0.0))
+
+    lax.while_loop(more, lambda state: (state[0] + 1, attempt(state[0])), (0, 0.0))
+
+    for h in range(m_rows // rows):
+        cut = slice(h * rows, (h + 1) * rows)
+        o_ref[:, h * HD : (h + 1) * HD] = (acc_ref[cut, :HD] / acc_ref[cut, HD:]).astype(BF16)
+
+
+def attend(info, q, key_cache, value_cache, ka, kb, va, vb):
+    heads, rows, _ = q.shape
+    span = key_cache.shape[1]
+    m_rows = heads * rows
+    q = q.reshape(m_rows, HD)
+    cache = pl.BlockSpec((1, span, HD), lambda i, s: (s[0], 0, s[1]))
+    fresh = pl.BlockSpec((rows, HD), whole)
+    return pl.pallas_call(
+        attend_kernel,
+        grid_spec=pltpu.PrefetchScalarGridSpec(
+            num_scalar_prefetch=1,
+            grid=(1,),
+            in_specs=[
+                pl.BlockSpec((m_rows, HD), whole),
+                cache,
+                cache,
+                fresh,
+                fresh,
+                fresh,
+                fresh,
+            ],
+            out_specs=pl.BlockSpec((rows, heads * HD), whole),
+            scratch_shapes=[
+                pltpu.VMEM((span + 2 * rows, 2 * HD), BF16),
+                pltpu.VMEM((m_rows, 2 * HD), F32),
+                pltpu.VMEM((m_rows, HD), F32),
+            ],
+        ),
+        out_shape=sds((rows, heads * HD), BF16),
+        compiler_params=params(),
+        cost_estimate=HINT,
+        name="attend",
+    )(info, q, key_cache, value_cache, ka, kb, va, vb)
+
+
+def out_kernel(s_ref, *refs, sources, before, outs):
+    a_refs, refs = refs[:sources], refs[sources:]
+    x_ref, sem = refs[-2:]
+    o_refs = refs[-2 - outs : -2]
+    depth = a_refs[0].shape[1]
+
+    @pl.when(pl.program_id(0) == 0)
+    def _():
+        copies = [
+            pltpu.make_async_copy(
+                ref, x_ref.at[:, pl.ds(pl.multiple_of(s_ref[i] * depth, depth), depth)], sem.at[i]
+            )
+            for i, ref in enumerate(a_refs)
+        ]
+        for c in copies:
+            c.start()
+        for c in copies:
+            c.wait()
+
+    total = jnp.dot(x_ref[...], refs[0][...], preferred_element_type=F32)
+    if before:
+        total += refs[1][...]
+    for i, o_ref in enumerate(o_refs):
+
+        @pl.when(pl.program_id(0) * outs // pl.num_programs(0) == i)
+        def _():
+            o_ref[...] = total.astype(o_ref.dtype)
+
+
+def out_project(index, pieces, w, before, first, width, dtype, outs=1, cols=1024):
+    rows, depth = pieces[0].shape
+    n = len(pieces)
+    start = first // cols
+    cols = min(cols, width)
+    specs = [pl.BlockSpec(memory_space=pl.ANY)] * n + [
+        pl.BlockSpec((n * depth, cols), lambda j, s: (s[n], start + j))
+    ]
+    operands = list(pieces) + [w]
+    if before is not None:
+        operands.append(before)
+        specs.append(pl.BlockSpec((rows, cols), lambda j, s: (0, start + j)))
+    each = width // cols // outs
+    out = pl.pallas_call(
+        lambda *refs: out_kernel(*refs, sources=n, before=before is not None, outs=outs),
+        grid_spec=pltpu.PrefetchScalarGridSpec(
+            num_scalar_prefetch=1,
+            grid=(width // cols,),
+            in_specs=specs,
+            out_specs=[
+                pl.BlockSpec((rows, cols), lambda j, s, i=i: (0, jnp.clip(j - i * each, 0, each - 1)))
+                for i in range(outs)
+            ],
+            scratch_shapes=[pltpu.VMEM((rows, n * depth), BF16), pltpu.SemaphoreType.DMA((n,))],
+        ),
+        out_shape=[sds((rows, width // outs), dtype)] * outs,
+        compiler_params=params(),
+        cost_estimate=HINT,
+        name="out_project",
+    )(index, *operands)
+    return out[0] if outs == 1 else out
+
+
+def choose_kernel(s_ref, a_ref, b_ref, o_ref):
+    o_ref[...] = jnp.where(s_ref[0] == 1, a_ref[...], b_ref[...])
+
+
+def choose(flag, a, b):
+    rows, cols = a.shape
+    part = rows // 2
+    block = pl.BlockSpec((part, cols), lambda i, s: (i, 0))
+    return pl.pallas_call(
+        choose_kernel,
+        grid_spec=pltpu.PrefetchScalarGridSpec(
+            num_scalar_prefetch=1,
+            grid=(rows // part,),
+            in_specs=[block] * 2,
+            out_specs=block,
+        ),
+        out_shape=sds(a.shape, a.dtype),
+        compiler_params=params(),
+        cost_estimate=LONGER,
+        name="choose",
+    )(flag.astype(jnp.int32)[None], a, b)
+
+
+def add_kernel(*refs):
+    total = refs[0][...].astype(F32)
+    for ref in refs[1:-1]:
+        total += ref[...].astype(F32)
+    refs[-1][...] = total.astype(BF16)
+
+
+def add(*xs):
+    rows, cols = xs[0].shape
+    block = pl.BlockSpec((rows, cols), lambda: (0, 0))
+    return pl.pallas_call(
+        add_kernel,
+        in_specs=[block] * len(xs),
+        out_specs=block,
+        out_shape=sds((rows, cols), BF16),
+        compiler_params=params(),
+        cost_estimate=HINT,
+        name="add",
+    )(*xs)
+
+
+def in_turn_kernel(s_ref, ka_ref, kb_ref, va_ref, vb_ref, k0_ref, k1_ref, v0_ref, v1_ref):
+    first = s_ref[0] == 1
+
+    @pl.when(first)
+    def _():
+        k0_ref[...], k1_ref[...] = ka_ref[...], kb_ref[...]
+        v0_ref[...], v1_ref[...] = va_ref[...], vb_ref[...]
+
+    @pl.when(jnp.logical_not(first))
+    def _():
+        k0_ref[...], k1_ref[...] = kb_ref[...], ka_ref[...]
+        v0_ref[...], v1_ref[...] = vb_ref[...], va_ref[...]
+
+
+def in_turn(flag, ka, kb, va, vb):
+    block = pl.BlockSpec(ka.shape, whole)
+    return pl.pallas_call(
+        in_turn_kernel,
+        grid_spec=pltpu.PrefetchScalarGridSpec(
+            num_scalar_prefetch=1, grid=(1,), in_specs=[block] * 4, out_specs=[block] * 4
+        ),
+        out_shape=[sds(ka.shape, BF16)] * 4,
+        compiler_params=params(),
+        cost_estimate=HINT,
+        name="in_turn",
+    )(flag[None], ka, kb, va, vb)
+
+
+class Order:
+    def __init__(self, mark):
+        self.mark = mark
+
+    def wait(self, x):
+        x, self.mark = lax.optimization_barrier((x, self.mark))
+        return x
+
+    def do(self, f, first, *args):
+        return self.wait(f(self.wait(first), *args))
+
+
+def pipelined_body(
+    tokens, norm_gain, qkv_weight, out_weight, key_cache, value_cache, prefix_len, stretch_len
+):
+    gx = lax.axis_index("gx")
+    z = lax.axis_index("gy")
+    chip, core = gx // 2, gx % 2
+    rows = tokens.shape[0]
+    half = rows // 2
+    width = out_weight.shape[1]
+    pieces = 4
+    order = Order(prefix_len)
+    do, wait = order.do, order.wait
+
+    def along(x, pairs):
+        return lax.ppermute(x, "gy", pairs)
+
+    def over_core(x):
+        return lax.ppermute(x, "gx", [(i, i ^ 1) for i in range(4)])
+
+    def over_chip(x):
+        return lax.ppermute(x, "gx", [(i, i ^ 2) for i in range(4)])
+
+    sibling = [(0, 1), (1, 0), (2, 3), (3, 2)]
+    middle = [(1, 2), (2, 1)]
+    outward = [(1, 0), (2, 3)]
+    inward = [(0, 1), (3, 2)]
+    is_mid = (z == 1) | (z == 2)
+
+    request, second = z // 2, z % 2
+    other = 1 - request
+    local = jnp.arange(8, dtype=jnp.int32)
+    pairs = jnp.array([0, 2, 1, 3, 9, 11, 10, 12], jnp.int32)
+    tiles = jnp.concatenate(
+        [
+            is_mid.astype(jnp.int32)[None],
+            pairs + (1 - core) * 4,
+            jnp.array([8, 17], jnp.int32),
+            (local // 4) * 9 + core * 4 + local % 4,
+        ]
+    )
+    spots = jnp.stack([gx, gx ^ 1, gx ^ 2, gx ^ 3, 0 * gx]).astype(jnp.int32)
+    near = jnp.stack([core, 1 - core, chip]).astype(jnp.int32)
+    far = jnp.stack([core, 1 - core, 1 - chip]).astype(jnp.int32)
+
+    def pick(flag, a, b):
+        return jnp.where(flag, a, b)
+
+    def row_squares(x):
+        v = x.astype(F32)
+        return jnp.sum(v * v, axis=1, keepdims=True)
+
+    def tables(starts):
+        pos = (starts[:, None] + jnp.arange(rows, dtype=jnp.int32)[None, :]).reshape(-1)
+        lane = jnp.arange(HD, dtype=jnp.int32)
+        freq = THETA ** (-((lane % (HD // 2)).astype(F32) * 2.0) / HD)
+        angles = pos.astype(F32)[:, None] * freq[None, :]
+        sign = jnp.where(lane < HD // 2, -1.0, 1.0).astype(F32)
+        return jnp.cos(angles), jnp.sin(angles) * sign[None, :]
+
+    def attention(q, req, part, ka, kb, va, vb):
+        info = jnp.stack([req, chip, prefix_len[req], stretch_len[req], part]).astype(jnp.int32)
+        return attend(info, q, key_cache, value_cache, ka, kb, va, vb)
+
+    at_two = z == 2
+    squares = do(row_squares, tokens)
+    squares_c = over_core(squares)
+    starts = jnp.stack(
+        [
+            prefix_len[request] + second * rows,
+            prefix_len[request] + (1 - second) * rows,
+            prefix_len[other],
+            prefix_len[other] + rows,
+        ]
+    )
+    squares_c = wait(squares_c)
+    squares = do(lambda a: a + squares_c, squares)
+    squares_x = wait(over_chip(squares))
+
+    def normed(x, i):
+        cut = slice(i * half, (i + 1) * half)
+        scale = lax.rsqrt((squares + squares_x)[cut] / D + EPSILON)
+        return (x[cut].astype(F32) * scale * norm_gain[None, :]).astype(BF16)
+
+    own_a = do(lambda x: normed(x, 0), tokens)
+    a0 = along(own_a, sibling)
+    own_b = do(lambda x: normed(x, 1), tokens)
+    a1 = along(own_b, sibling)
+    *mine_o, keep_o = do(lambda x: project(tiles, [x, own_b], qkv_weight), own_a)
+    recv_o = [over_core(x) for x in mine_o]
+    a0 = wait(a0)
+    m0 = along(do(lambda x: choose(at_two, own_a, x), a0), middle)
+    cos, sin = do(tables, starts)
+    a1 = wait(a1)
+    m1 = along(do(lambda x: choose(at_two, own_b, x), a1), middle)
+    recv_o = wait(recv_o)
+    cross_o = over_chip(do(lambda x: combine(chip, keep_o, mine_o, x), recv_o))
+    m0 = wait(m0)
+    n0 = along(m0, outward)
+
+    *mine_a, keep_a = do(lambda x: project(tiles, [x, a1], qkv_weight), a0)
+    recv_a = [over_core(x) for x in mine_a]
+    n0 = wait(n0)
+    cross_o = wait(cross_o)
+    m1 = wait(m1)
+    n1 = along(m1, outward)
+    m2 = along(do(lambda x: choose(at_two, x, own_a), a0), middle)
+    recv_a = wait(recv_a)
+    cross_a = over_chip(do(lambda x: combine(chip, keep_a, mine_a, x), recv_a))
+    q_o, k_o, v_o = do(
+        lambda x: finish(chip, keep_o, mine_o, recv_o, x, cos, sin, 0), cross_o
+    )
+    cross_a = wait(cross_a)
+    q_a, k_a, v_a = do(
+        lambda x: finish(chip, keep_a, mine_a, recv_a, x, cos, sin, 1), cross_a
+    )
+    own_first = (second == 0).astype(jnp.int32)
+    k0, k1, v0, v1 = do(lambda k: in_turn(own_first, k_o, k, v_o, v_a), k_a)
+    m2 = wait(m2)
+    n2 = along(m2, outward)
+    m3 = along(do(lambda x: choose(at_two, x, own_b), a1), middle)
+    att_a = do(lambda q: attention(q, request, 1 - second, k0, k1, v0, v1), q_a)
+    att_ax = over_chip(att_a)
+    att_ac = over_core(att_a)
+
+    n1 = wait(n1)
+    *mine_b, keep_b = do(lambda x: project(tiles, [x, m1, n0, n1], qkv_weight), m0)
+    recv_b = [over_core(x) for x in mine_b]
+    n2 = wait(n2)
+    m3 = wait(m3)
+    n3 = along(m3, outward)
+    att_ax = wait(att_ax)
+    att_ad = over_core(att_ax)
+    att_ac, att_ad = wait((att_ac, att_ad))
+    recv_b = wait(recv_b)
+    cross_b = over_chip(do(lambda x: combine(chip, keep_b, mine_b, x), recv_b))
+    part_a = do(
+        lambda a: out_project(
+            spots, [a, att_ac, att_ax, att_ad], out_weight, None, 0, width, BF16, pieces
+        ),
+        att_a,
+    )
+    sum_a = [along(x, inward) for x in part_a]
+    n3 = wait(n3)
+    cross_b = wait(cross_b)
+    q_b, k_b, v_b = do(
+        lambda x: finish(chip, keep_b, mine_b, recv_b, x, cos, sin, 2), cross_b
+    )
+    att_b = do(lambda q: attention(q, other, 0, k_b, k_b, v_b, v_b), q_b)
+    att_bx = over_chip(att_b)
+    att_bc = over_core(att_b)
+
+    *mine_c, keep_c = do(lambda x: project(tiles, [x, m3, n2, n3], qkv_weight), m2)
+    recv_c = [over_core(x) for x in mine_c]
+    sum_a = wait(sum_a)
+    att_bx = wait(att_bx)
+    att_bd = over_core(att_bx)
+    att_bc, att_bd = wait((att_bc, att_bd))
+    recv_c = wait(recv_c)
+    cross_c = over_chip(do(lambda x: combine(chip, keep_c, mine_c, x), recv_c))
+    part_b = do(
+        lambda a: out_project(
+            spots, [a, att_bc, att_bx, att_bd], out_weight, None, 0, width, BF16, pieces
+        ),
+        att_b,
+    )
+    b1 = [along(x, inward) for x in part_b]
+    att_o = do(lambda q: attention(q, request, second, k0, k1, v0, v1), q_o)
+    att_ox = over_chip(att_o)
+    att_oc = over_core(att_o)
+    cross_c = wait(cross_c)
+    q_c, k_c, v_c = do(
+        lambda x: finish(chip, keep_c, mine_c, recv_c, x, cos, sin, 3), cross_c
+    )
+    b2, b3, c2, c3 = [], [], [], []
+
+    def pass_b1(i):
+        b1[i] = wait(b1[i])
+        b2.append(along(do(add, b1[i], part_b[i]), middle))
+
+    def pass_b2(i):
+        b2[i] = wait(b2[i])
+        b3.append(along(do(add, b2[i], part_a[i]), [(1, 0)]))
+
+    def pass_c1(i):
+        c1[i] = wait(c1[i])
+        c2.append(along(do(add, c1[i], part_c[i]), middle))
+
+    def pass_c2(i):
+        c2[i] = wait(c2[i])
+        c3.append(along(do(add, c2[i], part_a[i]), [(2, 3)]))
+
+    def output_own(i):
+        return do(
+            lambda a: out_project(
+                spots,
+                [a, att_oc, att_ox, att_od],
+                out_weight,
+                None,
+                i * (width // 2),
+                width // 2,
+                BF16,
+                pieces // 2,
+            ),
+            att_o,
+        )
+
+    pass_b1(0)
+    att_c = do(lambda q: attention(q, other, 1, k_b, k_c, v_b, v_c), q_c)
+    att_cx = over_chip(att_c)
+    att_cc = over_core(att_c)
+    for i in range(1, pieces):
+        pass_b1(i)
+    att_ox = wait(att_ox)
+    att_od = over_core(att_ox)
+    att_oc, att_od = wait((att_oc, att_od))
+    part_o = output_own(0)
+    att_cx = wait(att_cx)
+    att_cd = over_core(att_cx)
+    att_cc, att_cd = wait((att_cc, att_cd))
+    part_c = do(
+        lambda a: out_project(
+            spots, [a, att_cc, att_cx, att_cd], out_weight, None, 0, width, BF16, pieces
+        ),
+        att_c,
+    )
+    c1 = [along(x, inward) for x in part_c]
+    part_o += output_own(1)
+    pass_b2(0)
+    pass_c1(0)
+    pass_b2(1)
+    pass_c1(1)
+    b3[0] = wait(b3[0])
+    pass_c2(0)
+    pass_b2(2)
+    pass_c1(2)
+    b3[1] = wait(b3[1])
+    pass_c2(1)
+    pass_b2(3)
+    pass_c1(3)
+    b3[2] = wait(b3[2])
+    pass_c2(2)
+    b3[3] = wait(b3[3])
+    pass_c2(3)
+    zero = jnp.zeros((), BF16)
+    total = lambda *xs: sum(x.astype(F32) for x in xs).astype(BF16)
+    side = lambda xs: jnp.concatenate(xs, 1)
+    base = do(lambda o: total(side(o), side(sum_a), side(b3), pick(z == 2, side(b2), zero)), part_o)
+    c3 = wait(c3)
+    ends = (z == 1) & (order.mark[0] > 0)
+    return total(base, side(c3), pick(ends, side(c2), zero))
 
 
 def rotate(values, positions):
@@ -31,7 +760,9 @@
     return start + row_ids % STRETCH
 
 
-def attend(queries, offsets, cached_keys, cached_values, fresh_keys, fresh_values, prefix, live):
+def attend_any(
+    queries, offsets, cached_keys, cached_values, fresh_keys, fresh_values, prefix, live
+):
     keys = jnp.concatenate([cached_keys, fresh_keys], 0)
     values = jnp.concatenate([cached_values, fresh_values], 0)
     scores = jnp.dot(queries, keys.T, preferred_element_type=jnp.float32) * queries.shape[-1] ** (
@@ -53,7 +784,7 @@
     return jnp.dot(probs, values, preferred_element_type=jnp.float32).astype(jnp.bfloat16)
 
 
-def body(
+def general_body(
     tokens, norm_gain, qkv_weight, out_weight, key_cache, value_cache, prefix_len, stretch_len
 ):
     group = QH // KVH
@@ -87,7 +818,7 @@
         for request in range(requests):
             lower = request * STRETCH
             upper = lower + STRETCH
-            result = attend(
+            result = attend_any(
                 queries[lower:upper, head],
                 offsets,
                 lax.dynamic_slice_in_dim(key_cache[request], group_index * HD, HD, 1),
@@ -121,6 +852,11 @@
         P("groups"),
         P("groups"),
     )
+    fits = mesh.shape["gx"] == 4 and mesh.shape["gy"] == 4
     return jax.shard_map(
-        body, mesh=mesh, in_specs=placed, out_specs=P(("groups", "gy"), "gx"), check_vma=False
-    )
+        pipelined_body if fits else general_body,
+        mesh=mesh,
+        in_specs=placed,
+        out_specs=P(("groups", "gy"), "gx"),
+        check_vma=False,
+    )

time: 995 us -> 523 us (0.53)
  waiting for transfers between devices: 597 us -> 69.4 us
  Pallas kernels: 0 us -> 307 us
  matrix products: 232 us -> 0 us
  starting transfers between devices: 0.17 us -> 83.3 us
  other arithmetic: 62.9 us -> 16 us
  local copies, waits for them, and re-layouts: 71.4 us -> 34 us
  between operations: 15.4 us -> 3.42 us
    reduce_scatter x2 -> x0, waiting for transfers between devices: 369 us -> none  [the longest x1 280 us: body(): lax.psum_scatter(jnp.dot(gathered_out, out_weight, preferred_element_type...]
    pallas_call x0 -> x42, Pallas kernels: none -> 307 us  [the longest x4 88.1 us: project(): pl.pallas_call(lambda *refs: project_kernel(*refs, sources=len(xs)), grid...]
    dot_general x34 -> x0, matrix products: 232 us -> none  [the longest x16 83.8 us: attend(): jnp.dot(queries, keys.T, preferred_element_type=jnp.float32)]
    all_gather x2 -> x0, waiting for transfers between devices: 208 us -> none  [the longest x1 149 us: body(): whole = lax.all_gather(tokens, 'gy', axis=0, tiled=True)]
    ppermute x0 -> x64, starting transfers between devices: none -> 83.3 us  [the longest x38 68.8 us: along(): return lax.ppermute(x, 'gy', pairs)]
    ppermute x0 -> x64, waiting for transfers between devices: none -> 69.4 us  [the longest x38 49.2 us: along(): return lax.ppermute(x, 'gy', pairs)]
    dynamic_slice x37 -> x1, local copies, waits for them, and re-layouts: 48 us -> 0.65 us  [attention(): stretch_len[req]]
    reduce_sum x5 -> x1, other arithmetic: 47.6 us -> 2.24 us  [row_squares(): return jnp.sum(v * v, axis=1, keepdims=True)]
  transfers between devices with their start and end apart: 5 -> 64, of which waited for: 5 -> 14; matrix products, arithmetic and copies ran while one was open for 7% -> 3% of each run, Pallas kernels for 0% -> 59%
where the time goes in v1:
time: 523 us; the launch traced here: 513 us
  Pallas kernels  307 us (59%)
  starting transfers between devices  83.3 us (16%)
  waiting for transfers between devices  69.4 us (13%)
  local copies, waits for them, and re-layouts  34 us (7%)
  other arithmetic  16 us (3%)
    pallas_call x4, Pallas kernels, project(): pl.pallas_call(lambda *refs: project_kernel(*refs, sources=len(xs)), grid...  88.1 us
    pallas_call x5, Pallas kernels, out_project(): pl.pallas_call(lambda *refs: out_kernel(*refs, sources=n, before=before i...  84.2 us
    ppermute x38, starting transfers between devices, along(): return lax.ppermute(x, 'gy', pairs)  68.8 us
    pallas_call x4, Pallas kernels, attend(): pl.pallas_call(attend_kernel, grid_spec=pltpu.PrefetchScalarGridSpec(num_...  68.6 us
    ppermute x38, waiting for transfers between devices, along(): return lax.ppermute(x, 'gy', pairs)  49.2 us
    pallas_call x16, Pallas kernels, add(): pl.pallas_call(add_kernel, in_specs=[block] * len(xs), out_specs=block, o...  34 us
    unnamed x167, local copies, waits for them, and re-layouts  25.5 us
    ppermute x9, waiting for transfers between devices, over_chip(): return lax.ppermute(x, 'gx', [(i, i ^ 2) for i in range(4)])  13.8 us
  transfers between devices with their start and end apart: 64, of which 14 were waited for; matrix products, arithmetic and copies ran while one was open for 3% of the time, Pallas kernels for 59%

profile of v1, /device:TPU:28, one launch (start us, length us, event | category | flops | bytes accessed | tf_op | source)
XLA Modules:
  0.0 513.3 jit_solution(6177857171974996121)
XLA Ops:
  0.0 2.2 multiply_reduce_fusion
  11.7 22.0 %project.4 = (bf16[256,1280]{1,0:T(8,128)(2,1)}, bf16[256,1280]{1,0:T(8,128)(2,1)}, f32[256,2048]{1,0:T(8,128)}) custom-call(s32[19]{0:T(128)} %pad_add_fusion.refs_0_, bf16[128,4096]{1,0:T(8,128)(2,1)} %copy-done.1, bf16[128,4096]{1,0:T(8,128)(2,1)} %copy-done, bf16[4096,4608]{1,0:T(8,128)(2,1)} %refs_6_.3, bf16[4096,4608]{1,0:T(8,128)(2,1)} %refs_6_.3), custom_call_target="tpu_custom_call" | custom-call | flops 1024 | bytes 1024 | tf_op jit(solution)/shard_map/project/pallas_call | solution.py:95
  35.7 2.4 choose.4
  42.8 3.0 fusion
  45.9 9.4 %collective-permute-done.4.b_ref.refs_2_.a_ref = bf16[128,4096]{1,0:T(8,128)(2,1)S(1)} collective-permute-done((bf16[128,4096]{1,0:T(8,128)(2,1)S(1)}, bf16[128,4096]{1,0:T(8,128)(2,1)S(1)}, u32[]{:S(2)}, u32[]{:S(2)}) %collective-permute-start.4) | collective-permute-done | bytes 1048608 | tf_op jit(solution)/shard_map/ppermute | solution.py:508
  56.2 2.4 choose.5
  59.7 2.3 combine.4
  66.6 22.1 %project.5 = (bf16[256,1280]{1,0:T(8,128)(2,1)}, bf16[256,1280]{1,0:T(8,128)(2,1)}, f32[256,2048]{1,0:T(8,128)}) custom-call(s32[19]{0:T(128)} %pad_add_fusion.refs_0_, bf16[128,4096]{1,0:T(8,128)(2,1)} %copy-done.11, bf16[128,4096]{1,0:T(8,128)(2,1)} %copy-done.10, bf16[4096,4608]{1,0:T(8,128)(2,1)} %refs_6_.3, bf16[4096,4608]{1,0:T(8,128)(2,1)} %refs_6_.3), custom_call_target="tpu_custom_call" | custom-call | flops 1024 | bytes 1024 | tf_op jit(solution)/shard_map/project/pallas_call | solution.py:95
  89.3 3.0 choose.6
  94.7 2.3 combine.5
  98.9 2.8 finish.4
  101.7 12.3 %collective-permute-done.13.rest_0_ = bf16[256,1280]{1,0:T(8,128)(2,1)S(1)} collective-permute-done((bf16[256,1280]{1,0:T(8,128)(2,1)}, bf16[256,1280]{1,0:T(8,128)(2,1)S(1)}, u32[]{:S(2)}, u32[]{:S(2)}) %collective-permute-start.13) | collective-permute-done | bytes 655392 | tf_op jit(solution)/shard_map/ppermute | solution.py:514
  114.8 2.8 finish.5
  120.6 2.4 choose.7
  126.1 17.7 %attend.4.refs_1_ = bf16[256,1024]{1,0:T(8,128)(2,1)} custom-call(s32[5]{0:T(128)} %stack.72.s_ref, bf16[2048,128]{1,0:T(8,128)(2,1)} %bitcast.31, bf16[2,3072,256]{2,1,0:T(8,128)(2,1)} %k_ref.7, bf16[2,3072,256]{2,1,0:T(8,128)(2,1)} %v_ref.7, bf16[256,128]{1,0:T(8,128)(2,1)} %get-tuple-element.465.ka_ref, bf16[256,128]{1,0:T(8,128)(2,1)} %get-tuple-element.466.kb_ref, ...), custom_call_target="tpu_custom_call" | custom-call | flops 1024 | bytes 1024 | tf_op jit(solution)/shard_map/attend/pallas_call | solution.py:320
  144.3 22.0 %project.6 = (bf16[256,1280]{1,0:T(8,128)(2,1)}, bf16[256,1280]{1,0:T(8,128)(2,1)}, f32[256,2048]{1,0:T(8,128)}) custom-call(s32[19]{0:T(128)} %pad_add_fusion.refs_0_, bf16[128,4096]{1,0:T(8,128)(2,1)} %copy-done.34, bf16[128,4096]{1,0:T(8,128)(2,1)} %collective-permute-done.11.refs_2_, bf16[128,4096]{1,0:T(8,128)(2,1)} %copy-done.38, ...), custom_call_target="tpu_custom_call" | custom-call | flops 1024 | bytes 1024 | tf_op jit(solution)/shard_map/project/pallas_call | solution.py:95
  172.6 2.3 combine.6
  177.2 19.3 %out_project.5 = (bf16[256,1024]{1,0:T(8,128)(2,1)}, bf16[256,1024]{1,0:T(8,128)(2,1)}, bf16[256,1024]{1,0:T(8,128)(2,1)}, bf16[256,1024]{1,0:T(8,128)(2,1)}) custom-call(s32[5]{0:T(128)} %stack.61.refs_0_, bf16[256,1024]{1,0:T(8,128)(2,1)} %attend.4.refs_1_, bf16[256,1024]{1,0:T(8,128)(2,1)} %copy-done.46, bf16[256,1024]{1,0:T(8,128)(2,1)} %copy-done.44, ...), custom_call_target="tpu_custom_call" | custom-call | flops 1024 | bytes 1024 | tf_op jit(solution)/shard_map/out_project/pallas_call | solution.py:390
  196.5 9.4 %collective-permute-start.28 = (bf16[256,1024]{1,0:T(8,128)(2,1)}, bf16[256,1024]{1,0:T(8,128)(2,1)S(1)}, u32[]{:S(2)}, u32[]{:S(2)}) collective-permute-start(bf16[256,1024]{1,0:T(8,128)(2,1)} %get-tuple-element.532.refs_1_), channel_id=1, source_target_pairs={{0,1},{3,2},{4,5},{7,6},{8,9},{11,10},{12,13},{15,14},{16,17},{19,... | collective-permute-start | bytes 1572872 | tf_op jit(solution)/shard_map/ppermute | solution.py:508
  212.6 2.8 finish.6
  215.4 16.6 %attend.5.refs_1_ = bf16[256,1024]{1,0:T(8,128)(2,1)} custom-call(s32[5]{0:T(128)} %stack.70.s_ref, bf16[2048,128]{1,0:T(8,128)(2,1)} %bitcast.33, bf16[2,3072,256]{2,1,0:T(8,128)(2,1)} %k_ref.7, bf16[2,3072,256]{2,1,0:T(8,128)(2,1)} %v_ref.7, bf16[256,128]{1,0:T(8,128)(2,1)} %get-tuple-element.517.ka_ref.kb_ref, ...), custom_call_target="tpu_custom_call" | custom-call | flops 1024 | bytes 1024 | tf_op jit(solution)/shard_map/attend/pallas_call | solution.py:320
  232.6 22.0 %project.7 = (bf16[256,1280]{1,0:T(8,128)(2,1)}, bf16[256,1280]{1,0:T(8,128)(2,1)}, f32[256,2048]{1,0:T(8,128)}) custom-call(s32[19]{0:T(128)} %pad_add_fusion.refs_0_, bf16[128,4096]{1,0:T(8,128)(2,1)} %copy-done.35, bf16[128,4096]{1,0:T(8,128)(2,1)} %copy-done.37, bf16[128,4096]{1,0:T(8,128)(2,1)} %copy-done.36, bf16[128,4096]{1,0:T(8,128)(2,1)} %copy-done.39, ...), custom_call_target="tpu_custom_call" | custom-call | flops 1024 | bytes 1024 | tf_op jit(solution)/shard_map/project/pallas_call | solution.py:95
  261.0 2.3 combine.7
  264.8 19.4 %out_project.6 = (bf16[256,1024]{1,0:T(8,128)(2,1)}, bf16[256,1024]{1,0:T(8,128)(2,1)}, bf16[256,1024]{1,0:T(8,128)(2,1)}, bf16[256,1024]{1,0:T(8,128)(2,1)}) custom-call(s32[5]{0:T(128)} %stack.61.refs_0_, bf16[256,1024]{1,0:T(8,128)(2,1)} %attend.5.refs_1_, bf16[256,1024]{1,0:T(8,128)(2,1)} %copy-done.49, bf16[256,1024]{1,0:T(8,128)(2,1)} %copy-done.45, ...), custom_call_target="tpu_custom_call" | custom-call | flops 1024 | bytes 1024 | tf_op jit(solution)/shard_map/out_project/pallas_call | solution.py:390
  284.2 2.1 collective-permute-start.39
  292.4 17.7 %attend.6.refs_1_ = bf16[256,1024]{1,0:T(8,128)(2,1)} custom-call(s32[5]{0:T(128)} %stack.65.s_ref, bf16[2048,128]{1,0:T(8,128)(2,1)} %bitcast.30, bf16[2,3072,256]{2,1,0:T(8,128)(2,1)} %k_ref.7, bf16[2,3072,256]{2,1,0:T(8,128)(2,1)} %v_ref.7, bf16[256,128]{1,0:T(8,128)(2,1)} %get-tuple-element.465.ka_ref, bf16[256,128]{1,0:T(8,128)(2,1)} %get-tuple-element.466.kb_ref, ...), custom_call_target="tpu_custom_call" | custom-call | flops 1024 | bytes 1024 | tf_op jit(solution)/shard_map/attend/pallas_call | solution.py:320
  312.5 2.8 finish.7
  317.4 16.6 %attend.7.refs_1_ = bf16[256,1024]{1,0:T(8,128)(2,1)} custom-call(s32[5]{0:T(128)} %stack.73.s_ref, bf16[2048,128]{1,0:T(8,128)(2,1)} %bitcast.32, bf16[2,3072,256]{2,1,0:T(8,128)(2,1)} %k_ref.7, bf16[2,3072,256]{2,1,0:T(8,128)(2,1)} %v_ref.7, bf16[256,128]{1,0:T(8,128)(2,1)} %get-tuple-element.517.ka_ref.kb_ref, ...), custom_call_target="tpu_custom_call" | custom-call | flops 1024 | bytes 1024 | tf_op jit(solution)/shard_map/attend/pallas_call | solution.py:320
  334.8 2.2 add.210
  346.5 13.0 %out_project.7 = (bf16[256,1024]{1,0:T(8,128)(2,1)}, bf16[256,1024]{1,0:T(8,128)(2,1)}) custom-call(s32[5]{0:T(128)} %stack.61.refs_0_, bf16[256,1024]{1,0:T(8,128)(2,1)} %attend.6.refs_1_, bf16[256,1024]{1,0:T(8,128)(2,1)} %copy-done.15, bf16[256,1024]{1,0:T(8,128)(2,1)} %copy-done.14, bf16[256,1024]{1,0:T(8,128)(2,1)} %copy-done.16, ...), custom_call_target="tpu_custom_call" | custom-call | flops 1024 | bytes 1024 | tf_op jit(solution)/shard_map/out_project/pallas_call | solution.py:390
  362.7 19.4 %out_project.8 = (bf16[256,1024]{1,0:T(8,128)(2,1)}, bf16[256,1024]{1,0:T(8,128)(2,1)}, bf16[256,1024]{1,0:T(8,128)(2,1)}, bf16[256,1024]{1,0:T(8,128)(2,1)}) custom-call(s32[5]{0:T(128)} %stack.61.refs_0_, bf16[256,1024]{1,0:T(8,128)(2,1)} %attend.7.refs_1_, bf16[256,1024]{1,0:T(8,128)(2,1)} %copy-done.50, bf16[256,1024]{1,0:T(8,128)(2,1)} %copy-done.48, ...), custom_call_target="tpu_custom_call" | custom-call | flops 1024 | bytes 1024 | tf_op jit(solution)/shard_map/out_project/pallas_call | solution.py:390
  382.1 2.6 collective-permute-start.48
  386.2 5.7 %collective-permute-start.46 = (bf16[256,1024]{1,0:T(8,128)(2,1)}, bf16[256,1024]{1,0:T(8,128)(2,1)S(1)}, u32[]{:S(2)}, u32[]{:S(2)}) collective-permute-start(bf16[256,1024]{1,0:T(8,128)(2,1)} %get-tuple-element.622.refs_1_), channel_id=1, source_target_pairs={{0,1},{3,2},{4,5},{7,6},{8,9},{11,10},{12,13},{15,14},{16,17},{19,... | collective-permute-start | bytes 1572872 | tf_op jit(solution)/shard_map/ppermute | solution.py:508
  391.9 13.0 %out_project.9 = (bf16[256,1024]{1,0:T(8,128)(2,1)}, bf16[256,1024]{1,0:T(8,128)(2,1)}) custom-call(s32[5]{0:T(128)} %stack.61.refs_0_, bf16[256,1024]{1,0:T(8,128)(2,1)} %attend.6.refs_1_, bf16[256,1024]{1,0:T(8,128)(2,1)} %copy-done.15, bf16[256,1024]{1,0:T(8,128)(2,1)} %copy-done.14, bf16[256,1024]{1,0:T(8,128)(2,1)} %copy-done.16, ...), custom_call_target="tpu_custom_call" | custom-call | flops 1024 | bytes 1024 | tf_op jit(solution)/shard_map/out_project/pallas_call | solution.py:390
  405.8 2.1 add.213
  412.2 6.7 %collective-permute-start.52 = (bf16[256,1024]{1,0:T(8,128)(2,1)S(1)}, bf16[256,1024]{1,0:T(8,128)(2,1)S(1)}, u32[]{:S(2)}, u32[]{:S(2)}) collective-permute-start(bf16[256,1024]{1,0:T(8,128)(2,1)S(1)} %copy-done.58), channel_id=1, source_target_pairs={{0,1},{3,2},{4,5},{7,6},{8,9},{11,10},{12,13},{15,14},{16,17},{19,... | collective-permute-start | bytes 1572872 | tf_op jit(solution)/shard_map/ppermute | solution.py:508
  426.3 7.6 %collective-permute-start.44 = (bf16[256,1024]{1,0:T(8,128)(2,1)S(1)}, bf16[256,1024]{1,0:T(8,128)(2,1)S(1)}, u32[]{:S(2)}, u32[]{:S(2)}) collective-permute-start(bf16[256,1024]{1,0:T(8,128)(2,1)S(1)} %copy-done.54), channel_id=1, source_target_pairs={{0,1},{3,2},{4,5},{7,6},{8,9},{11,10},{12,13},{15,14},{16,17},{19,... | collective-permute-start | bytes 1572872 | tf_op jit(solution)/shard_map/ppermute | solution.py:508
  433.9 2.1 add.217
  436.0 2.2 add.218
  441.9 2.1 add.220
  444.9 2.1 add.221
  459.3 2.1 add.224
  464.2 3.5 add_convert_fusion.1
  467.7 11.2 %collective-permute-done.60 = bf16[256,1024]{1,0:T(8,128)(2,1)S(1)} collective-permute-done((bf16[256,1024]{1,0:T(8,128)(2,1)S(1)}, bf16[256,1024]{1,0:T(8,128)(2,1)S(1)}, u32[]{:S(2)}, u32[]{:S(2)}) %collective-permute-start.60) | collective-permute-done | bytes 524320 | tf_op jit(solution)/shard_map/ppermute | solution.py:508
  479.7 10.4 %collective-permute-done.61 = bf16[256,1024]{1,0:T(8,128)(2,1)S(1)} collective-permute-done((bf16[256,1024]{1,0:T(8,128)(2,1)}, bf16[256,1024]{1,0:T(8,128)(2,1)S(1)}, u32[]{:S(2)}, u32[]{:S(2)}) %collective-permute-start.61) | collective-permute-done | bytes 524320 | tf_op jit(solution)/shard_map/ppermute | solution.py:508
  490.9 10.4 %collective-permute-done.63 = bf16[256,1024]{1,0:T(8,128)(2,1)S(1)} collective-permute-done((bf16[256,1024]{1,0:T(8,128)(2,1)}, bf16[256,1024]{1,0:T(8,128)(2,1)S(1)}, u32[]{:S(2)}, u32[]{:S(2)}) %collective-permute-start.63) | collective-permute-done | bytes 524320 | tf_op jit(solution)/shard_map/ppermute | solution.py:508
  502.2 6.7 %collective-permute-done.62 = bf16[256,1024]{1,0:T(8,128)(2,1)S(1)} collective-permute-done((bf16[256,1024]{1,0:T(8,128)(2,1)}, bf16[256,1024]{1,0:T(8,128)(2,1)S(1)}, u32[]{:S(2)}, u32[]{:S(2)}) %collective-permute-start.62) | collective-permute-done | bytes 524320 | tf_op jit(solution)/shard_map/ppermute | solution.py:508
  509.7 3.3 add_convert_fusion
  (309 shorter events, 116.7 us)
Async XLA Ops:
  8.6 26.2 %collective-permute-start.5 = (bf16[128,4096]{1,0:T(8,128)(2,1)S(1)}, bf16[128,4096]{1,0:T(8,128)(2,1)S(1)}, u32[]{:S(2)}, u32[]{:S(2)}) collective-permute-start(bf16[128,4096]{1,0:T(8,128)(2,1)S(1)} %multiply_convert_fusion.1.refs_1_.a_ref.b_ref), channel_id=1, source_target_pairs={{0,1},{1,0},{2,3},{3,2},{4,5},{5,4},{6,7},{7,6},{8,9},{9,8},{10,11... | collective-permute-start | bytes 3145736 | tf_op jit(solution)/shard_map/ppermute | solution.py:508
  10.1 45.2 %collective-permute-start.4 = (bf16[128,4096]{1,0:T(8,128)(2,1)S(1)}, bf16[128,4096]{1,0:T(8,128)(2,1)S(1)}, u32[]{:S(2)}, u32[]{:S(2)}) collective-permute-start(bf16[128,4096]{1,0:T(8,128)(2,1)S(1)} %multiply_convert_fusion.refs_2_.a_ref.b_ref), channel_id=1, source_target_pairs={{0,1},{1,0},{2,3},{3,2},{4,5},{5,4},{6,7},{7,6},{8,9},{9,8},{10,11... | collective-permute-start | bytes 3145736 | tf_op jit(solution)/shard_map/ppermute | solution.py:508
  38.1 23.9 %collective-permute-start.7 = (bf16[128,4096]{1,0:T(8,128)(2,1)}, bf16[128,4096]{1,0:T(8,128)(2,1)S(1)}, u32[]{:S(2)}, u32[]{:S(2)}) collective-permute-start(bf16[128,4096]{1,0:T(8,128)(2,1)} %choose.4), channel_id=1, source_target_pairs={{1,2},{2,1},{5,6},{6,5},{9,10},{10,9},{13,14},{14,13},{17,18},{18,... | collective-permute-start | bytes 3145736 | tf_op jit(solution)/shard_map/ppermute | solution.py:508
  41.4 17.2 %collective-permute-start.2 = (bf16[256,1280]{1,0:T(8,128)(2,1)}, bf16[256,1280]{1,0:T(8,128)(2,1)S(1)}, u32[]{:S(2)}, u32[]{:S(2)}) collective-permute-start(bf16[256,1280]{1,0:T(8,128)(2,1)} %get-tuple-element.383.kva_ref), channel_id=1, source_target_pairs={{0,4},{4,0},{8,12},{12,8},{1,5},{5,1},{9,13},{13,9},{2,6},{6,2},{1... | collective-permute-start | bytes 1966088 | tf_op jit(solution)/shard_map/ppermute | solution.py:511
  41.5 17.1 %collective-permute-start.3 = (bf16[256,1280]{1,0:T(8,128)(2,1)}, bf16[256,1280]{1,0:T(8,128)(2,1)S(1)}, u32[]{:S(2)}, u32[]{:S(2)}) collective-permute-start(bf16[256,1280]{1,0:T(8,128)(2,1)} %get-tuple-element.384.kvb_ref), channel_id=1, source_target_pairs={{0,4},{4,0},{8,12},{12,8},{1,5},{5,1},{9,13},{13,9},{2,6},{6,2},{1... | collective-permute-start | bytes 1966088 | tf_op jit(solution)/shard_map/ppermute | solution.py:511
  62.0 27.2 %collective-permute-start.8 = (bf16[128,4096]{1,0:T(8,128)(2,1)S(1)}, bf16[128,4096]{1,0:T(8,128)(2,1)S(1)}, u32[]{:S(2)}, u32[]{:S(2)}) collective-permute-start(bf16[128,4096]{1,0:T(8,128)(2,1)S(1)} %collective-permute-done.7.refs_1_), channel_id=1, source_target_pairs={{1,0},{2,3},{5,4},{6,7},{9,8},{10,11},{13,12},{14,15},{17,16},{18,... | collective-permute-start | bytes 3145736 | tf_op jit(solution)/shard_map/ppermute | solution.py:508
  63.3 25.9 %collective-permute-start.11 = (bf16[128,4096]{1,0:T(8,128)(2,1)S(1)}, bf16[128,4096]{1,0:T(8,128)(2,1)}, u32[]{:S(2)}, u32[]{:S(2)}) collective-permute-start(bf16[128,4096]{1,0:T(8,128)(2,1)S(1)} %copy-done.40), channel_id=1, source_target_pairs={{1,2},{2,1},{5,6},{6,5},{9,10},{10,9},{13,14},{14,13},{17,18},{18,... | collective-permute-start | bytes 3145736 | tf_op jit(solution)/shard_map/ppermute | solution.py:508
  65.1 24.2 %collective-permute-start.6 = (bf16[256,1280]{1,0:T(8,128)(2,1)}, bf16[256,1280]{1,0:T(8,128)(2,1)S(1)}, u32[]{:S(2)}, u32[]{:S(2)}) collective-permute-start(bf16[256,1280]{1,0:T(8,128)(2,1)} %combine.4), channel_id=1, source_target_pairs={{0,8},{4,12},{8,0},{12,4},{1,9},{5,13},{9,1},{13,5},{2,10},{6,14},... | collective-permute-start | bytes 1966088 | tf_op jit(solution)/shard_map/ppermute | solution.py:514
  92.3 27.1 %collective-permute-start.14 = (bf16[128,4096]{1,0:T(8,128)(2,1)}, bf16[128,4096]{1,0:T(8,128)(2,1)S(1)}, u32[]{:S(2)}, u32[]{:S(2)}) collective-permute-start(bf16[128,4096]{1,0:T(8,128)(2,1)} %choose.6), channel_id=1, source_target_pairs={{1,2},{2,1},{5,6},{6,5},{9,10},{10,9},{13,14},{14,13},{17,18},{18,... | collective-permute-start | bytes 3145736 | tf_op jit(solution)/shard_map/ppermute | solution.py:508
  97.0 17.0 %collective-permute-start.13 = (bf16[256,1280]{1,0:T(8,128)(2,1)}, bf16[256,1280]{1,0:T(8,128)(2,1)S(1)}, u32[]{:S(2)}, u32[]{:S(2)}) collective-permute-start(bf16[256,1280]{1,0:T(8,128)(2,1)} %combine.5), channel_id=1, source_target_pairs={{0,8},{4,12},{8,0},{12,4},{1,9},{5,13},{9,1},{13,5},{2,10},{6,14},... | collective-permute-start | bytes 1966088 | tf_op jit(solution)/shard_map/ppermute | solution.py:514
  97.6 46.7 %collective-permute-start.12 = (bf16[128,4096]{1,0:T(8,128)(2,1)}, bf16[128,4096]{1,0:T(8,128)(2,1)}, u32[]{:S(2)}, u32[]{:S(2)}) collective-permute-start(bf16[128,4096]{1,0:T(8,128)(2,1)} %collective-permute-done.11.refs_2_), channel_id=1, source_target_pairs={{1,0},{2,3},{5,4},{6,7},{9,8},{10,11},{13,12},{14,15},{17,16},{18,... | collective-permute-start | bytes 3145736 | tf_op jit(solution)/shard_map/ppermute | solution.py:508
  119.3 47.6 %collective-permute-start.20 = (bf16[128,4096]{1,0:T(8,128)(2,1)S(1)}, bf16[128,4096]{1,0:T(8,128)(2,1)S(1)}, u32[]{:S(2)}, u32[]{:S(2)}) collective-permute-start(bf16[128,4096]{1,0:T(8,128)(2,1)S(1)} %collective-permute-done.14.refs_1_), channel_id=1, source_target_pairs={{1,0},{2,3},{5,4},{6,7},{9,8},{10,11},{13,12},{14,15},{17,16},{18,... | collective-permute-start | bytes 3145736 | tf_op jit(solution)/shard_map/ppermute | solution.py:508
  123.0 44.1 %collective-permute-start.19 = (bf16[128,4096]{1,0:T(8,128)(2,1)}, bf16[128,4096]{1,0:T(8,128)(2,1)S(1)}, u32[]{:S(2)}, u32[]{:S(2)}) collective-permute-start(bf16[128,4096]{1,0:T(8,128)(2,1)} %choose.7), channel_id=1, source_target_pairs={{1,2},{2,1},{5,6},{6,5},{9,10},{10,9},{13,14},{14,13},{17,18},{18,... | collective-permute-start | bytes 3145736 | tf_op jit(solution)/shard_map/ppermute | solution.py:508
  143.8 23.3 %collective-permute-start.18 = (bf16[256,1024]{1,0:T(8,128)(2,1)}, bf16[256,1024]{1,0:T(8,128)(2,1)S(1)}, u32[]{:S(2)}, u32[]{:S(2)}) collective-permute-start(bf16[256,1024]{1,0:T(8,128)(2,1)} %attend.4.refs_1_), channel_id=1, source_target_pairs={{0,8},{4,12},{8,0},{12,4},{1,9},{5,13},{9,1},{13,5},{2,10},{6,14},... | collective-permute-start | bytes 1572872 | tf_op jit(solution)/shard_map/ppermute | solution.py:514
  167.6 43.5 %collective-permute-start.23 = (bf16[128,4096]{1,0:T(8,128)(2,1)S(1)}, bf16[128,4096]{1,0:T(8,128)(2,1)S(1)}, u32[]{:S(2)}, u32[]{:S(2)}) collective-permute-start(bf16[128,4096]{1,0:T(8,128)(2,1)S(1)} %collective-permute-done.19.refs_2_), channel_id=1, source_target_pairs={{1,0},{2,3},{5,4},{6,7},{9,8},{10,11},{13,12},{14,15},{17,16},{18,... | collective-permute-start | bytes 3145736 | tf_op jit(solution)/shard_map/ppermute | solution.py:508
  175.0 37.6 %collective-permute-start.22 = (bf16[256,1280]{1,0:T(8,128)(2,1)}, bf16[256,1280]{1,0:T(8,128)(2,1)}, u32[]{:S(2)}, u32[]{:S(2)}) collective-permute-start(bf16[256,1280]{1,0:T(8,128)(2,1)} %combine.6), channel_id=1, source_target_pairs={{0,8},{4,12},{8,0},{12,4},{1,9},{5,13},{9,1},{13,5},{2,10},{6,14},... | collective-permute-start | bytes 1966088 | tf_op jit(solution)/shard_map/ppermute | solution.py:514
  196.5 58.1 %collective-permute-start.28 = (bf16[256,1024]{1,0:T(8,128)(2,1)}, bf16[256,1024]{1,0:T(8,128)(2,1)S(1)}, u32[]{:S(2)}, u32[]{:S(2)}) collective-permute-start(bf16[256,1024]{1,0:T(8,128)(2,1)} %get-tuple-element.532.refs_1_), channel_id=1, source_target_pairs={{0,1},{3,2},{4,5},{7,6},{8,9},{11,10},{12,13},{15,14},{16,17},{19,... | collective-permute-start | bytes 1572872 | tf_op jit(solution)/shard_map/ppermute | solution.py:508
  205.9 48.8 %collective-permute-start.29 = (bf16[256,1024]{1,0:T(8,128)(2,1)}, bf16[256,1024]{1,0:T(8,128)(2,1)S(1)}, u32[]{:S(2)}, u32[]{:S(2)}) collective-permute-start(bf16[256,1024]{1,0:T(8,128)(2,1)} %get-tuple-element.533.refs_1_), channel_id=1, source_target_pairs={{0,1},{3,2},{4,5},{7,6},{8,9},{11,10},{12,13},{15,14},{16,17},{19,... | collective-permute-start | bytes 1572872 | tf_op jit(solution)/shard_map/ppermute | solution.py:508
  209.0 46.2 %collective-permute-start.30 = (bf16[256,1024]{1,0:T(8,128)(2,1)}, bf16[256,1024]{1,0:T(8,128)(2,1)}, u32[]{:S(2)}, u32[]{:S(2)}) collective-permute-start(bf16[256,1024]{1,0:T(8,128)(2,1)} %get-tuple-element.534.refs_1_), channel_id=1, source_target_pairs={{0,1},{3,2},{4,5},{7,6},{8,9},{11,10},{12,13},{15,14},{16,17},{19,... | collective-permute-start | bytes 1572872 | tf_op jit(solution)/shard_map/ppermute | solution.py:508
  211.1 44.2 %collective-permute-start.31 = (bf16[256,1024]{1,0:T(8,128)(2,1)}, bf16[256,1024]{1,0:T(8,128)(2,1)S(1)}, u32[]{:S(2)}, u32[]{:S(2)}) collective-permute-start(bf16[256,1024]{1,0:T(8,128)(2,1)} %get-tuple-element.535.refs_1_), channel_id=1, source_target_pairs={{0,1},{3,2},{4,5},{7,6},{8,9},{11,10},{12,13},{15,14},{16,17},{19,... | collective-permute-start | bytes 1572872 | tf_op jit(solution)/shard_map/ppermute | solution.py:508
  232.1 24.1 %collective-permute-start.27 = (bf16[256,1024]{1,0:T(8,128)(2,1)}, bf16[256,1024]{1,0:T(8,128)(2,1)S(1)}, u32[]{:S(2)}, u32[]{:S(2)}) collective-permute-start(bf16[256,1024]{1,0:T(8,128)(2,1)} %attend.5.refs_1_), channel_id=1, source_target_pairs={{0,8},{4,12},{8,0},{12,4},{1,9},{5,13},{9,1},{13,5},{2,10},{6,14},... | collective-permute-start | bytes 1572872 | tf_op jit(solution)/shard_map/ppermute | solution.py:514
  263.3 46.8 %collective-permute-start.38 = (bf16[256,1280]{1,0:T(8,128)(2,1)}, bf16[256,1280]{1,0:T(8,128)(2,1)S(1)}, u32[]{:S(2)}, u32[]{:S(2)}) collective-permute-start(bf16[256,1280]{1,0:T(8,128)(2,1)} %combine.7), channel_id=1, source_target_pairs={{0,8},{4,12},{8,0},{12,4},{1,9},{5,13},{9,1},{13,5},{2,10},{6,14},... | collective-permute-start | bytes 1966088 | tf_op jit(solution)/shard_map/ppermute | solution.py:514
  284.2 31.0 %collective-permute-start.39 = (bf16[256,1024]{1,0:T(8,128)(2,1)}, bf16[256,1024]{1,0:T(8,128)(2,1)}, u32[]{:S(2)}, u32[]{:S(2)}) collective-permute-start(bf16[256,1024]{1,0:T(8,128)(2,1)} %get-tuple-element.570.refs_1_), channel_id=1, source_target_pairs={{0,1},{3,2},{4,5},{7,6},{8,9},{11,10},{12,13},{15,14},{16,17},{19,... | collective-permute-start | bytes 1572872 | tf_op jit(solution)/shard_map/ppermute | solution.py:508
  286.4 47.7 %collective-permute-start.37 = (bf16[256,1024]{1,0:T(8,128)(2,1)}, bf16[256,1024]{1,0:T(8,128)(2,1)S(1)}, u32[]{:S(2)}, u32[]{:S(2)}) collective-permute-start(bf16[256,1024]{1,0:T(8,128)(2,1)} %get-tuple-element.559.refs_1_), channel_id=1, source_target_pairs={{0,1},{3,2},{4,5},{7,6},{8,9},{11,10},{12,13},{15,14},{16,17},{19,... | collective-permute-start | bytes 1572872 | tf_op jit(solution)/shard_map/ppermute | solution.py:508
  287.7 49.3 %collective-permute-start.36 = (bf16[256,1024]{1,0:T(8,128)(2,1)}, bf16[256,1024]{1,0:T(8,128)(2,1)S(1)}, u32[]{:S(2)}, u32[]{:S(2)}) collective-permute-start(bf16[256,1024]{1,0:T(8,128)(2,1)} %get-tuple-element.558.refs_1_), channel_id=1, source_target_pairs={{0,1},{3,2},{4,5},{7,6},{8,9},{11,10},{12,13},{15,14},{16,17},{19,... | collective-permute-start | bytes 1572872 | tf_op jit(solution)/shard_map/ppermute | solution.py:508
  290.9 49.0 %collective-permute-start.35 = (bf16[256,1024]{1,0:T(8,128)(2,1)}, bf16[256,1024]{1,0:T(8,128)(2,1)S(1)}, u32[]{:S(2)}, u32[]{:S(2)}) collective-permute-start(bf16[256,1024]{1,0:T(8,128)(2,1)} %get-tuple-element.557.refs_1_), channel_id=1, source_target_pairs={{0,1},{3,2},{4,5},{7,6},{8,9},{11,10},{12,13},{15,14},{16,17},{19,... | collective-permute-start | bytes 1572872 | tf_op jit(solution)/shard_map/ppermute | solution.py:508
  310.1 32.7 %collective-permute-start.34 = (bf16[256,1024]{1,0:T(8,128)(2,1)}, bf16[256,1024]{1,0:T(8,128)(2,1)S(1)}, u32[]{:S(2)}, u32[]{:S(2)}) collective-permute-start(bf16[256,1024]{1,0:T(8,128)(2,1)} %attend.6.refs_1_), channel_id=1, source_target_pairs={{0,8},{4,12},{8,0},{12,4},{1,9},{5,13},{9,1},{13,5},{2,10},{6,14},... | collective-permute-start | bytes 1572872 | tf_op jit(solution)/shard_map/ppermute | solution.py:514
  315.3 29.6 %collective-permute-start.33 = (bf16[256,1024]{1,0:T(8,128)(2,1)S(1)}, bf16[256,1024]{1,0:T(8,128)(2,1)S(1)}, u32[]{:S(2)}, u32[]{:S(2)}) collective-permute-start(bf16[256,1024]{1,0:T(8,128)(2,1)S(1)} %copy-done.13), channel_id=1, source_target_pairs={{0,4},{4,0},{8,12},{12,8},{1,5},{5,1},{9,13},{13,9},{2,6},{6,2},{1... | collective-permute-start | bytes 1572872 | tf_op jit(solution)/shard_map/ppermute | solution.py:511
  343.4 16.2 %collective-permute-start.42 = (bf16[256,1024]{1,0:T(8,128)(2,1)S(1)}, bf16[256,1024]{1,0:T(8,128)(2,1)S(1)}, u32[]{:S(2)}, u32[]{:S(2)}) collective-permute-start(bf16[256,1024]{1,0:T(8,128)(2,1)S(1)} %copy-done.18), channel_id=1, source_target_pairs={{0,8},{4,12},{8,0},{12,4},{1,9},{5,13},{9,1},{13,5},{2,10},{6,14},... | collective-permute-start | bytes 1572872 | tf_op jit(solution)/shard_map/ppermute | solution.py:514
  344.9 16.2 %collective-permute-start.41 = (bf16[256,1024]{1,0:T(8,128)(2,1)S(1)}, bf16[256,1024]{1,0:T(8,128)(2,1)S(1)}, u32[]{:S(2)}, u32[]{:S(2)}) collective-permute-start(bf16[256,1024]{1,0:T(8,128)(2,1)S(1)} %copy-done.18), channel_id=1, source_target_pairs={{0,4},{4,0},{8,12},{12,8},{1,5},{5,1},{9,13},{13,9},{2,6},{6,2},{1... | collective-permute-start | bytes 1572872 | tf_op jit(solution)/shard_map/ppermute | solution.py:511
  360.1 44.8 %collective-permute-start.49 = (bf16[256,1024]{1,0:T(8,128)(2,1)S(1)}, bf16[256,1024]{1,0:T(8,128)(2,1)S(1)}, u32[]{:S(2)}, u32[]{:S(2)}) collective-permute-start(bf16[256,1024]{1,0:T(8,128)(2,1)S(1)} %copy-done.57), channel_id=1, source_target_pairs={{1,2},{2,1},{5,6},{6,5},{9,10},{10,9},{13,14},{14,13},{17,18},{18,... | collective-permute-start | bytes 1572872 | tf_op jit(solution)/shard_map/ppermute | solution.py:508
  382.1 26.5 %collective-permute-start.48 = (bf16[256,1024]{1,0:T(8,128)(2,1)}, bf16[256,1024]{1,0:T(8,128)(2,1)S(1)}, u32[]{:S(2)}, u32[]{:S(2)}) collective-permute-start(bf16[256,1024]{1,0:T(8,128)(2,1)} %get-tuple-element.624.refs_1_), channel_id=1, source_target_pairs={{0,1},{3,2},{4,5},{7,6},{8,9},{11,10},{12,13},{15,14},{16,17},{19,... | collective-permute-start | bytes 1572872 | tf_op jit(solution)/shard_map/ppermute | solution.py:508
  384.8 27.4 %collective-permute-start.47 = (bf16[256,1024]{1,0:T(8,128)(2,1)S(1)}, bf16[256,1024]{1,0:T(8,128)(2,1)S(1)}, u32[]{:S(2)}, u32[]{:S(2)}) collective-permute-start(bf16[256,1024]{1,0:T(8,128)(2,1)S(1)} %copy-done.56), channel_id=1, source_target_pairs={{1,2},{2,1},{5,6},{6,5},{9,10},{10,9},{13,14},{14,13},{17,18},{18,... | collective-permute-start | bytes 1572872 | tf_op jit(solution)/shard_map/ppermute | solution.py:508
  385.5 39.2 %collective-permute-start.53 = (bf16[256,1024]{1,0:T(8,128)(2,1)S(1)}, bf16[256,1024]{1,0:T(8,128)(2,1)S(1)}, u32[]{:S(2)}, u32[]{:S(2)}) collective-permute-start(bf16[256,1024]{1,0:T(8,128)(2,1)S(1)} %copy-done.55), channel_id=1, source_target_pairs={{1,2},{2,1},{5,6},{6,5},{9,10},{10,9},{13,14},{14,13},{17,18},{18,... | collective-permute-start | bytes 1572872 | tf_op jit(solution)/shard_map/ppermute | solution.py:508
  386.2 34.9 %collective-permute-start.46 = (bf16[256,1024]{1,0:T(8,128)(2,1)}, bf16[256,1024]{1,0:T(8,128)(2,1)S(1)}, u32[]{:S(2)}, u32[]{:S(2)}) collective-permute-start(bf16[256,1024]{1,0:T(8,128)(2,1)} %get-tuple-element.622.refs_1_), channel_id=1, source_target_pairs={{0,1},{3,2},{4,5},{7,6},{8,9},{11,10},{12,13},{15,14},{16,17},{19,... | collective-permute-start | bytes 1572872 | tf_op jit(solution)/shard_map/ppermute | solution.py:508
  407.9 17.5 %collective-permute-start.55 = (bf16[256,1024]{1,0:T(8,128)(2,1)}, bf16[256,1024]{1,0:T(8,128)(2,1)S(1)}, u32[]{:S(2)}, u32[]{:S(2)}) collective-permute-start(bf16[256,1024]{1,0:T(8,128)(2,1)} %add.213), channel_id=1, source_target_pairs={{1,0},{5,4},{9,8},{13,12},{17,16},{21,20},{25,24},{29,28}} | collective-permute-start | bytes 1572872 | tf_op jit(solution)/shard_map/ppermute | solution.py:508
  411.5 14.7 %collective-permute-start.54 = (bf16[256,1024]{1,0:T(8,128)(2,1)}, bf16[256,1024]{1,0:T(8,128)(2,1)S(1)}, u32[]{:S(2)}, u32[]{:S(2)}) collective-permute-start(bf16[256,1024]{1,0:T(8,128)(2,1)} %add.214), channel_id=1, source_target_pairs={{1,2},{2,1},{5,6},{6,5},{9,10},{10,9},{13,14},{14,13},{17,18},{18,... | collective-permute-start | bytes 1572872 | tf_op jit(solution)/shard_map/ppermute | solution.py:508
  412.2 26.0 %collective-permute-start.52 = (bf16[256,1024]{1,0:T(8,128)(2,1)S(1)}, bf16[256,1024]{1,0:T(8,128)(2,1)S(1)}, u32[]{:S(2)}, u32[]{:S(2)}) collective-permute-start(bf16[256,1024]{1,0:T(8,128)(2,1)S(1)} %copy-done.58), channel_id=1, source_target_pairs={{0,1},{3,2},{4,5},{7,6},{8,9},{11,10},{12,13},{15,14},{16,17},{19,... | collective-permute-start | bytes 1572872 | tf_op jit(solution)/shard_map/ppermute | solution.py:508
  424.0 17.1 %collective-permute-start.51 = (bf16[256,1024]{1,0:T(8,128)(2,1)}, bf16[256,1024]{1,0:T(8,128)(2,1)S(1)}, u32[]{:S(2)}, u32[]{:S(2)}) collective-permute-start(bf16[256,1024]{1,0:T(8,128)(2,1)} %add.215), channel_id=1, source_target_pairs={{1,0},{5,4},{9,8},{13,12},{17,16},{21,20},{25,24},{29,28}} | collective-permute-start | bytes 1572872 | tf_op jit(solution)/shard_map/ppermute | solution.py:508
  424.7 16.4 %collective-permute-start.50 = (bf16[256,1024]{1,0:T(8,128)(2,1)}, bf16[256,1024]{1,0:T(8,128)(2,1)S(1)}, u32[]{:S(2)}, u32[]{:S(2)}) collective-permute-start(bf16[256,1024]{1,0:T(8,128)(2,1)} %add.216), channel_id=1, source_target_pairs={{1,2},{2,1},{5,6},{6,5},{9,10},{10,9},{13,14},{14,13},{17,18},{18,... | collective-permute-start | bytes 1572872 | tf_op jit(solution)/shard_map/ppermute | solution.py:508
  425.5 18.6 %collective-permute-start.45 = (bf16[256,1024]{1,0:T(8,128)(2,1)S(1)}, bf16[256,1024]{1,0:T(8,128)(2,1)S(1)}, u32[]{:S(2)}, u32[]{:S(2)}) collective-permute-start(bf16[256,1024]{1,0:T(8,128)(2,1)S(1)} %copy-done.53), channel_id=1, source_target_pairs={{1,2},{2,1},{5,6},{6,5},{9,10},{10,9},{13,14},{14,13},{17,18},{18,... | collective-permute-start | bytes 1572872 | tf_op jit(solution)/shard_map/ppermute | solution.py:508
  426.3 21.6 %collective-permute-start.44 = (bf16[256,1024]{1,0:T(8,128)(2,1)S(1)}, bf16[256,1024]{1,0:T(8,128)(2,1)S(1)}, u32[]{:S(2)}, u32[]{:S(2)}) collective-permute-start(bf16[256,1024]{1,0:T(8,128)(2,1)S(1)} %copy-done.54), channel_id=1, source_target_pairs={{0,1},{3,2},{4,5},{7,6},{8,9},{11,10},{12,13},{15,14},{16,17},{19,... | collective-permute-start | bytes 1572872 | tf_op jit(solution)/shard_map/ppermute | solution.py:508
  438.2 15.2 %collective-permute-start.59 = (bf16[256,1024]{1,0:T(8,128)(2,1)}, bf16[256,1024]{1,0:T(8,128)(2,1)S(1)}, u32[]{:S(2)}, u32[]{:S(2)}) collective-permute-start(bf16[256,1024]{1,0:T(8,128)(2,1)} %add.218), channel_id=1, source_target_pairs={{1,0},{5,4},{9,8},{13,12},{17,16},{21,20},{25,24},{29,28}} | collective-permute-start | bytes 1572872 | tf_op jit(solution)/shard_map/ppermute | solution.py:508
  447.0 7.8 %collective-permute-start.58 = (bf16[256,1024]{1,0:T(8,128)(2,1)}, bf16[256,1024]{1,0:T(8,128)(2,1)S(1)}, u32[]{:S(2)}, u32[]{:S(2)}) collective-permute-start(bf16[256,1024]{1,0:T(8,128)(2,1)} %add.219), channel_id=1, source_target_pairs={{1,2},{2,1},{5,6},{6,5},{9,10},{10,9},{13,14},{14,13},{17,18},{18,... | collective-permute-start | bytes 1572872 | tf_op jit(solution)/shard_map/ppermute | solution.py:508
  452.2 26.8 %collective-permute-start.60 = (bf16[256,1024]{1,0:T(8,128)(2,1)S(1)}, bf16[256,1024]{1,0:T(8,128)(2,1)S(1)}, u32[]{:S(2)}, u32[]{:S(2)}) collective-permute-start(bf16[256,1024]{1,0:T(8,128)(2,1)S(1)} %copy-done.59), channel_id=1, source_target_pairs={{2,3},{6,7},{10,11},{14,15},{18,19},{22,23},{26,27},{30,31}} | collective-permute-start | bytes 1572872 | tf_op jit(solution)/shard_map/ppermute | solution.py:508
  453.5 36.7 %collective-permute-start.61 = (bf16[256,1024]{1,0:T(8,128)(2,1)}, bf16[256,1024]{1,0:T(8,128)(2,1)S(1)}, u32[]{:S(2)}, u32[]{:S(2)}) collective-permute-start(bf16[256,1024]{1,0:T(8,128)(2,1)} %add.220), channel_id=1, source_target_pairs={{2,3},{6,7},{10,11},{14,15},{18,19},{22,23},{26,27},{30,31}} | collective-permute-start | bytes 1572872 | tf_op jit(solution)/shard_map/ppermute | solution.py:508
  461.5 39.9 %collective-permute-start.63 = (bf16[256,1024]{1,0:T(8,128)(2,1)}, bf16[256,1024]{1,0:T(8,128)(2,1)S(1)}, u32[]{:S(2)}, u32[]{:S(2)}) collective-permute-start(bf16[256,1024]{1,0:T(8,128)(2,1)} %add.224), channel_id=1, source_target_pairs={{2,3},{6,7},{10,11},{14,15},{18,19},{22,23},{26,27},{30,31}} | collective-permute-start | bytes 1572872 | tf_op jit(solution)/shard_map/ppermute | solution.py:508
  462.9 46.0 %collective-permute-start.62 = (bf16[256,1024]{1,0:T(8,128)(2,1)}, bf16[256,1024]{1,0:T(8,128)(2,1)S(1)}, u32[]{:S(2)}, u32[]{:S(2)}) collective-permute-start(bf16[256,1024]{1,0:T(8,128)(2,1)} %add.223), channel_id=1, source_target_pairs={{2,3},{6,7},{10,11},{14,15},{18,19},{22,23},{26,27},{30,31}} | collective-permute-start | bytes 1572872 | tf_op jit(solution)/shard_map/ppermute | solution.py:508
  (99 other events, 881.1 us)

commit v2 on v1

--- a/solution.py
+++ b/solution.py
@@ -26,8 +26,6 @@
 
 HINT = pl.CostEstimate(flops=1024, bytes_accessed=1024, transcendentals=0)
 
-LONGER = pl.CostEstimate(flops=1024, bytes_accessed=2**25, transcendentals=0)
-
 
 def params(**kw):
     return pltpu.CompilerParams(vmem_limit_bytes=VMEM_LIMIT, **kw)
@@ -44,72 +42,89 @@
 PER = 2
 
 
-def project_kernel(s_ref, *refs, sources):
+def project_kernel(s_ref, *refs, pieces, sources, blocks):
     x_refs, refs = refs[:sources], refs[sources:]
-    w_refs, (*peer_refs, own_ref, x_ref, sem) = refs[:PER], refs[PER:]
+    w_refs, refs = refs[:PER], refs[PER:]
+    out_refs, (x_ref, sem) = refs[:-2], refs[-2:]
     step = pl.program_id(0)
     half = x_refs[0].shape[0]
-
-    def fetch(pair):
-        for i, ref in enumerate(pair):
-            pltpu.make_async_copy(ref, x_ref.at[pl.ds(i * half, half)], sem.at[i]).start()
-        for i, ref in enumerate(pair):
-            pltpu.make_async_copy(ref, x_ref.at[pl.ds(i * half, half)], sem.at[i]).wait()
+    rows = x_ref.shape[0] // blocks
+
+    def fetch(group):
+        copies = [
+            pltpu.make_async_copy(ref, x_ref.at[pl.ds(i * half, half)], sem.at[i])
+            for i, ref in enumerate(group)
+        ]
+        for c in copies:
+            c.start()
+        for c in copies:
+            c.wait()
 
     @pl.when(step == 0)
     def _():
-        if sources == 2:
+        if sources == pieces:
             fetch(x_refs)
         else:
 
             @pl.when(s_ref[0] == 1)
             def _():
-                fetch(x_refs[:2])
+                fetch(x_refs[:pieces])
 
             @pl.when(s_ref[0] == 0)
             def _():
-                fetch(x_refs[2:])
+                fetch(x_refs[pieces:])
 
     peer_steps = 10 // PER
     products = [jnp.dot(x_ref[...], w[...], preferred_element_type=F32) for w in w_refs]
 
     @pl.when(step < peer_steps)
     def _():
-        for v, o_ref in zip(products, peer_refs):
-            o_ref[...] = v.astype(BF16)
+        for b in range(blocks):
+            for i, v in enumerate(products):
+                out_refs[3 * b + i][...] = v[b * rows : (b + 1) * rows].astype(BF16)
 
     @pl.when(step >= peer_steps)
     def _():
-        for i, v in enumerate(products):
-            own_ref[:, i * TILE : (i + 1) * TILE] = v
-
-
-def project(info, xs, w):
+        for b in range(blocks):
+            for i, v in enumerate(products):
+                cut = slice(i * TILE, (i + 1) * TILE)
+                out_refs[3 * b + 2][:, cut] = v[b * rows : (b + 1) * rows]
+
+
+def project(info, xs, w, pieces=2):
     half, depth = xs[0].shape
     peer_steps = 10 // PER
     steps = 18 // PER
+    blocks = pieces // 2
     weights = [
         pl.BlockSpec((depth, TILE), lambda j, s, i=i: (0, s[1 + j * PER + i])) for i in range(PER)
     ]
     rows = 2 * half
-    return pl.pallas_call(
-        lambda *refs: project_kernel(*refs, sources=len(xs)),
+    peer = pl.BlockSpec((rows, TILE), lambda j, s: (0, jnp.minimum(j, peer_steps - 1)))
+    own = pl.BlockSpec((rows, PER * TILE), lambda j, s: (0, jnp.maximum(j - peer_steps, 0)))
+    out = pl.pallas_call(
+        lambda *refs: project_kernel(*refs, pieces=pieces, sources=len(xs), blocks=blocks),
         grid_spec=pltpu.PrefetchScalarGridSpec(
             num_scalar_prefetch=1,
             grid=(steps,),
             in_specs=[pl.BlockSpec(memory_space=pl.ANY)] * len(xs) + weights,
-            out_specs=[
-                pl.BlockSpec((rows, TILE), lambda j, s: (0, jnp.minimum(j, peer_steps - 1))),
-                pl.BlockSpec((rows, TILE), lambda j, s: (0, jnp.minimum(j, peer_steps - 1))),
-                pl.BlockSpec((rows, PER * TILE), lambda j, s: (0, jnp.maximum(j - peer_steps, 0))),
+            out_specs=[peer, peer, own] * blocks,
+            scratch_shapes=[
+                pltpu.VMEM((half * pieces, depth), BF16),
+                pltpu.SemaphoreType.DMA((pieces,)),
             ],
-            scratch_shapes=[pltpu.VMEM((rows, depth), BF16), pltpu.SemaphoreType.DMA((2,))],
-        ),
-        out_shape=[sds((rows, 5 * TILE), BF16)] * 2 + [sds((rows, 8 * TILE), F32)],
+        ),
+        out_shape=[
+            sds((rows, 5 * TILE), BF16),
+            sds((rows, 5 * TILE), BF16),
+            sds((rows, 8 * TILE), F32),
+        ]
+        * blocks,
         compiler_params=params(),
         cost_estimate=HINT,
         name="project",
     )(info, *xs, *([w] * PER))
+    return out
 
 
 def core_sums(s_ref, own_ref, kv_refs, recv_refs):
@@ -214,9 +229,9 @@
 
 
 def attend_kernel(
-    s_ref, q_ref, k_ref, v_ref, ka_ref, kb_ref, va_ref, vb_ref, o_ref, vx_ref, acc_ref, top_ref
+    s_ref, q_ref, k_ref, v_ref, ka_ref, kb_ref, va_ref, vb_ref, o_ref, vx_ref, acc_ref, top_ref, at
 ):
-    prefix, live, half = s_ref[2], s_ref[3], s_ref[4]
+    prefix, live, half = s_ref[at + 2], s_ref[at + 3], s_ref[at + 4]
     rows = ka_ref.shape[0]
     m_rows = q_ref.shape[0]
     span = k_ref.shape[1]
@@ -278,8 +293,8 @@
 
         @pl.when(rest > 0)
         def _():
-            at = block(count)
-            cuts(PIECE, lambda cut: add(rest_scores(cut, at), cut, at))
+            last = block(count)
+            cuts(PIECE, lambda cut: add(rest_scores(cut, last), cut, last))
 
         cuts(CHUNK, lambda cut: blocks(count, lambda at: add(scores(cut, at), cut, at)))
 
@@ -294,8 +309,8 @@
 
             @pl.when(rest > 0)
             def _():
-                at = block(count)
-                cuts(PIECE, lambda cut: raise_top(rest_scores(cut, at), cut))
+                last = block(count)
+                cuts(PIECE, lambda cut: raise_top(rest_scores(cut, last), cut))
 
         sweep()
         return jnp.max(jnp.where(acc_ref[:, HD:] < LARGE, 0.0, 1.0))
@@ -310,15 +325,16 @@
         o_ref[:, h * HD : (h + 1) * HD] = (acc_ref[cut, :HD] / acc_ref[cut, HD:]).astype(BF16)
 
 
-def attend(info, q, key_cache, value_cache, ka, kb, va, vb):
+def attend(info, slot, q, key_cache, value_cache, ka, kb, va, vb):
     heads, rows, _ = q.shape
     span = key_cache.shape[1]
     m_rows = heads * rows
+    at = 5 * slot
     q = q.reshape(m_rows, HD)
-    cache = pl.BlockSpec((1, span, HD), lambda i, s: (s[0], 0, s[1]))
+    cache = pl.BlockSpec((1, span, HD), lambda i, s: (s[at], 0, s[at + 1]))
     fresh = pl.BlockSpec((rows, HD), whole)
     return pl.pallas_call(
-        attend_kernel,
+        lambda *refs: attend_kernel(*refs, at=at),
         grid_spec=pltpu.PrefetchScalarGridSpec(
             num_scalar_prefetch=1,
             grid=(1,),
@@ -425,30 +441,29 @@
         ),
         out_shape=sds(a.shape, a.dtype),
         compiler_params=params(),
-        cost_estimate=LONGER,
+        cost_estimate=HINT,
         name="choose",
     )(flag.astype(jnp.int32)[None], a, b)
 
 
-def add_kernel(*refs):
-    total = refs[0][...].astype(F32)
-    for ref in refs[1:-1]:
-        total += ref[...].astype(F32)
-    refs[-1][...] = total.astype(BF16)
-
-
-def add(*xs):
-    rows, cols = xs[0].shape
-    block = pl.BlockSpec((rows, cols), lambda: (0, 0))
+def add_kernel(a_ref, b_ref, o_ref):
+    o_ref[...] = (a_ref[...].astype(F32) + b_ref[...].astype(F32)).astype(BF16)
+
+
+def add(a, b, part=0, cuts=1):
+    shape = (a.shape[0], a.shape[1] // cuts)
+    there = pl.BlockSpec(shape, lambda i: (0, part))
+    block = pl.BlockSpec(shape, lambda i: (0, 0))
     return pl.pallas_call(
         add_kernel,
-        in_specs=[block] * len(xs),
+        grid=(1,),
+        in_specs=[block if cuts == 1 else there, there],
         out_specs=block,
-        out_shape=sds((rows, cols), BF16),
+        out_shape=sds(shape, BF16),
         compiler_params=params(),
         cost_estimate=HINT,
         name="add",
-    )(*xs)
+    )(a, b)
 
 
 def in_turn_kernel(s_ref, ka_ref, kb_ref, va_ref, vb_ref, k0_ref, k1_ref, v0_ref, v1_ref):
@@ -550,9 +565,16 @@
         sign = jnp.where(lane < HD // 2, -1.0, 1.0).astype(F32)
         return jnp.cos(angles), jnp.sin(angles) * sign[None, :]
 
-    def attention(q, req, part, ka, kb, va, vb):
-        info = jnp.stack([req, chip, prefix_len[req], stretch_len[req], part]).astype(jnp.int32)
-        return attend(info, q, key_cache, value_cache, ka, kb, va, vb)
+    parts = [(request, second), (request, 1 - second), (other, 0 * z), (other, 0 * z + 1)]
+
+    def numbers(prefix):
+        values = [
+            v for req, part in parts for v in (req, chip, prefix[req], stretch_len[req], part)
+        ]
+        return jnp.stack(values).astype(jnp.int32)
+
+    def attention(slot, q, ka, kb, va, vb):
+        return attend(info, slot, q, key_cache, value_cache, ka, kb, va, vb)
 
     at_two = z == 2
     squares = do(row_squares, tokens)
@@ -583,10 +605,11 @@
     a0 = wait(a0)
     m0 = along(do(lambda x: choose(at_two, own_a, x), a0), middle)
     cos, sin = do(tables, starts)
+    info = do(numbers, prefix_len)
+    recv_o = wait(recv_o)
+    cross_o = over_chip(do(lambda x: combine(chip, keep_o, mine_o, x), recv_o))
     a1 = wait(a1)
     m1 = along(do(lambda x: choose(at_two, own_b, x), a1), middle)
-    recv_o = wait(recv_o)
-    cross_o = over_chip(do(lambda x: combine(chip, keep_o, mine_o, x), recv_o))
     m0 = wait(m0)
     n0 = along(m0, outward)
 
@@ -602,6 +625,7 @@
     q_o, k_o, v_o = do(
         lambda x: finish(chip, keep_o, mine_o, recv_o, x, cos, sin, 0), cross_o
     )
+    n1 = wait(n1)
     cross_a = wait(cross_a)
     q_a, k_a, v_a = do(
         lambda x: finish(chip, keep_a, mine_a, recv_a, x, cos, sin, 1), cross_a
@@ -611,45 +635,70 @@
     m2 = wait(m2)
     n2 = along(m2, outward)
     m3 = along(do(lambda x: choose(at_two, x, own_b), a1), middle)
-    att_a = do(lambda q: attention(q, request, 1 - second, k0, k1, v0, v1), q_a)
+    att_a = do(lambda q: attention(1, q, k0, k1, v0, v1), q_a)
     att_ax = over_chip(att_a)
     att_ac = over_core(att_a)
-
-    n1 = wait(n1)
-    *mine_b, keep_b = do(lambda x: project(tiles, [x, m1, n0, n1], qkv_weight), m0)
-    recv_b = [over_core(x) for x in mine_b]
-    n2 = wait(n2)
     m3 = wait(m3)
     n3 = along(m3, outward)
+    att_o = do(lambda q: attention(0, q, k0, k1, v0, v1), q_o)
+    att_ox = over_chip(att_o)
+    att_oc = over_core(att_o)
+    n2 = wait(n2)
     att_ax = wait(att_ax)
     att_ad = over_core(att_ax)
     att_ac, att_ad = wait((att_ac, att_ad))
+    part_a = do(
+        lambda a: out_project(
+            spots, [a, att_ac, att_ax, att_ad], out_weight, None, 0, width, BF16, 2
+        ),
+        att_a,
+    )
+    sum_a = [along(x, inward) for x in part_a]
+
+    att_ox = wait(att_ox)
+    att_od = over_core(att_ox)
+    n3 = wait(n3)
+    out = do(
+        lambda x: project(tiles, [x, m1, m2, m3, n0, n1, n2, n3], qkv_weight, 4), m0
+    )
+    *mine_b, keep_b = out[:3]
+    *mine_c, keep_c = out[3:]
+    recv_b = [over_core(x) for x in mine_b]
+    recv_c = [over_core(x) for x in mine_c]
+    att_oc, att_od = wait((att_oc, att_od))
+    sum_a[0] = wait(sum_a[0])
     recv_b = wait(recv_b)
     cross_b = over_chip(do(lambda x: combine(chip, keep_b, mine_b, x), recv_b))
-    part_a = do(
-        lambda a: out_project(
-            spots, [a, att_ac, att_ax, att_ad], out_weight, None, 0, width, BF16, pieces
-        ),
-        att_a,
-    )
-    sum_a = [along(x, inward) for x in part_a]
-    n3 = wait(n3)
+    recv_c = wait(recv_c)
+    cross_c = over_chip(do(lambda x: combine(chip, keep_c, mine_c, x), recv_c))
+    def output_own(i):
+        cut = width // 2
+        return do(
+            lambda a: out_project(
+                spots, [a, att_oc, att_ox, att_od], out_weight, None, i * cut, cut, BF16, 2
+            ),
+            att_o,
+        )
+
+    part_o = output_own(0)
+    sum_a[1] = wait(sum_a[1])
     cross_b = wait(cross_b)
     q_b, k_b, v_b = do(
         lambda x: finish(chip, keep_b, mine_b, recv_b, x, cos, sin, 2), cross_b
     )
-    att_b = do(lambda q: attention(q, other, 0, k_b, k_b, v_b, v_b), q_b)
+    att_b = do(lambda q: attention(2, q, k_b, k_b, v_b, v_b), q_b)
     att_bx = over_chip(att_b)
     att_bc = over_core(att_b)
-
-    *mine_c, keep_c = do(lambda x: project(tiles, [x, m3, n2, n3], qkv_weight), m2)
-    recv_c = [over_core(x) for x in mine_c]
-    sum_a = wait(sum_a)
+    cross_c = wait(cross_c)
+    q_c, k_c, v_c = do(
+        lambda x: finish(chip, keep_c, mine_c, recv_c, x, cos, sin, 3), cross_c
+    )
+    att_c = do(lambda q: attention(3, q, k_b, k_c, v_b, v_c), q_c)
+    att_cx = over_chip(att_c)
+    att_cc = over_core(att_c)
     att_bx = wait(att_bx)
     att_bd = over_core(att_bx)
     att_bc, att_bd = wait((att_bc, att_bd))
-    recv_c = wait(recv_c)
-    cross_c = over_chip(do(lambda x: combine(chip, keep_c, mine_c, x), recv_c))
     part_b = do(
         lambda a: out_project(
             spots, [a, att_bc, att_bx, att_bd], out_weight, None, 0, width, BF16, pieces
@@ -657,78 +706,50 @@
         att_b,
     )
     b1 = [along(x, inward) for x in part_b]
-    att_o = do(lambda q: attention(q, request, second, k0, k1, v0, v1), q_o)
-    att_ox = over_chip(att_o)
-    att_oc = over_core(att_o)
-    cross_c = wait(cross_c)
-    q_c, k_c, v_c = do(
-        lambda x: finish(chip, keep_c, mine_c, recv_c, x, cos, sin, 3), cross_c
-    )
-    b2, b3, c2, c3 = [], [], [], []
-
-    def pass_b1(i):
-        b1[i] = wait(b1[i])
-        b2.append(along(do(add, b1[i], part_b[i]), middle))
-
-    def pass_b2(i):
-        b2[i] = wait(b2[i])
-        b3.append(along(do(add, b2[i], part_a[i]), [(1, 0)]))
-
-    def pass_c1(i):
-        c1[i] = wait(c1[i])
-        c2.append(along(do(add, c1[i], part_c[i]), middle))
-
-    def pass_c2(i):
-        c2[i] = wait(c2[i])
-        c3.append(along(do(add, c2[i], part_a[i]), [(2, 3)]))
-
-    def output_own(i):
-        return do(
-            lambda a: out_project(
-                spots,
-                [a, att_oc, att_ox, att_od],
-                out_weight,
-                None,
-                i * (width // 2),
-                width // 2,
-                BF16,
-                pieces // 2,
-            ),
-            att_o,
-        )
-
-    pass_b1(0)
-    att_c = do(lambda q: attention(q, other, 1, k_b, k_c, v_b, v_c), q_c)
-    att_cx = over_chip(att_c)
-    att_cc = over_core(att_c)
-    for i in range(1, pieces):
-        pass_b1(i)
-    att_ox = wait(att_ox)
-    att_od = over_core(att_ox)
-    att_oc, att_od = wait((att_oc, att_od))
-    part_o = output_own(0)
     att_cx = wait(att_cx)
     att_cd = over_core(att_cx)
     att_cc, att_cd = wait((att_cc, att_cd))
     part_c = do(
         lambda a: out_project(
-            spots, [a, att_cc, att_cx, att_cd], out_weight, None, 0, width, BF16, pieces
+            spots, [a, att_cc, att_cx, att_cd], out_weight, None, 0, width, BF16, 2
         ),
         att_c,
     )
     c1 = [along(x, inward) for x in part_c]
+    b2, b3, c2, c3 = [], [], [], []
+
+    def pass_b1(i):
+        b1[i] = wait(b1[i])
+        b2.append(along(do(add, b1[i], part_b[i]), middle))
+
+    def pass_b2(i):
+        b2[i] = wait(b2[i])
+        b3.append(along(do(add, b2[i], part_a[i // 2], i % 2), [(1, 0)]))
+
+    def pass_c1(i):
+        c1[i // 2] = wait(c1[i // 2])
+        c2.append(along(do(add, c1[i // 2], part_c[i // 2], i % 2, 2), middle))
+
+    def pass_c2(i):
+        c2[i] = wait(c2[i])
+        c3.append(along(do(add, c2[i], part_a[i // 2], i % 2), [(2, 3)]))
+
+    pass_b1(0)
+    pass_b1(1)
+    pass_b1(2)
     part_o += output_own(1)
+    pass_b1(3)
     pass_b2(0)
+    pass_b2(1)
     pass_c1(0)
-    pass_b2(1)
     pass_c1(1)
+    pass_b2(2)
+    pass_b2(3)
+    pass_c2(0)
+    pass_c2(1)
     b3[0] = wait(b3[0])
-    pass_c2(0)
-    pass_b2(2)
+    b3[1] = wait(b3[1])
     pass_c1(2)
-    b3[1] = wait(b3[1])
-    pass_c2(1)
-    pass_b2(3)
     pass_c1(3)
     b3[2] = wait(b3[2])
     pass_c2(2)

time: 523 us -> 517 us (0.989)
  waiting for transfers between devices: 69.4 us -> 94.3 us
  Pallas kernels: 307 us -> 296 us
  starting transfers between devices: 83.3 us -> 74 us
  local copies, waits for them, and re-layouts: 34 us -> 28.3 us
    ppermute x38 -> x34, waiting for transfers between devices: 49.2 us -> 90.8 us  [along(): return lax.ppermute(x, 'gy', pairs)]
    ppermute x9, waiting for transfers between devices: 13.8 us -> 2.09 us  [over_chip(): return lax.ppermute(x, 'gx', [(i, i ^ 2) for i in range(4)])]
    pallas_call x24 -> x23, Pallas kernels: 191 us -> 179 us  [the longest x3 73.2 us: project(): pl.pallas_call(lambda *refs: project_kernel(*refs, pieces=pieces, sources...]
    ppermute x38 -> x34, starting transfers between devices: 68.8 us -> 58.7 us  [along(): return lax.ppermute(x, 'gy', pairs)]
    unnamed x167 -> x133, local copies, waits for them, and re-layouts: 25.5 us -> 20.9 us
  transfers between devices with their start and end apart: 64 -> 60, of which waited for: 14 -> 13; matrix products, arithmetic and copies ran while one was open for 3% -> 3% of each run, Pallas kernels for 59% -> 57%
where the time goes in v2:
time: 517 us; the launch traced here: 511 us
  Pallas kernels  296 us (57%)
  waiting for transfers between devices  94.3 us (18%)
  starting transfers between devices  74 us (14%)
  local copies, waits for them, and re-layouts  28.3 us (5%)
  other arithmetic  16 us (3%)
    ppermute x34, waiting for transfers between devices, along(): return lax.ppermute(x, 'gy', pairs)  90.8 us
    pallas_call x5, Pallas kernels, out_project(): pl.pallas_call(lambda *refs: out_kernel(*refs, sources=n, before=before i...  84.4 us
    pallas_call x3, Pallas kernels, project(): pl.pallas_call(lambda *refs: project_kernel(*refs, pieces=pieces, sources...  73.2 us
    pallas_call x4, Pallas kernels, attend(): pl.pallas_call(lambda *refs: attend_kernel(*refs, at=at), grid_spec=pltpu...  72 us
    ppermute x34, starting transfers between devices, along(): return lax.ppermute(x, 'gy', pairs)  58.7 us
    pallas_call x16, Pallas kernels, add(): pl.pallas_call(add_kernel, grid=(1,), in_specs=[block if cuts == 1 else t...  34.2 us
    unnamed x133, local copies, waits for them, and re-layouts  20.9 us
    pallas_call x4, Pallas kernels, finish(): pl.pallas_call(finish_kernel, grid_spec=pltpu.PrefetchScalarGridSpec(num_...  11.2 us
  transfers between devices with their start and end apart: 60, of which 13 were waited for; matrix products, arithmetic and copies ran while one was open for 3% of the time, Pallas kernels for 57%

profile of v2, /device:TPU:28, one launch (start us, length us, event | category | flops | bytes accessed | tf_op | source)
XLA Modules:
  0.0 511.5 jit_solution(5225990163505671051)
XLA Ops:
  0.0 2.2 multiply_reduce_fusion
  11.8 22.0 %project.3 = (bf16[256,1280]{1,0:T(8,128)(2,1)}, bf16[256,1280]{1,0:T(8,128)(2,1)}, f32[256,2048]{1,0:T(8,128)}) custom-call(s32[19]{0:T(128)} %pad_add_fusion.1.refs_0_, bf16[128,4096]{1,0:T(8,128)(2,1)} %copy-done.1, bf16[128,4096]{1,0:T(8,128)(2,1)} %copy-done, bf16[4096,4608]{1,0:T(8,128)(2,1)} %refs_10_.1, bf16[4096,4608]{1,0:T(8,128)(2,1)} %refs_10_.1), custom_call_target="tpu_custom_call" | custom-call | flops 1024 | bytes 1024 | tf_op jit(solution)/shard_map/project/pallas_call | solution.py:105
  35.8 2.4 choose.4
  43.7 3.1 fusion
  47.4 5.4 %stack.61.refs_0_ = s32[20]{0:T(128)} concatenate(s32[1]{0:T(128)} %bitcast.4, s32[1]{0:T(128)} %bitcast.5.s_ref, s32[1]{0:T(128)} %get-tuple-element.707, s32[1]{0:T(128)} %get-tuple-element.702, s32[1]{0:T(128)} %bitcast.14, s32[1]{0:T(128)} %bitcast.4, s32[1]{0:T(128)} %bitcast.5.s_ref, s32[1]{0:T(128)} %get-tuple-element.707, s32[1]{0:T(128)} %get-tuple-element.702, ...), dimensions={0} | concatenate | bytes 160 | tf_op jit(solution)/shard_map/stack | solution.py:574
  54.0 2.3 combine.4
  57.3 2.4 choose.5
  63.2 22.1 %project.4 = (bf16[256,1280]{1,0:T(8,128)(2,1)}, bf16[256,1280]{1,0:T(8,128)(2,1)}, f32[256,2048]{1,0:T(8,128)}) custom-call(s32[19]{0:T(128)} %pad_add_fusion.1.refs_0_, bf16[128,4096]{1,0:T(8,128)(2,1)} %copy-done.12, bf16[128,4096]{1,0:T(8,128)(2,1)} %copy-done.11, bf16[4096,4608]{1,0:T(8,128)(2,1)} %refs_10_.1, bf16[4096,4608]{1,0:T(8,128)(2,1)} %refs_10_.1), custom_call_target="tpu_custom_call" | custom-call | flops 1024 | bytes 1024 | tf_op jit(solution)/shard_map/project/pallas_call | solution.py:105
  88.2 2.4 choose.6
  94.0 2.3 combine.5
  97.9 2.8 finish.4
  100.7 16.0 %collective-permute-done.14.refs_6_ = bf16[128,4096]{1,0:T(8,128)(2,1)} collective-permute-done((bf16[128,4096]{1,0:T(8,128)(2,1)S(1)}, bf16[128,4096]{1,0:T(8,128)(2,1)}, u32[]{:S(2)}, u32[]{:S(2)}) %collective-permute-start.14) | collective-permute-done | bytes 1048608 | tf_op jit(solution)/shard_map/ppermute | solution.py:523
  116.7 2.8 finish.5
  121.2 2.4 choose.7
  125.8 17.7 %attend.4.refs_1_ = bf16[256,1024]{1,0:T(8,128)(2,1)} custom-call(s32[20]{0:T(128)} %stack.61.refs_0_, bf16[2048,128]{1,0:T(8,128)(2,1)} %bitcast.31, bf16[2,3072,256]{2,1,0:T(8,128)(2,1)} %refs_2_.7, bf16[2,3072,256]{2,1,0:T(8,128)(2,1)} %refs_3_.11, bf16[256,128]{1,0:T(8,128)(2,1)} %get-tuple-element.465.refs_4_, ...), custom_call_target="tpu_custom_call" | custom-call | flops 1024 | bytes 1024 | tf_op jit(solution)/shard_map/attend/pallas_call | solution.py:336
  144.0 17.7 %attend.5.refs_1_ = bf16[256,1024]{1,0:T(8,128)(2,1)} custom-call(s32[20]{0:T(128)} %stack.61.refs_0_, bf16[2048,128]{1,0:T(8,128)(2,1)} %bitcast.30, bf16[2,3072,256]{2,1,0:T(8,128)(2,1)} %refs_2_.7, bf16[2,3072,256]{2,1,0:T(8,128)(2,1)} %refs_3_.11, bf16[256,128]{1,0:T(8,128)(2,1)} %get-tuple-element.465.refs_4_, ...), custom_call_target="tpu_custom_call" | custom-call | flops 1024 | bytes 1024 | tf_op jit(solution)/shard_map/attend/pallas_call | solution.py:336
  165.8 19.4 %out_project.5 = (bf16[256,2048]{1,0:T(8,128)(2,1)}, bf16[256,2048]{1,0:T(8,128)(2,1)}) custom-call(s32[5]{0:T(128)} %stack.52.refs_0_, bf16[256,1024]{1,0:T(8,128)(2,1)} %attend.4.refs_1_, bf16[256,1024]{1,0:T(8,128)(2,1)} %collective-permute-done.18.refs_2_, bf16[256,1024]{1,0:T(8,128)(2,1)} %copy-done.45, ...), custom_call_target="tpu_custom_call" | custom-call | flops 1024 | bytes 1024 | tf_op jit(solution)/shard_map/out_project/pallas_call | solution.py:406
  185.3 12.3 %collective-permute-start.26 = (bf16[256,2048]{1,0:T(8,128)(2,1)}, bf16[256,2048]{1,0:T(8,128)(2,1)S(1)}, u32[]{:S(2)}, u32[]{:S(2)}) collective-permute-start(bf16[256,2048]{1,0:T(8,128)(2,1)} %get-tuple-element.510.b_ref), channel_id=1, source_target_pairs={{0,1},{3,2},{4,5},{7,6},{8,9},{11,10},{12,13},{15,14},{16,17},{19,... | collective-permute-start | bytes 3145736 | tf_op jit(solution)/shard_map/ppermute | solution.py:523
  198.2 29.1 %project.5 = (bf16[256,1280]{1,0:T(8,128)(2,1)}, bf16[256,1280]{1,0:T(8,128)(2,1)}, f32[256,2048]{1,0:T(8,128)}, bf16[256,1280]{1,0:T(8,128)(2,1)}, bf16[256,1280]{1,0:T(8,128)(2,1)}, /*index=5*/f32[256,2048]{1,0:T(8,128)}) custom-call(s32[19]{0:T(128)} %pad_add_fusion.1.refs_0_, bf16[128,4096]{1,0:T(8,128)(2,1)} %collective-permute-done.6.refs_1_, ...), custom_call_target="tpu_custom_call" | custom-call | flops 1024 | bytes 1024 | tf_op jit(solution)/shard_map/project/pallas_call | solution.py:105
  231.8 2.3 combine.6
  236.7 2.3 combine.7
  240.2 13.1 %out_project.6 = (bf16[256,1024]{1,0:T(8,128)(2,1)}, bf16[256,1024]{1,0:T(8,128)(2,1)}) custom-call(s32[5]{0:T(128)} %stack.52.refs_0_, bf16[256,1024]{1,0:T(8,128)(2,1)} %attend.5.refs_1_, bf16[256,1024]{1,0:T(8,128)(2,1)} %copy-done.19, bf16[256,1024]{1,0:T(8,128)(2,1)} %copy-done.18, bf16[256,1024]{1,0:T(8,128)(2,1)} %copy-done.20, bf16[4096,4096]{1,0:T(8,128)(2,1)} %refs_5_.9), custom_call_target="tpu_custom_call" | custom-call | flops 1024 | bytes 1024 | tf_op jit(solution)/shard_map/out_project/pallas_call | solution.py:406
  254.2 2.8 finish.6
  257.0 18.2 %attend.6.refs_1_ = bf16[256,1024]{1,0:T(8,128)(2,1)} custom-call(s32[20]{0:T(128)} %stack.61.refs_0_, bf16[2048,128]{1,0:T(8,128)(2,1)} %bitcast.33, bf16[2,3072,256]{2,1,0:T(8,128)(2,1)} %refs_2_.7, bf16[2,3072,256]{2,1,0:T(8,128)(2,1)} %refs_3_.11, bf16[256,128]{1,0:T(8,128)(2,1)} %get-tuple-element.545.refs_4_.refs_5_, ...), custom_call_target="tpu_custom_call" | custom-call | flops 1024 | bytes 1024 | tf_op jit(solution)/shard_map/attend/pallas_call | solution.py:336
  277.0 2.8 finish.7
  279.8 18.3 %attend.7.refs_1_ = bf16[256,1024]{1,0:T(8,128)(2,1)} custom-call(s32[20]{0:T(128)} %stack.61.refs_0_, bf16[2048,128]{1,0:T(8,128)(2,1)} %bitcast.32, bf16[2,3072,256]{2,1,0:T(8,128)(2,1)} %refs_2_.7, bf16[2,3072,256]{2,1,0:T(8,128)(2,1)} %refs_3_.11, bf16[256,128]{1,0:T(8,128)(2,1)} %get-tuple-element.545.refs_4_.refs_5_, ...), custom_call_target="tpu_custom_call" | custom-call | flops 1024 | bytes 1024 | tf_op jit(solution)/shard_map/attend/pallas_call | solution.py:336
  301.4 19.6 %out_project.7 = (bf16[256,1024]{1,0:T(8,128)(2,1)}, bf16[256,1024]{1,0:T(8,128)(2,1)}, bf16[256,1024]{1,0:T(8,128)(2,1)}, bf16[256,1024]{1,0:T(8,128)(2,1)}) custom-call(s32[5]{0:T(128)} %stack.52.refs_0_, bf16[256,1024]{1,0:T(8,128)(2,1)} %attend.6.refs_1_, bf16[256,1024]{1,0:T(8,128)(2,1)} %copy-done.46, bf16[256,1024]{1,0:T(8,128)(2,1)} %copy-done.44, ...), custom_call_target="tpu_custom_call" | custom-call | flops 1024 | bytes 1024 | tf_op jit(solution)/shard_map/out_project/pallas_call | solution.py:406
  321.6 3.2 collective-permute-start.37
  329.1 19.2 %out_project.8 = (bf16[256,2048]{1,0:T(8,128)(2,1)}, bf16[256,2048]{1,0:T(8,128)(2,1)}) custom-call(s32[5]{0:T(128)} %stack.52.refs_0_, bf16[256,1024]{1,0:T(8,128)(2,1)} %attend.7.refs_1_, bf16[256,1024]{1,0:T(8,128)(2,1)} %copy-done.48, bf16[256,1024]{1,0:T(8,128)(2,1)} %copy-done.47, bf16[256,1024]{1,0:T(8,128)(2,1)} %copy-done.49, bf16[4096,4096]{1,0:T(8,128)(2,1)} %refs_5_.9), custom_call_target="tpu_custom_call" | custom-call | flops 1024 | bytes 1024 | tf_op jit(solution)/shard_map/out_project/pallas_call | solution.py:406
  355.5 2.1 add.210
  360.7 2.1 add.211
  362.8 13.1 %out_project.9 = (bf16[256,1024]{1,0:T(8,128)(2,1)}, bf16[256,1024]{1,0:T(8,128)(2,1)}) custom-call(s32[5]{0:T(128)} %stack.52.refs_0_, bf16[256,1024]{1,0:T(8,128)(2,1)} %attend.5.refs_1_, bf16[256,1024]{1,0:T(8,128)(2,1)} %copy-done.19, bf16[256,1024]{1,0:T(8,128)(2,1)} %copy-done.18, bf16[256,1024]{1,0:T(8,128)(2,1)} %copy-done.20, bf16[4096,4096]{1,0:T(8,128)(2,1)} %refs_5_.9), custom_call_target="tpu_custom_call" | custom-call | flops 1024 | bytes 1024 | tf_op jit(solution)/shard_map/out_project/pallas_call | solution.py:406
  375.9 16.8 %collective-permute-done.44.a_ref = bf16[256,1024]{1,0:T(8,128)(2,1)S(1)} collective-permute-done((bf16[256,1024]{1,0:T(8,128)(2,1)S(1)}, bf16[256,1024]{1,0:T(8,128)(2,1)S(1)}, u32[]{:S(2)}, u32[]{:S(2)}) %collective-permute-start.44) | collective-permute-done | bytes 524320 | tf_op jit(solution)/shard_map/ppermute | solution.py:523
  393.5 2.1 add.212
  397.0 8.9 %collective-permute-start.41 = (bf16[256,2048]{1,0:T(8,128)(2,1)S(1)}, bf16[256,2048]{1,0:T(8,128)(2,1)S(1)}, u32[]{:S(2)}, u32[]{:S(2)}) collective-permute-start(bf16[256,2048]{1,0:T(8,128)(2,1)S(1)} %copy-done.15), channel_id=1, source_target_pairs={{0,1},{3,2},{4,5},{7,6},{8,9},{11,10},{12,13},{15,14},{16,17},{19,... | collective-permute-start | bytes 3145736 | tf_op jit(solution)/shard_map/ppermute | solution.py:523
  406.0 2.1 add.213
  408.9 2.1 add.214
  412.0 2.1 add.215
  414.9 2.1 add.216
  425.9 2.1 add.219
  428.8 2.1 add.220
  432.0 2.3 add.221
  449.8 3.3 add_convert_fusion.1
  453.1 23.8 %collective-permute-done.56 = bf16[256,1024]{1,0:T(8,128)(2,1)} collective-permute-done((bf16[256,1024]{1,0:T(8,128)(2,1)S(1)}, bf16[256,1024]{1,0:T(8,128)(2,1)}, u32[]{:S(2)}, u32[]{:S(2)}) %collective-permute-start.56) | collective-permute-done | bytes 524320 | tf_op jit(solution)/shard_map/ppermute | solution.py:523
  476.9 11.2 %collective-permute-done.57 = bf16[256,1024]{1,0:T(8,128)(2,1)} collective-permute-done((bf16[256,1024]{1,0:T(8,128)(2,1)}, bf16[256,1024]{1,0:T(8,128)(2,1)}, u32[]{:S(2)}, u32[]{:S(2)}) %collective-permute-start.57) | collective-permute-done | bytes 524320 | tf_op jit(solution)/shard_map/ppermute | solution.py:523
  488.1 11.2 %collective-permute-done.58 = bf16[256,1024]{1,0:T(8,128)(2,1)} collective-permute-done((bf16[256,1024]{1,0:T(8,128)(2,1)}, bf16[256,1024]{1,0:T(8,128)(2,1)}, u32[]{:S(2)}, u32[]{:S(2)}) %collective-permute-start.58) | collective-permute-done | bytes 524320 | tf_op jit(solution)/shard_map/ppermute | solution.py:523
  499.3 8.3 %collective-permute-done.59 = bf16[256,1024]{1,0:T(8,128)(2,1)} collective-permute-done((bf16[256,1024]{1,0:T(8,128)(2,1)}, bf16[256,1024]{1,0:T(8,128)(2,1)}, u32[]{:S(2)}, u32[]{:S(2)}) %collective-permute-start.59) | collective-permute-done | bytes 524320 | tf_op jit(solution)/shard_map/ppermute | solution.py:523
  507.7 3.3 add_convert_fusion
  (266 shorter events, 97.8 us)
Async XLA Ops:
  8.6 26.2 %collective-permute-start.2 = (bf16[128,4096]{1,0:T(8,128)(2,1)S(1)}, bf16[128,4096]{1,0:T(8,128)(2,1)S(1)}, u32[]{:S(2)}, u32[]{:S(2)}) collective-permute-start(bf16[128,4096]{1,0:T(8,128)(2,1)S(1)} %multiply_convert_fusion.1.refs_1_.a_ref.b_ref), channel_id=1, source_target_pairs={{0,1},{1,0},{2,3},{3,2},{4,5},{5,4},{6,7},{7,6},{8,9},{9,8},{10,11... | collective-permute-start | bytes 3145736 | tf_op jit(solution)/shard_map/ppermute | solution.py:523
  10.1 46.1 %collective-permute-start.7 = (bf16[128,4096]{1,0:T(8,128)(2,1)S(1)}, bf16[128,4096]{1,0:T(8,128)(2,1)S(1)}, u32[]{:S(2)}, u32[]{:S(2)}) collective-permute-start(bf16[128,4096]{1,0:T(8,128)(2,1)S(1)} %multiply_convert_fusion.refs_2_.a_ref.b_ref), channel_id=1, source_target_pairs={{0,1},{1,0},{2,3},{3,2},{4,5},{5,4},{6,7},{7,6},{8,9},{9,8},{10,11... | collective-permute-start | bytes 3145736 | tf_op jit(solution)/shard_map/ppermute | solution.py:523
  38.2 21.5 %collective-permute-start.6 = (bf16[128,4096]{1,0:T(8,128)(2,1)}, bf16[128,4096]{1,0:T(8,128)(2,1)}, u32[]{:S(2)}, u32[]{:S(2)}) collective-permute-start(bf16[128,4096]{1,0:T(8,128)(2,1)} %choose.4), channel_id=1, source_target_pairs={{1,2},{2,1},{5,6},{6,5},{9,10},{10,9},{13,14},{14,13},{17,18},{18,... | collective-permute-start | bytes 3145736 | tf_op jit(solution)/shard_map/ppermute | solution.py:523
  42.3 10.5 %collective-permute-start.3 = (bf16[256,1280]{1,0:T(8,128)(2,1)}, bf16[256,1280]{1,0:T(8,128)(2,1)S(1)}, u32[]{:S(2)}, u32[]{:S(2)}) collective-permute-start(bf16[256,1280]{1,0:T(8,128)(2,1)} %get-tuple-element.387.kva_ref), channel_id=1, source_target_pairs={{0,4},{4,0},{8,12},{12,8},{1,5},{5,1},{9,13},{13,9},{2,6},{6,2},{1... | collective-permute-start | bytes 1966088 | tf_op jit(solution)/shard_map/ppermute | solution.py:526
  42.4 10.5 %collective-permute-start.4 = (bf16[256,1280]{1,0:T(8,128)(2,1)}, bf16[256,1280]{1,0:T(8,128)(2,1)S(1)}, u32[]{:S(2)}, u32[]{:S(2)}) collective-permute-start(bf16[256,1280]{1,0:T(8,128)(2,1)} %get-tuple-element.388.kvb_ref), channel_id=1, source_target_pairs={{0,4},{4,0},{8,12},{12,8},{1,5},{5,1},{9,13},{13,9},{2,6},{6,2},{1... | collective-permute-start | bytes 1966088 | tf_op jit(solution)/shard_map/ppermute | solution.py:526
  59.7 27.2 %collective-permute-start.8 = (bf16[128,4096]{1,0:T(8,128)(2,1)}, bf16[128,4096]{1,0:T(8,128)(2,1)S(1)}, u32[]{:S(2)}, u32[]{:S(2)}) collective-permute-start(bf16[128,4096]{1,0:T(8,128)(2,1)} %collective-permute-done.6.refs_1_), channel_id=1, source_target_pairs={{1,0},{2,3},{5,4},{6,7},{9,8},{10,11},{13,12},{14,15},{17,16},{18,... | collective-permute-start | bytes 3145736 | tf_op jit(solution)/shard_map/ppermute | solution.py:523
  61.0 26.0 %collective-permute-start.11 = (bf16[128,4096]{1,0:T(8,128)(2,1)}, bf16[128,4096]{1,0:T(8,128)(2,1)S(1)}, u32[]{:S(2)}, u32[]{:S(2)}) collective-permute-start(bf16[128,4096]{1,0:T(8,128)(2,1)} %choose.5), channel_id=1, source_target_pairs={{1,2},{2,1},{5,6},{6,5},{9,10},{10,9},{13,14},{14,13},{17,18},{18,... | collective-permute-start | bytes 3145736 | tf_op jit(solution)/shard_map/ppermute | solution.py:523
  61.7 25.2 %collective-permute-start.5 = (bf16[256,1280]{1,0:T(8,128)(2,1)}, bf16[256,1280]{1,0:T(8,128)(2,1)S(1)}, u32[]{:S(2)}, u32[]{:S(2)}) collective-permute-start(bf16[256,1280]{1,0:T(8,128)(2,1)} %combine.4), channel_id=1, source_target_pairs={{0,8},{4,12},{8,0},{12,4},{1,9},{5,13},{9,1},{13,5},{2,10},{6,14},... | collective-permute-start | bytes 1966088 | tf_op jit(solution)/shard_map/ppermute | solution.py:529
  85.3 7.0 %collective-permute-start.9 = (bf16[256,1280]{1,0:T(8,128)(2,1)}, bf16[256,1280]{1,0:T(8,128)(2,1)S(1)}, u32[]{:S(2)}, u32[]{:S(2)}) collective-permute-start(bf16[256,1280]{1,0:T(8,128)(2,1)} %get-tuple-element.414.kva_ref), channel_id=1, source_target_pairs={{0,4},{4,0},{8,12},{12,8},{1,5},{5,1},{9,13},{13,9},{2,6},{6,2},{1... | collective-permute-start | bytes 1966088 | tf_op jit(solution)/shard_map/ppermute | solution.py:526
  86.9 29.8 %collective-permute-start.14 = (bf16[128,4096]{1,0:T(8,128)(2,1)S(1)}, bf16[128,4096]{1,0:T(8,128)(2,1)}, u32[]{:S(2)}, u32[]{:S(2)}) collective-permute-start(bf16[128,4096]{1,0:T(8,128)(2,1)S(1)} %collective-permute-done.11.refs_2_), channel_id=1, source_target_pairs={{1,0},{2,3},{5,4},{6,7},{9,8},{10,11},{13,12},{14,15},{17,16},{18,... | collective-permute-start | bytes 3145736 | tf_op jit(solution)/shard_map/ppermute | solution.py:523
  90.6 30.5 %collective-permute-start.12 = (bf16[128,4096]{1,0:T(8,128)(2,1)}, bf16[128,4096]{1,0:T(8,128)(2,1)}, u32[]{:S(2)}, u32[]{:S(2)}) collective-permute-start(bf16[128,4096]{1,0:T(8,128)(2,1)} %choose.6), channel_id=1, source_target_pairs={{1,2},{2,1},{5,6},{6,5},{9,10},{10,9},{13,14},{14,13},{17,18},{18,... | collective-permute-start | bytes 3145736 | tf_op jit(solution)/shard_map/ppermute | solution.py:523
  96.3 20.4 %collective-permute-start.13 = (bf16[256,1280]{1,0:T(8,128)(2,1)}, bf16[256,1280]{1,0:T(8,128)(2,1)}, u32[]{:S(2)}, u32[]{:S(2)}) collective-permute-start(bf16[256,1280]{1,0:T(8,128)(2,1)} %combine.5), channel_id=1, source_target_pairs={{0,8},{4,12},{8,0},{12,4},{1,9},{5,13},{9,1},{13,5},{2,10},{6,14},... | collective-permute-start | bytes 1966088 | tf_op jit(solution)/shard_map/ppermute | solution.py:529
  123.6 20.5 %collective-permute-start.15 = (bf16[128,4096]{1,0:T(8,128)(2,1)}, bf16[128,4096]{1,0:T(8,128)(2,1)S(1)}, u32[]{:S(2)}, u32[]{:S(2)}) collective-permute-start(bf16[128,4096]{1,0:T(8,128)(2,1)} %choose.7), channel_id=1, source_target_pairs={{1,2},{2,1},{5,6},{6,5},{9,10},{10,9},{13,14},{14,13},{17,18},{18,... | collective-permute-start | bytes 3145736 | tf_op jit(solution)/shard_map/ppermute | solution.py:523
  124.3 38.8 %collective-permute-start.20 = (bf16[128,4096]{1,0:T(8,128)(2,1)}, bf16[128,4096]{1,0:T(8,128)(2,1)S(1)}, u32[]{:S(2)}, u32[]{:S(2)}) collective-permute-start(bf16[128,4096]{1,0:T(8,128)(2,1)} %collective-permute-done.12.refs_3_), channel_id=1, source_target_pairs={{1,0},{2,3},{5,4},{6,7},{9,8},{10,11},{13,12},{14,15},{17,16},{18,... | collective-permute-start | bytes 3145736 | tf_op jit(solution)/shard_map/ppermute | solution.py:523
  143.5 19.6 %collective-permute-start.19 = (bf16[256,1024]{1,0:T(8,128)(2,1)}, bf16[256,1024]{1,0:T(8,128)(2,1)S(1)}, u32[]{:S(2)}, u32[]{:S(2)}) collective-permute-start(bf16[256,1024]{1,0:T(8,128)(2,1)} %attend.4.refs_1_), channel_id=1, source_target_pairs={{0,8},{4,12},{8,0},{12,4},{1,9},{5,13},{9,1},{13,5},{2,10},{6,14},... | collective-permute-start | bytes 1572872 | tf_op jit(solution)/shard_map/ppermute | solution.py:529
  144.0 21.8 %collective-permute-start.18 = (bf16[256,1024]{1,0:T(8,128)(2,1)}, bf16[256,1024]{1,0:T(8,128)(2,1)}, u32[]{:S(2)}, u32[]{:S(2)}) collective-permute-start(bf16[256,1024]{1,0:T(8,128)(2,1)} %attend.4.refs_1_), channel_id=1, source_target_pairs={{0,4},{4,0},{8,12},{12,8},{1,5},{5,1},{9,13},{13,9},{2,6},{6,2},{1... | collective-permute-start | bytes 1572872 | tf_op jit(solution)/shard_map/ppermute | solution.py:526
  161.8 36.4 %collective-permute-start.16 = (bf16[128,4096]{1,0:T(8,128)(2,1)S(1)}, bf16[128,4096]{1,0:T(8,128)(2,1)}, u32[]{:S(2)}, u32[]{:S(2)}) collective-permute-start(bf16[128,4096]{1,0:T(8,128)(2,1)S(1)} %collective-permute-done.15.refs_4_), channel_id=1, source_target_pairs={{1,0},{2,3},{5,4},{6,7},{9,8},{10,11},{13,12},{14,15},{17,16},{18,... | collective-permute-start | bytes 3145736 | tf_op jit(solution)/shard_map/ppermute | solution.py:523
  163.7 34.0 %collective-permute-start.17 = (bf16[256,1024]{1,0:T(8,128)(2,1)}, bf16[256,1024]{1,0:T(8,128)(2,1)S(1)}, u32[]{:S(2)}, u32[]{:S(2)}) collective-permute-start(bf16[256,1024]{1,0:T(8,128)(2,1)} %attend.5.refs_1_), channel_id=1, source_target_pairs={{0,8},{4,12},{8,0},{12,4},{1,9},{5,13},{9,1},{13,5},{2,10},{6,14},... | collective-permute-start | bytes 1572872 | tf_op jit(solution)/shard_map/ppermute | solution.py:529
  185.3 44.4 %collective-permute-start.26 = (bf16[256,2048]{1,0:T(8,128)(2,1)}, bf16[256,2048]{1,0:T(8,128)(2,1)S(1)}, u32[]{:S(2)}, u32[]{:S(2)}) collective-permute-start(bf16[256,2048]{1,0:T(8,128)(2,1)} %get-tuple-element.510.b_ref), channel_id=1, source_target_pairs={{0,1},{3,2},{4,5},{7,6},{8,9},{11,10},{12,13},{15,14},{16,17},{19,... | collective-permute-start | bytes 3145736 | tf_op jit(solution)/shard_map/ppermute | solution.py:523
  197.6 30.3 %collective-permute-start.27 = (bf16[256,1024]{1,0:T(8,128)(2,1)S(1)}, bf16[256,1024]{1,0:T(8,128)(2,1)S(1)}, u32[]{:S(2)}, u32[]{:S(2)}) collective-permute-start(bf16[256,1024]{1,0:T(8,128)(2,1)S(1)} %copy-done.14), channel_id=1, source_target_pairs={{0,4},{4,0},{8,12},{12,8},{1,5},{5,1},{9,13},{13,9},{2,6},{6,2},{1... | collective-permute-start | bytes 1572872 | tf_op jit(solution)/shard_map/ppermute | solution.py:526
  197.7 31.8 %collective-permute-start.28 = (bf16[256,1024]{1,0:T(8,128)(2,1)S(1)}, bf16[256,1024]{1,0:T(8,128)(2,1)S(1)}, u32[]{:S(2)}, u32[]{:S(2)}) collective-permute-start(bf16[256,1024]{1,0:T(8,128)(2,1)S(1)} %collective-permute-done.17.refs_3_), channel_id=1, source_target_pairs={{0,4},{4,0},{8,12},{12,8},{1,5},{5,1},{9,13},{13,9},{2,6},{6,2},{1... | collective-permute-start | bytes 1572872 | tf_op jit(solution)/shard_map/ppermute | solution.py:526
  227.9 25.4 %collective-permute-start.30 = (bf16[256,2048]{1,0:T(8,128)(2,1)S(1)}, bf16[256,2048]{1,0:T(8,128)(2,1)S(1)}, u32[]{:S(2)}, u32[]{:S(2)}) collective-permute-start(bf16[256,2048]{1,0:T(8,128)(2,1)S(1)} %copy-done.2), channel_id=1, source_target_pairs={{0,1},{3,2},{4,5},{7,6},{8,9},{11,10},{12,13},{15,14},{16,17},{19,... | collective-permute-start | bytes 3145736 | tf_op jit(solution)/shard_map/ppermute | solution.py:523
  234.1 19.2 %collective-permute-start.29 = (bf16[256,1280]{1,0:T(8,128)(2,1)}, bf16[256,1280]{1,0:T(8,128)(2,1)S(1)}, u32[]{:S(2)}, u32[]{:S(2)}) collective-permute-start(bf16[256,1280]{1,0:T(8,128)(2,1)} %combine.6), channel_id=1, source_target_pairs={{0,8},{4,12},{8,0},{12,4},{1,9},{5,13},{9,1},{13,5},{2,10},{6,14},... | collective-permute-start | bytes 1966088 | tf_op jit(solution)/shard_map/ppermute | solution.py:529
  239.0 37.1 %collective-permute-start.33 = (bf16[256,1280]{1,0:T(8,128)(2,1)}, bf16[256,1280]{1,0:T(8,128)(2,1)S(1)}, u32[]{:S(2)}, u32[]{:S(2)}) collective-permute-start(bf16[256,1280]{1,0:T(8,128)(2,1)} %combine.7), channel_id=1, source_target_pairs={{0,8},{4,12},{8,0},{12,4},{1,9},{5,13},{9,1},{13,5},{2,10},{6,14},... | collective-permute-start | bytes 1966088 | tf_op jit(solution)/shard_map/ppermute | solution.py:529
  275.3 22.8 %collective-permute-start.32 = (bf16[256,1024]{1,0:T(8,128)(2,1)}, bf16[256,1024]{1,0:T(8,128)(2,1)S(1)}, u32[]{:S(2)}, u32[]{:S(2)}) collective-permute-start(bf16[256,1024]{1,0:T(8,128)(2,1)} %attend.6.refs_1_), channel_id=1, source_target_pairs={{0,8},{4,12},{8,0},{12,4},{1,9},{5,13},{9,1},{13,5},{2,10},{6,14},... | collective-permute-start | bytes 1572872 | tf_op jit(solution)/shard_map/ppermute | solution.py:529
  276.1 23.6 %collective-permute-start.31 = (bf16[256,1024]{1,0:T(8,128)(2,1)}, bf16[256,1024]{1,0:T(8,128)(2,1)S(1)}, u32[]{:S(2)}, u32[]{:S(2)}) collective-permute-start(bf16[256,1024]{1,0:T(8,128)(2,1)} %attend.6.refs_1_), channel_id=1, source_target_pairs={{0,4},{4,0},{8,12},{12,8},{1,5},{5,1},{9,13},{13,9},{2,6},{6,2},{1... | collective-permute-start | bytes 1572872 | tf_op jit(solution)/shard_map/ppermute | solution.py:526
  298.6 22.5 %collective-permute-start.39 = (bf16[256,1024]{1,0:T(8,128)(2,1)}, bf16[256,1024]{1,0:T(8,128)(2,1)S(1)}, u32[]{:S(2)}, u32[]{:S(2)}) collective-permute-start(bf16[256,1024]{1,0:T(8,128)(2,1)} %attend.7.refs_1_), channel_id=1, source_target_pairs={{0,8},{4,12},{8,0},{12,4},{1,9},{5,13},{9,1},{13,5},{2,10},{6,14},... | collective-permute-start | bytes 1572872 | tf_op jit(solution)/shard_map/ppermute | solution.py:529
  299.8 27.7 %collective-permute-start.38 = (bf16[256,1024]{1,0:T(8,128)(2,1)}, bf16[256,1024]{1,0:T(8,128)(2,1)S(1)}, u32[]{:S(2)}, u32[]{:S(2)}) collective-permute-start(bf16[256,1024]{1,0:T(8,128)(2,1)} %attend.7.refs_1_), channel_id=1, source_target_pairs={{0,4},{4,0},{8,12},{12,8},{1,5},{5,1},{9,13},{13,9},{2,6},{6,2},{1... | collective-permute-start | bytes 1572872 | tf_op jit(solution)/shard_map/ppermute | solution.py:526
  321.6 29.4 %collective-permute-start.37 = (bf16[256,1024]{1,0:T(8,128)(2,1)}, bf16[256,1024]{1,0:T(8,128)(2,1)S(1)}, u32[]{:S(2)}, u32[]{:S(2)}) collective-permute-start(bf16[256,1024]{1,0:T(8,128)(2,1)} %get-tuple-element.578.b_ref), channel_id=1, source_target_pairs={{0,1},{3,2},{4,5},{7,6},{8,9},{11,10},{12,13},{15,14},{16,17},{19,... | collective-permute-start | bytes 1572872 | tf_op jit(solution)/shard_map/ppermute | solution.py:523
  324.8 29.8 %collective-permute-start.36 = (bf16[256,1024]{1,0:T(8,128)(2,1)}, bf16[256,1024]{1,0:T(8,128)(2,1)S(1)}, u32[]{:S(2)}, u32[]{:S(2)}) collective-permute-start(bf16[256,1024]{1,0:T(8,128)(2,1)} %get-tuple-element.577.b_ref), channel_id=1, source_target_pairs={{0,1},{3,2},{4,5},{7,6},{8,9},{11,10},{12,13},{15,14},{16,17},{19,... | collective-permute-start | bytes 1572872 | tf_op jit(solution)/shard_map/ppermute | solution.py:523
  326.2 33.7 %collective-permute-start.35 = (bf16[256,1024]{1,0:T(8,128)(2,1)}, bf16[256,1024]{1,0:T(8,128)(2,1)S(1)}, u32[]{:S(2)}, u32[]{:S(2)}) collective-permute-start(bf16[256,1024]{1,0:T(8,128)(2,1)} %get-tuple-element.576.b_ref), channel_id=1, source_target_pairs={{0,1},{3,2},{4,5},{7,6},{8,9},{11,10},{12,13},{15,14},{16,17},{19,... | collective-permute-start | bytes 1572872 | tf_op jit(solution)/shard_map/ppermute | solution.py:523
  348.3 62.7 %collective-permute-start.47 = (bf16[256,2048]{1,0:T(8,128)(2,1)}, bf16[256,2048]{1,0:T(8,128)(2,1)S(1)}, u32[]{:S(2)}, u32[]{:S(2)}) collective-permute-start(bf16[256,2048]{1,0:T(8,128)(2,1)} %get-tuple-element.621.b_ref), channel_id=1, source_target_pairs={{0,1},{3,2},{4,5},{7,6},{8,9},{11,10},{12,13},{15,14},{16,17},{19,... | collective-permute-start | bytes 3145736 | tf_op jit(solution)/shard_map/ppermute | solution.py:523
  349.7 43.0 %collective-permute-start.44 = (bf16[256,1024]{1,0:T(8,128)(2,1)S(1)}, bf16[256,1024]{1,0:T(8,128)(2,1)S(1)}, u32[]{:S(2)}, u32[]{:S(2)}) collective-permute-start(bf16[256,1024]{1,0:T(8,128)(2,1)S(1)} %copy-done.51), channel_id=1, source_target_pairs={{0,1},{3,2},{4,5},{7,6},{8,9},{11,10},{12,13},{15,14},{16,17},{19,... | collective-permute-start | bytes 1572872 | tf_op jit(solution)/shard_map/ppermute | solution.py:523
  354.0 43.0 %collective-permute-start.43 = (bf16[256,1024]{1,0:T(8,128)(2,1)}, bf16[256,1024]{1,0:T(8,128)(2,1)S(1)}, u32[]{:S(2)}, u32[]{:S(2)}) collective-permute-start(bf16[256,1024]{1,0:T(8,128)(2,1)} %add.209), channel_id=1, source_target_pairs={{1,2},{2,1},{5,6},{6,5},{9,10},{10,9},{13,14},{14,13},{17,18},{18,... | collective-permute-start | bytes 1572872 | tf_op jit(solution)/shard_map/ppermute | solution.py:523
  357.6 50.4 %collective-permute-start.42 = (bf16[256,1024]{1,0:T(8,128)(2,1)}, bf16[256,1024]{1,0:T(8,128)(2,1)S(1)}, u32[]{:S(2)}, u32[]{:S(2)}) collective-permute-start(bf16[256,1024]{1,0:T(8,128)(2,1)} %add.210), channel_id=1, source_target_pairs={{1,2},{2,1},{5,6},{6,5},{9,10},{10,9},{13,14},{14,13},{17,18},{18,... | collective-permute-start | bytes 1572872 | tf_op jit(solution)/shard_map/ppermute | solution.py:523
  395.6 22.1 %collective-permute-start.50 = (bf16[256,1024]{1,0:T(8,128)(2,1)}, bf16[256,1024]{1,0:T(8,128)(2,1)S(1)}, u32[]{:S(2)}, u32[]{:S(2)}) collective-permute-start(bf16[256,1024]{1,0:T(8,128)(2,1)} %add.212), channel_id=1, source_target_pairs={{1,2},{2,1},{5,6},{6,5},{9,10},{10,9},{13,14},{14,13},{17,18},{18,... | collective-permute-start | bytes 1572872 | tf_op jit(solution)/shard_map/ppermute | solution.py:523
  396.3 22.9 %collective-permute-start.51 = (bf16[256,1024]{1,0:T(8,128)(2,1)S(1)}, bf16[256,1024]{1,0:T(8,128)(2,1)S(1)}, u32[]{:S(2)}, u32[]{:S(2)}) collective-permute-start(bf16[256,1024]{1,0:T(8,128)(2,1)S(1)} %copy-done.52), channel_id=1, source_target_pairs={{1,2},{2,1},{5,6},{6,5},{9,10},{10,9},{13,14},{14,13},{17,18},{18,... | collective-permute-start | bytes 1572872 | tf_op jit(solution)/shard_map/ppermute | solution.py:523
  397.0 34.0 %collective-permute-start.41 = (bf16[256,2048]{1,0:T(8,128)(2,1)S(1)}, bf16[256,2048]{1,0:T(8,128)(2,1)S(1)}, u32[]{:S(2)}, u32[]{:S(2)}) collective-permute-start(bf16[256,2048]{1,0:T(8,128)(2,1)S(1)} %copy-done.15), channel_id=1, source_target_pairs={{0,1},{3,2},{4,5},{7,6},{8,9},{11,10},{12,13},{15,14},{16,17},{19,... | collective-permute-start | bytes 3145736 | tf_op jit(solution)/shard_map/ppermute | solution.py:523
  414.2 10.1 %collective-permute-start.49 = (bf16[256,1024]{1,0:T(8,128)(2,1)}, bf16[256,1024]{1,0:T(8,128)(2,1)S(1)}, u32[]{:S(2)}, u32[]{:S(2)}) collective-permute-start(bf16[256,1024]{1,0:T(8,128)(2,1)} %add.215), channel_id=1, source_target_pairs={{1,2},{2,1},{5,6},{6,5},{9,10},{10,9},{13,14},{14,13},{17,18},{18,... | collective-permute-start | bytes 1572872 | tf_op jit(solution)/shard_map/ppermute | solution.py:523
  417.0 11.0 %collective-permute-start.48 = (bf16[256,1024]{1,0:T(8,128)(2,1)}, bf16[256,1024]{1,0:T(8,128)(2,1)S(1)}, u32[]{:S(2)}, u32[]{:S(2)}) collective-permute-start(bf16[256,1024]{1,0:T(8,128)(2,1)} %add.216), channel_id=1, source_target_pairs={{1,2},{2,1},{5,6},{6,5},{9,10},{10,9},{13,14},{14,13},{17,18},{18,... | collective-permute-start | bytes 1572872 | tf_op jit(solution)/shard_map/ppermute | solution.py:523
  417.7 13.3 %collective-permute-start.46 = (bf16[256,1024]{1,0:T(8,128)(2,1)S(1)}, bf16[256,1024]{1,0:T(8,128)(2,1)}, u32[]{:S(2)}, u32[]{:S(2)}) collective-permute-start(bf16[256,1024]{1,0:T(8,128)(2,1)S(1)} %copy-done.59), channel_id=1, source_target_pairs={{1,0},{5,4},{9,8},{13,12},{17,16},{21,20},{25,24},{29,28}} | collective-permute-start | bytes 1572872 | tf_op jit(solution)/shard_map/ppermute | solution.py:523
  419.2 11.8 %collective-permute-start.45 = (bf16[256,1024]{1,0:T(8,128)(2,1)S(1)}, bf16[256,1024]{1,0:T(8,128)(2,1)S(1)}, u32[]{:S(2)}, u32[]{:S(2)}) collective-permute-start(bf16[256,1024]{1,0:T(8,128)(2,1)S(1)} %copy-done.60), channel_id=1, source_target_pairs={{1,0},{5,4},{9,8},{13,12},{17,16},{21,20},{25,24},{29,28}} | collective-permute-start | bytes 1572872 | tf_op jit(solution)/shard_map/ppermute | solution.py:523
  424.3 14.3 %collective-permute-start.55 = (bf16[256,1024]{1,0:T(8,128)(2,1)}, bf16[256,1024]{1,0:T(8,128)(2,1)}, u32[]{:S(2)}, u32[]{:S(2)}) collective-permute-start(bf16[256,1024]{1,0:T(8,128)(2,1)} %add.217), channel_id=1, source_target_pairs={{1,0},{5,4},{9,8},{13,12},{17,16},{21,20},{25,24},{29,28}} | collective-permute-start | bytes 1572872 | tf_op jit(solution)/shard_map/ppermute | solution.py:523
  435.0 9.1 %collective-permute-start.53 = (bf16[256,1024]{1,0:T(8,128)(2,1)S(1)}, bf16[256,1024]{1,0:T(8,128)(2,1)S(1)}, u32[]{:S(2)}, u32[]{:S(2)}) collective-permute-start(bf16[256,1024]{1,0:T(8,128)(2,1)S(1)} %copy-done.58), channel_id=1, source_target_pairs={{1,0},{5,4},{9,8},{13,12},{17,16},{21,20},{25,24},{29,28}} | collective-permute-start | bytes 1572872 | tf_op jit(solution)/shard_map/ppermute | solution.py:523
  438.5 38.3 %collective-permute-start.56 = (bf16[256,1024]{1,0:T(8,128)(2,1)S(1)}, bf16[256,1024]{1,0:T(8,128)(2,1)}, u32[]{:S(2)}, u32[]{:S(2)}) collective-permute-start(bf16[256,1024]{1,0:T(8,128)(2,1)S(1)} %copy-done.57), channel_id=1, source_target_pairs={{2,3},{6,7},{10,11},{14,15},{18,19},{22,23},{26,27},{30,31}} | collective-permute-start | bytes 1572872 | tf_op jit(solution)/shard_map/ppermute | solution.py:523
  439.8 48.3 %collective-permute-start.57 = (bf16[256,1024]{1,0:T(8,128)(2,1)}, bf16[256,1024]{1,0:T(8,128)(2,1)}, u32[]{:S(2)}, u32[]{:S(2)}) collective-permute-start(bf16[256,1024]{1,0:T(8,128)(2,1)} %add.220), channel_id=1, source_target_pairs={{2,3},{6,7},{10,11},{14,15},{18,19},{22,23},{26,27},{30,31}} | collective-permute-start | bytes 1572872 | tf_op jit(solution)/shard_map/ppermute | solution.py:523
  447.0 52.3 %collective-permute-start.58 = (bf16[256,1024]{1,0:T(8,128)(2,1)}, bf16[256,1024]{1,0:T(8,128)(2,1)}, u32[]{:S(2)}, u32[]{:S(2)}) collective-permute-start(bf16[256,1024]{1,0:T(8,128)(2,1)} %add.223), channel_id=1, source_target_pairs={{2,3},{6,7},{10,11},{14,15},{18,19},{22,23},{26,27},{30,31}} | collective-permute-start | bytes 1572872 | tf_op jit(solution)/shard_map/ppermute | solution.py:523
  448.4 59.2 %collective-permute-start.59 = (bf16[256,1024]{1,0:T(8,128)(2,1)}, bf16[256,1024]{1,0:T(8,128)(2,1)}, u32[]{:S(2)}, u32[]{:S(2)}) collective-permute-start(bf16[256,1024]{1,0:T(8,128)(2,1)} %add.224), channel_id=1, source_target_pairs={{2,3},{6,7},{10,11},{14,15},{18,19},{22,23},{26,27},{30,31}} | collective-permute-start | bytes 1572872 | tf_op jit(solution)/shard_map/ppermute | solution.py:523
  (78 other events, 792.2 us)

commit v3 on v2

--- a/solution.py
+++ b/solution.py
@@ -701,7 +701,7 @@
     att_bc, att_bd = wait((att_bc, att_bd))
     part_b = do(
         lambda a: out_project(
-            spots, [a, att_bc, att_bx, att_bd], out_weight, None, 0, width, BF16, pieces
+            spots, [a, att_bc, att_bx, att_bd], out_weight, None, 0, width, BF16, 2
         ),
         att_b,
     )
@@ -719,8 +719,8 @@
     b2, b3, c2, c3 = [], [], [], []
 
     def pass_b1(i):
-        b1[i] = wait(b1[i])
-        b2.append(along(do(add, b1[i], part_b[i]), middle))
+        b1[i // 2] = wait(b1[i // 2])
+        b2.append(along(do(add, b1[i // 2], part_b[i // 2], i % 2, 2), middle))
 
     def pass_b2(i):
         b2[i] = wait(b2[i])
@@ -736,8 +736,8 @@
 
     pass_b1(0)
     pass_b1(1)
+    part_o += output_own(1)
     pass_b1(2)
-    part_o += output_own(1)
     pass_b1(3)
     pass_b2(0)
     pass_b2(1)

time: 517 us -> 497 us (0.961)
  waiting for transfers between devices: 94.3 us -> 76.7 us
    ppermute x34 -> x32, waiting for transfers between devices: 90.8 us -> 72.4 us  [along(): return lax.ppermute(x, 'gy', pairs)]
    unnamed x133 -> x127, local copies, waits for them, and re-layouts: 20.9 us -> 18.6 us
    ppermute x34 -> x32, starting transfers between devices: 58.7 us -> 57.1 us  [along(): return lax.ppermute(x, 'gy', pairs)]
  transfers between devices with their start and end apart: 60 -> 58, of which waited for: 13 -> 15; matrix products, arithmetic and copies ran while one was open for 3% -> 3% of each run, Pallas kernels for 57% -> 60%
where the time goes in v3:
time: 497 us; the launch traced here: 489 us
  Pallas kernels  295 us (59%)
  waiting for transfers between devices  76.7 us (15%)
  starting transfers between devices  72.4 us (15%)
  local copies, waits for them, and re-layouts  26 us (5%)
  other arithmetic  15.9 us (3%)
    pallas_call x5, Pallas kernels, out_project(): pl.pallas_call(lambda *refs: out_kernel(*refs, sources=n, before=before i...  84.1 us
    pallas_call x3, Pallas kernels, project(): pl.pallas_call(lambda *refs: project_kernel(*refs, pieces=pieces, sources...  73.2 us
    ppermute x32, waiting for transfers between devices, along(): return lax.ppermute(x, 'gy', pairs)  72.4 us
    pallas_call x4, Pallas kernels, attend(): pl.pallas_call(lambda *refs: attend_kernel(*refs, at=at), grid_spec=pltpu...  71.9 us
    ppermute x32, starting transfers between devices, along(): return lax.ppermute(x, 'gy', pairs)  57.1 us
    pallas_call x16, Pallas kernels, add(): pl.pallas_call(add_kernel, grid=(1,), in_specs=[block if cuts == 1 else t...  33.9 us
    unnamed x127, local copies, waits for them, and re-layouts  18.6 us
    pallas_call x4, Pallas kernels, finish(): pl.pallas_call(finish_kernel, grid_spec=pltpu.PrefetchScalarGridSpec(num_...  11.1 us
  transfers between devices with their start and end apart: 58, of which 15 were waited for; matrix products, arithmetic and copies ran while one was open for 3% of the time, Pallas kernels for 60%

profile of v3, /device:TPU:28, one launch (start us, length us, event | category | flops | bytes accessed | tf_op | source)
XLA Modules:
  0.0 489.1 jit_solution(15360998196401330340)
XLA Ops:
  0.0 2.2 multiply_reduce_fusion
  11.8 22.0 %project.3 = (bf16[256,1280]{1,0:T(8,128)(2,1)}, bf16[256,1280]{1,0:T(8,128)(2,1)}, f32[256,2048]{1,0:T(8,128)}) custom-call(s32[19]{0:T(128)} %pad_add_fusion.1.refs_0_, bf16[128,4096]{1,0:T(8,128)(2,1)} %copy-done.1, bf16[128,4096]{1,0:T(8,128)(2,1)} %copy-done, bf16[4096,4608]{1,0:T(8,128)(2,1)} %refs_10_.1, bf16[4096,4608]{1,0:T(8,128)(2,1)} %refs_10_.1), custom_call_target="tpu_custom_call" | custom-call | flops 1024 | bytes 1024 | tf_op jit(solution)/shard_map/project/pallas_call | solution.py:105
  35.8 2.4 choose.4
  43.6 3.0 fusion
  47.3 5.5 %stack.61.refs_0_ = s32[20]{0:T(128)} concatenate(s32[1]{0:T(128)} %bitcast.4, s32[1]{0:T(128)} %bitcast.5.s_ref, s32[1]{0:T(128)} %get-tuple-element.703, s32[1]{0:T(128)} %get-tuple-element.698, s32[1]{0:T(128)} %bitcast.14, s32[1]{0:T(128)} %bitcast.4, s32[1]{0:T(128)} %bitcast.5.s_ref, s32[1]{0:T(128)} %get-tuple-element.703, s32[1]{0:T(128)} %get-tuple-element.698, ...), dimensions={0} | concatenate | bytes 160 | tf_op jit(solution)/shard_map/stack | solution.py:574
  53.9 2.3 combine.4
  57.2 2.4 choose.5
  63.2 22.1 %project.4 = (bf16[256,1280]{1,0:T(8,128)(2,1)}, bf16[256,1280]{1,0:T(8,128)(2,1)}, f32[256,2048]{1,0:T(8,128)}) custom-call(s32[19]{0:T(128)} %pad_add_fusion.1.refs_0_, bf16[128,4096]{1,0:T(8,128)(2,1)} %copy-done.12, bf16[128,4096]{1,0:T(8,128)(2,1)} %copy-done.11, bf16[4096,4608]{1,0:T(8,128)(2,1)} %refs_10_.1, bf16[4096,4608]{1,0:T(8,128)(2,1)} %refs_10_.1), custom_call_target="tpu_custom_call" | custom-call | flops 1024 | bytes 1024 | tf_op jit(solution)/shard_map/project/pallas_call | solution.py:105
  88.2 2.4 choose.6
  94.0 2.3 combine.5
  97.8 2.8 finish.4
  100.6 16.1 %collective-permute-done.14.refs_6_ = bf16[128,4096]{1,0:T(8,128)(2,1)} collective-permute-done((bf16[128,4096]{1,0:T(8,128)(2,1)S(1)}, bf16[128,4096]{1,0:T(8,128)(2,1)}, u32[]{:S(2)}, u32[]{:S(2)}) %collective-permute-start.14) | collective-permute-done | bytes 1048608 | tf_op jit(solution)/shard_map/ppermute | solution.py:523
  116.7 2.8 finish.5
  121.1 2.4 choose.7
  125.7 18.3 %attend.4.refs_1_ = bf16[256,1024]{1,0:T(8,128)(2,1)} custom-call(s32[20]{0:T(128)} %stack.61.refs_0_, bf16[2048,128]{1,0:T(8,128)(2,1)} %bitcast.31, bf16[2,3072,256]{2,1,0:T(8,128)(2,1)} %refs_2_.7, bf16[2,3072,256]{2,1,0:T(8,128)(2,1)} %refs_3_.11, bf16[256,128]{1,0:T(8,128)(2,1)} %get-tuple-element.463.refs_4_, ...), custom_call_target="tpu_custom_call" | custom-call | flops 1024 | bytes 1024 | tf_op jit(solution)/shard_map/attend/pallas_call | solution.py:336
  144.5 18.2 %attend.5.refs_1_ = bf16[256,1024]{1,0:T(8,128)(2,1)} custom-call(s32[20]{0:T(128)} %stack.61.refs_0_, bf16[2048,128]{1,0:T(8,128)(2,1)} %bitcast.30, bf16[2,3072,256]{2,1,0:T(8,128)(2,1)} %refs_2_.7, bf16[2,3072,256]{2,1,0:T(8,128)(2,1)} %refs_3_.11, bf16[256,128]{1,0:T(8,128)(2,1)} %get-tuple-element.463.refs_4_, ...), custom_call_target="tpu_custom_call" | custom-call | flops 1024 | bytes 1024 | tf_op jit(solution)/shard_map/attend/pallas_call | solution.py:336
  166.8 19.3 %out_project.5 = (bf16[256,2048]{1,0:T(8,128)(2,1)}, bf16[256,2048]{1,0:T(8,128)(2,1)}) custom-call(s32[5]{0:T(128)} %stack.52.refs_0_, bf16[256,1024]{1,0:T(8,128)(2,1)} %attend.4.refs_1_, bf16[256,1024]{1,0:T(8,128)(2,1)} %collective-permute-done.18.refs_2_, bf16[256,1024]{1,0:T(8,128)(2,1)} %copy-done.47, ...), custom_call_target="tpu_custom_call" | custom-call | flops 1024 | bytes 1024 | tf_op jit(solution)/shard_map/out_project/pallas_call | solution.py:406
  186.2 11.7 %collective-permute-start.26 = (bf16[256,2048]{1,0:T(8,128)(2,1)}, bf16[256,2048]{1,0:T(8,128)(2,1)S(1)}, u32[]{:S(2)}, u32[]{:S(2)}) collective-permute-start(bf16[256,2048]{1,0:T(8,128)(2,1)} %get-tuple-element.508.b_ref), channel_id=1, source_target_pairs={{0,1},{3,2},{4,5},{7,6},{8,9},{11,10},{12,13},{15,14},{16,17},{19,... | collective-permute-start | bytes 3145736 | tf_op jit(solution)/shard_map/ppermute | solution.py:523
  198.6 29.1 %project.5 = (bf16[256,1280]{1,0:T(8,128)(2,1)}, bf16[256,1280]{1,0:T(8,128)(2,1)}, f32[256,2048]{1,0:T(8,128)}, bf16[256,1280]{1,0:T(8,128)(2,1)}, bf16[256,1280]{1,0:T(8,128)(2,1)}, /*index=5*/f32[256,2048]{1,0:T(8,128)}) custom-call(s32[19]{0:T(128)} %pad_add_fusion.1.refs_0_, bf16[128,4096]{1,0:T(8,128)(2,1)} %collective-permute-done.6.refs_1_, ...), custom_call_target="tpu_custom_call" | custom-call | flops 1024 | bytes 1024 | tf_op jit(solution)/shard_map/project/pallas_call | solution.py:105
  232.2 2.3 combine.6
  237.1 2.3 combine.7
  240.5 13.1 %out_project.6 = (bf16[256,1024]{1,0:T(8,128)(2,1)}, bf16[256,1024]{1,0:T(8,128)(2,1)}) custom-call(s32[5]{0:T(128)} %stack.52.refs_0_, bf16[256,1024]{1,0:T(8,128)(2,1)} %attend.5.refs_1_, bf16[256,1024]{1,0:T(8,128)(2,1)} %copy-done.21, bf16[256,1024]{1,0:T(8,128)(2,1)} %copy-done.20, bf16[256,1024]{1,0:T(8,128)(2,1)} %copy-done.22, bf16[4096,4096]{1,0:T(8,128)(2,1)} %refs_5_.9), custom_call_target="tpu_custom_call" | custom-call | flops 1024 | bytes 1024 | tf_op jit(solution)/shard_map/out_project/pallas_call | solution.py:406
  254.5 2.8 finish.6
  257.3 17.7 %attend.6.refs_1_ = bf16[256,1024]{1,0:T(8,128)(2,1)} custom-call(s32[20]{0:T(128)} %stack.61.refs_0_, bf16[2048,128]{1,0:T(8,128)(2,1)} %bitcast.33, bf16[2,3072,256]{2,1,0:T(8,128)(2,1)} %refs_2_.7, bf16[2,3072,256]{2,1,0:T(8,128)(2,1)} %refs_3_.11, bf16[256,128]{1,0:T(8,128)(2,1)} %get-tuple-element.543.refs_4_.refs_5_, ...), custom_call_target="tpu_custom_call" | custom-call | flops 1024 | bytes 1024 | tf_op jit(solution)/shard_map/attend/pallas_call | solution.py:336
  276.7 2.8 finish.7
  279.5 17.7 %attend.7.refs_1_ = bf16[256,1024]{1,0:T(8,128)(2,1)} custom-call(s32[20]{0:T(128)} %stack.61.refs_0_, bf16[2048,128]{1,0:T(8,128)(2,1)} %bitcast.32, bf16[2,3072,256]{2,1,0:T(8,128)(2,1)} %refs_2_.7, bf16[2,3072,256]{2,1,0:T(8,128)(2,1)} %refs_3_.11, bf16[256,128]{1,0:T(8,128)(2,1)} %get-tuple-element.543.refs_4_.refs_5_, ...), custom_call_target="tpu_custom_call" | custom-call | flops 1024 | bytes 1024 | tf_op jit(solution)/shard_map/attend/pallas_call | solution.py:336
  300.5 19.5 %out_project.7 = (bf16[256,2048]{1,0:T(8,128)(2,1)}, bf16[256,2048]{1,0:T(8,128)(2,1)}) custom-call(s32[5]{0:T(128)} %stack.52.refs_0_, bf16[256,1024]{1,0:T(8,128)(2,1)} %attend.6.refs_1_, bf16[256,1024]{1,0:T(8,128)(2,1)} %copy-done.49, bf16[256,1024]{1,0:T(8,128)(2,1)} %copy-done.48, bf16[256,1024]{1,0:T(8,128)(2,1)} %copy-done.52, bf16[4096,4096]{1,0:T(8,128)(2,1)} %refs_5_.9), custom_call_target="tpu_custom_call" | custom-call | flops 1024 | bytes 1024 | tf_op jit(solution)/shard_map/out_project/pallas_call | solution.py:406
  320.0 3.4 collective-permute-start.35
  326.9 19.2 %out_project.8 = (bf16[256,2048]{1,0:T(8,128)(2,1)}, bf16[256,2048]{1,0:T(8,128)(2,1)}) custom-call(s32[5]{0:T(128)} %stack.52.refs_0_, bf16[256,1024]{1,0:T(8,128)(2,1)} %attend.7.refs_1_, bf16[256,1024]{1,0:T(8,128)(2,1)} %copy-done.51, bf16[256,1024]{1,0:T(8,128)(2,1)} %copy-done.50, bf16[256,1024]{1,0:T(8,128)(2,1)} %copy-done.53, bf16[4096,4096]{1,0:T(8,128)(2,1)} %refs_5_.9), custom_call_target="tpu_custom_call" | custom-call | flops 1024 | bytes 1024 | tf_op jit(solution)/shard_map/out_project/pallas_call | solution.py:406
  351.3 2.1 add.210
  354.1 13.0 %out_project.9 = (bf16[256,1024]{1,0:T(8,128)(2,1)}, bf16[256,1024]{1,0:T(8,128)(2,1)}) custom-call(s32[5]{0:T(128)} %stack.52.refs_0_, bf16[256,1024]{1,0:T(8,128)(2,1)} %attend.5.refs_1_, bf16[256,1024]{1,0:T(8,128)(2,1)} %copy-done.21, bf16[256,1024]{1,0:T(8,128)(2,1)} %copy-done.20, bf16[256,1024]{1,0:T(8,128)(2,1)} %copy-done.22, bf16[4096,4096]{1,0:T(8,128)(2,1)} %refs_5_.9), custom_call_target="tpu_custom_call" | custom-call | flops 1024 | bytes 1024 | tf_op jit(solution)/shard_map/out_project/pallas_call | solution.py:406
  367.1 2.5 collective-permute-done.42.a_ref
  370.6 2.1 add.211
  376.3 10.4 %collective-permute-start.39 = (bf16[256,2048]{1,0:T(8,128)(2,1)S(1)}, bf16[256,2048]{1,0:T(8,128)(2,1)S(1)}, u32[]{:S(2)}, u32[]{:S(2)}) collective-permute-start(bf16[256,2048]{1,0:T(8,128)(2,1)S(1)} %copy-done.15), channel_id=1, source_target_pairs={{0,1},{3,2},{4,5},{7,6},{8,9},{11,10},{12,13},{15,14},{16,17},{19,... | collective-permute-start | bytes 3145736 | tf_op jit(solution)/shard_map/ppermute | solution.py:523
  386.7 2.1 add.213
  389.6 2.1 add.214
  395.9 2.1 add.216
  400.9 2.1 add.217
  403.1 2.1 add.218
  406.8 2.1 add.219
  409.7 2.1 add.220
  418.0 2.1 add.222
  432.1 3.3 add_convert_fusion.1
  435.4 21.8 %collective-permute-done.54 = bf16[256,1024]{1,0:T(8,128)(2,1)} collective-permute-done((bf16[256,1024]{1,0:T(8,128)(2,1)S(1)}, bf16[256,1024]{1,0:T(8,128)(2,1)}, u32[]{:S(2)}, u32[]{:S(2)}) %collective-permute-start.54) | collective-permute-done | bytes 524320 | tf_op jit(solution)/shard_map/ppermute | solution.py:523
  457.2 10.4 %collective-permute-done.55 = bf16[256,1024]{1,0:T(8,128)(2,1)} collective-permute-done((bf16[256,1024]{1,0:T(8,128)(2,1)}, bf16[256,1024]{1,0:T(8,128)(2,1)}, u32[]{:S(2)}, u32[]{:S(2)}) %collective-permute-start.55) | collective-permute-done | bytes 524320 | tf_op jit(solution)/shard_map/ppermute | solution.py:523
  467.6 11.2 %collective-permute-done.56 = bf16[256,1024]{1,0:T(8,128)(2,1)} collective-permute-done((bf16[256,1024]{1,0:T(8,128)(2,1)}, bf16[256,1024]{1,0:T(8,128)(2,1)}, u32[]{:S(2)}, u32[]{:S(2)}) %collective-permute-start.56) | collective-permute-done | bytes 524320 | tf_op jit(solution)/shard_map/ppermute | solution.py:523
  478.8 6.4 %collective-permute-done.57 = bf16[256,1024]{1,0:T(8,128)(2,1)} collective-permute-done((bf16[256,1024]{1,0:T(8,128)(2,1)}, bf16[256,1024]{1,0:T(8,128)(2,1)}, u32[]{:S(2)}, u32[]{:S(2)}) %collective-permute-start.57) | collective-permute-done | bytes 524320 | tf_op jit(solution)/shard_map/ppermute | solution.py:523
  485.3 3.3 add_convert_fusion
  (256 shorter events, 94.1 us)
Async XLA Ops:
  8.6 26.2 %collective-permute-start.2 = (bf16[128,4096]{1,0:T(8,128)(2,1)S(1)}, bf16[128,4096]{1,0:T(8,128)(2,1)S(1)}, u32[]{:S(2)}, u32[]{:S(2)}) collective-permute-start(bf16[128,4096]{1,0:T(8,128)(2,1)S(1)} %multiply_convert_fusion.1.refs_1_.a_ref.b_ref), channel_id=1, source_target_pairs={{0,1},{1,0},{2,3},{3,2},{4,5},{5,4},{6,7},{7,6},{8,9},{9,8},{10,11... | collective-permute-start | bytes 3145736 | tf_op jit(solution)/shard_map/ppermute | solution.py:523
  10.1 46.1 %collective-permute-start.7 = (bf16[128,4096]{1,0:T(8,128)(2,1)S(1)}, bf16[128,4096]{1,0:T(8,128)(2,1)S(1)}, u32[]{:S(2)}, u32[]{:S(2)}) collective-permute-start(bf16[128,4096]{1,0:T(8,128)(2,1)S(1)} %multiply_convert_fusion.refs_2_.a_ref.b_ref), channel_id=1, source_target_pairs={{0,1},{1,0},{2,3},{3,2},{4,5},{5,4},{6,7},{7,6},{8,9},{9,8},{10,11... | collective-permute-start | bytes 3145736 | tf_op jit(solution)/shard_map/ppermute | solution.py:523
  38.1 21.5 %collective-permute-start.6 = (bf16[128,4096]{1,0:T(8,128)(2,1)}, bf16[128,4096]{1,0:T(8,128)(2,1)}, u32[]{:S(2)}, u32[]{:S(2)}) collective-permute-start(bf16[128,4096]{1,0:T(8,128)(2,1)} %choose.4), channel_id=1, source_target_pairs={{1,2},{2,1},{5,6},{6,5},{9,10},{10,9},{13,14},{14,13},{17,18},{18,... | collective-permute-start | bytes 3145736 | tf_op jit(solution)/shard_map/ppermute | solution.py:523
  42.3 10.5 %collective-permute-start.3 = (bf16[256,1280]{1,0:T(8,128)(2,1)}, bf16[256,1280]{1,0:T(8,128)(2,1)S(1)}, u32[]{:S(2)}, u32[]{:S(2)}) collective-permute-start(bf16[256,1280]{1,0:T(8,128)(2,1)} %get-tuple-element.385.kva_ref), channel_id=1, source_target_pairs={{0,4},{4,0},{8,12},{12,8},{1,5},{5,1},{9,13},{13,9},{2,6},{6,2},{1... | collective-permute-start | bytes 1966088 | tf_op jit(solution)/shard_map/ppermute | solution.py:526
  42.4 10.5 %collective-permute-start.4 = (bf16[256,1280]{1,0:T(8,128)(2,1)}, bf16[256,1280]{1,0:T(8,128)(2,1)S(1)}, u32[]{:S(2)}, u32[]{:S(2)}) collective-permute-start(bf16[256,1280]{1,0:T(8,128)(2,1)} %get-tuple-element.386.kvb_ref), channel_id=1, source_target_pairs={{0,4},{4,0},{8,12},{12,8},{1,5},{5,1},{9,13},{13,9},{2,6},{6,2},{1... | collective-permute-start | bytes 1966088 | tf_op jit(solution)/shard_map/ppermute | solution.py:526
  59.6 27.2 %collective-permute-start.8 = (bf16[128,4096]{1,0:T(8,128)(2,1)}, bf16[128,4096]{1,0:T(8,128)(2,1)S(1)}, u32[]{:S(2)}, u32[]{:S(2)}) collective-permute-start(bf16[128,4096]{1,0:T(8,128)(2,1)} %collective-permute-done.6.refs_1_), channel_id=1, source_target_pairs={{1,0},{2,3},{5,4},{6,7},{9,8},{10,11},{13,12},{14,15},{17,16},{18,... | collective-permute-start | bytes 3145736 | tf_op jit(solution)/shard_map/ppermute | solution.py:523
  60.9 26.0 %collective-permute-start.11 = (bf16[128,4096]{1,0:T(8,128)(2,1)}, bf16[128,4096]{1,0:T(8,128)(2,1)S(1)}, u32[]{:S(2)}, u32[]{:S(2)}) collective-permute-start(bf16[128,4096]{1,0:T(8,128)(2,1)} %choose.5), channel_id=1, source_target_pairs={{1,2},{2,1},{5,6},{6,5},{9,10},{10,9},{13,14},{14,13},{17,18},{18,... | collective-permute-start | bytes 3145736 | tf_op jit(solution)/shard_map/ppermute | solution.py:523
  61.6 25.2 %collective-permute-start.5 = (bf16[256,1280]{1,0:T(8,128)(2,1)}, bf16[256,1280]{1,0:T(8,128)(2,1)S(1)}, u32[]{:S(2)}, u32[]{:S(2)}) collective-permute-start(bf16[256,1280]{1,0:T(8,128)(2,1)} %combine.4), channel_id=1, source_target_pairs={{0,8},{4,12},{8,0},{12,4},{1,9},{5,13},{9,1},{13,5},{2,10},{6,14},... | collective-permute-start | bytes 1966088 | tf_op jit(solution)/shard_map/ppermute | solution.py:529
  85.3 7.0 %collective-permute-start.9 = (bf16[256,1280]{1,0:T(8,128)(2,1)}, bf16[256,1280]{1,0:T(8,128)(2,1)S(1)}, u32[]{:S(2)}, u32[]{:S(2)}) collective-permute-start(bf16[256,1280]{1,0:T(8,128)(2,1)} %get-tuple-element.412.kva_ref), channel_id=1, source_target_pairs={{0,4},{4,0},{8,12},{12,8},{1,5},{5,1},{9,13},{13,9},{2,6},{6,2},{1... | collective-permute-start | bytes 1966088 | tf_op jit(solution)/shard_map/ppermute | solution.py:526
  85.4 6.9 %collective-permute-start.10 = (bf16[256,1280]{1,0:T(8,128)(2,1)}, bf16[256,1280]{1,0:T(8,128)(2,1)S(1)}, u32[]{:S(2)}, u32[]{:S(2)}) collective-permute-start(bf16[256,1280]{1,0:T(8,128)(2,1)} %get-tuple-element.413.kvb_ref), channel_id=1, source_target_pairs={{0,4},{4,0},{8,12},{12,8},{1,5},{5,1},{9,13},{13,9},{2,6},{6,2},{1... | collective-permute-start | bytes 1966088 | tf_op jit(solution)/shard_map/ppermute | solution.py:526
  86.9 29.8 %collective-permute-start.14 = (bf16[128,4096]{1,0:T(8,128)(2,1)S(1)}, bf16[128,4096]{1,0:T(8,128)(2,1)}, u32[]{:S(2)}, u32[]{:S(2)}) collective-permute-start(bf16[128,4096]{1,0:T(8,128)(2,1)S(1)} %collective-permute-done.11.refs_2_), channel_id=1, source_target_pairs={{1,0},{2,3},{5,4},{6,7},{9,8},{10,11},{13,12},{14,15},{17,16},{18,... | collective-permute-start | bytes 3145736 | tf_op jit(solution)/shard_map/ppermute | solution.py:523
  90.6 30.6 %collective-permute-start.12 = (bf16[128,4096]{1,0:T(8,128)(2,1)}, bf16[128,4096]{1,0:T(8,128)(2,1)}, u32[]{:S(2)}, u32[]{:S(2)}) collective-permute-start(bf16[128,4096]{1,0:T(8,128)(2,1)} %choose.6), channel_id=1, source_target_pairs={{1,2},{2,1},{5,6},{6,5},{9,10},{10,9},{13,14},{14,13},{17,18},{18,... | collective-permute-start | bytes 3145736 | tf_op jit(solution)/shard_map/ppermute | solution.py:523
  96.3 20.4 %collective-permute-start.13 = (bf16[256,1280]{1,0:T(8,128)(2,1)}, bf16[256,1280]{1,0:T(8,128)(2,1)}, u32[]{:S(2)}, u32[]{:S(2)}) collective-permute-start(bf16[256,1280]{1,0:T(8,128)(2,1)} %combine.5), channel_id=1, source_target_pairs={{0,8},{4,12},{8,0},{12,4},{1,9},{5,13},{9,1},{13,5},{2,10},{6,14},... | collective-permute-start | bytes 1966088 | tf_op jit(solution)/shard_map/ppermute | solution.py:529
  123.5 21.0 %collective-permute-start.15 = (bf16[128,4096]{1,0:T(8,128)(2,1)}, bf16[128,4096]{1,0:T(8,128)(2,1)S(1)}, u32[]{:S(2)}, u32[]{:S(2)}) collective-permute-start(bf16[128,4096]{1,0:T(8,128)(2,1)} %choose.7), channel_id=1, source_target_pairs={{1,2},{2,1},{5,6},{6,5},{9,10},{10,9},{13,14},{14,13},{17,18},{18,... | collective-permute-start | bytes 3145736 | tf_op jit(solution)/shard_map/ppermute | solution.py:523
  124.2 39.8 %collective-permute-start.20 = (bf16[128,4096]{1,0:T(8,128)(2,1)}, bf16[128,4096]{1,0:T(8,128)(2,1)S(1)}, u32[]{:S(2)}, u32[]{:S(2)}) collective-permute-start(bf16[128,4096]{1,0:T(8,128)(2,1)} %collective-permute-done.12.refs_3_), channel_id=1, source_target_pairs={{1,0},{2,3},{5,4},{6,7},{9,8},{10,11},{13,12},{14,15},{17,16},{18,... | collective-permute-start | bytes 3145736 | tf_op jit(solution)/shard_map/ppermute | solution.py:523
  144.0 20.1 %collective-permute-start.19 = (bf16[256,1024]{1,0:T(8,128)(2,1)}, bf16[256,1024]{1,0:T(8,128)(2,1)S(1)}, u32[]{:S(2)}, u32[]{:S(2)}) collective-permute-start(bf16[256,1024]{1,0:T(8,128)(2,1)} %attend.4.refs_1_), channel_id=1, source_target_pairs={{0,8},{4,12},{8,0},{12,4},{1,9},{5,13},{9,1},{13,5},{2,10},{6,14},... | collective-permute-start | bytes 1572872 | tf_op jit(solution)/shard_map/ppermute | solution.py:529
  144.5 22.3 %collective-permute-start.18 = (bf16[256,1024]{1,0:T(8,128)(2,1)}, bf16[256,1024]{1,0:T(8,128)(2,1)}, u32[]{:S(2)}, u32[]{:S(2)}) collective-permute-start(bf16[256,1024]{1,0:T(8,128)(2,1)} %attend.4.refs_1_), channel_id=1, source_target_pairs={{0,4},{4,0},{8,12},{12,8},{1,5},{5,1},{9,13},{13,9},{2,6},{6,2},{1... | collective-permute-start | bytes 1572872 | tf_op jit(solution)/shard_map/ppermute | solution.py:526
  162.8 35.8 %collective-permute-start.16 = (bf16[128,4096]{1,0:T(8,128)(2,1)S(1)}, bf16[128,4096]{1,0:T(8,128)(2,1)}, u32[]{:S(2)}, u32[]{:S(2)}) collective-permute-start(bf16[128,4096]{1,0:T(8,128)(2,1)S(1)} %collective-permute-done.15.refs_4_), channel_id=1, source_target_pairs={{1,0},{2,3},{5,4},{6,7},{9,8},{10,11},{13,12},{14,15},{17,16},{18,... | collective-permute-start | bytes 3145736 | tf_op jit(solution)/shard_map/ppermute | solution.py:523
  164.7 33.4 %collective-permute-start.17 = (bf16[256,1024]{1,0:T(8,128)(2,1)}, bf16[256,1024]{1,0:T(8,128)(2,1)S(1)}, u32[]{:S(2)}, u32[]{:S(2)}) collective-permute-start(bf16[256,1024]{1,0:T(8,128)(2,1)} %attend.5.refs_1_), channel_id=1, source_target_pairs={{0,8},{4,12},{8,0},{12,4},{1,9},{5,13},{9,1},{13,5},{2,10},{6,14},... | collective-permute-start | bytes 1572872 | tf_op jit(solution)/shard_map/ppermute | solution.py:529
  186.2 43.8 %collective-permute-start.26 = (bf16[256,2048]{1,0:T(8,128)(2,1)}, bf16[256,2048]{1,0:T(8,128)(2,1)S(1)}, u32[]{:S(2)}, u32[]{:S(2)}) collective-permute-start(bf16[256,2048]{1,0:T(8,128)(2,1)} %get-tuple-element.508.b_ref), channel_id=1, source_target_pairs={{0,1},{3,2},{4,5},{7,6},{8,9},{11,10},{12,13},{15,14},{16,17},{19,... | collective-permute-start | bytes 3145736 | tf_op jit(solution)/shard_map/ppermute | solution.py:523
  198.0 30.3 %collective-permute-start.27 = (bf16[256,1024]{1,0:T(8,128)(2,1)S(1)}, bf16[256,1024]{1,0:T(8,128)(2,1)S(1)}, u32[]{:S(2)}, u32[]{:S(2)}) collective-permute-start(bf16[256,1024]{1,0:T(8,128)(2,1)S(1)} %copy-done.14), channel_id=1, source_target_pairs={{0,4},{4,0},{8,12},{12,8},{1,5},{5,1},{9,13},{13,9},{2,6},{6,2},{1... | collective-permute-start | bytes 1572872 | tf_op jit(solution)/shard_map/ppermute | solution.py:526
  198.1 31.8 %collective-permute-start.28 = (bf16[256,1024]{1,0:T(8,128)(2,1)S(1)}, bf16[256,1024]{1,0:T(8,128)(2,1)S(1)}, u32[]{:S(2)}, u32[]{:S(2)}) collective-permute-start(bf16[256,1024]{1,0:T(8,128)(2,1)S(1)} %collective-permute-done.17.refs_3_), channel_id=1, source_target_pairs={{0,4},{4,0},{8,12},{12,8},{1,5},{5,1},{9,13},{13,9},{2,6},{6,2},{1... | collective-permute-start | bytes 1572872 | tf_op jit(solution)/shard_map/ppermute | solution.py:526
  228.3 25.3 %collective-permute-start.30 = (bf16[256,2048]{1,0:T(8,128)(2,1)S(1)}, bf16[256,2048]{1,0:T(8,128)(2,1)S(1)}, u32[]{:S(2)}, u32[]{:S(2)}) collective-permute-start(bf16[256,2048]{1,0:T(8,128)(2,1)S(1)} %copy-done.2), channel_id=1, source_target_pairs={{0,1},{3,2},{4,5},{7,6},{8,9},{11,10},{12,13},{15,14},{16,17},{19,... | collective-permute-start | bytes 3145736 | tf_op jit(solution)/shard_map/ppermute | solution.py:523
  234.5 19.2 %collective-permute-start.29 = (bf16[256,1280]{1,0:T(8,128)(2,1)}, bf16[256,1280]{1,0:T(8,128)(2,1)S(1)}, u32[]{:S(2)}, u32[]{:S(2)}) collective-permute-start(bf16[256,1280]{1,0:T(8,128)(2,1)} %combine.6), channel_id=1, source_target_pairs={{0,8},{4,12},{8,0},{12,4},{1,9},{5,13},{9,1},{13,5},{2,10},{6,14},... | collective-permute-start | bytes 1966088 | tf_op jit(solution)/shard_map/ppermute | solution.py:529
  239.4 36.5 %collective-permute-start.33 = (bf16[256,1280]{1,0:T(8,128)(2,1)}, bf16[256,1280]{1,0:T(8,128)(2,1)S(1)}, u32[]{:S(2)}, u32[]{:S(2)}) collective-permute-start(bf16[256,1280]{1,0:T(8,128)(2,1)} %combine.7), channel_id=1, source_target_pairs={{0,8},{4,12},{8,0},{12,4},{1,9},{5,13},{9,1},{13,5},{2,10},{6,14},... | collective-permute-start | bytes 1966088 | tf_op jit(solution)/shard_map/ppermute | solution.py:529
  275.0 22.2 %collective-permute-start.32 = (bf16[256,1024]{1,0:T(8,128)(2,1)}, bf16[256,1024]{1,0:T(8,128)(2,1)S(1)}, u32[]{:S(2)}, u32[]{:S(2)}) collective-permute-start(bf16[256,1024]{1,0:T(8,128)(2,1)} %attend.6.refs_1_), channel_id=1, source_target_pairs={{0,8},{4,12},{8,0},{12,4},{1,9},{5,13},{9,1},{13,5},{2,10},{6,14},... | collective-permute-start | bytes 1572872 | tf_op jit(solution)/shard_map/ppermute | solution.py:529
  275.9 23.0 %collective-permute-start.31 = (bf16[256,1024]{1,0:T(8,128)(2,1)}, bf16[256,1024]{1,0:T(8,128)(2,1)S(1)}, u32[]{:S(2)}, u32[]{:S(2)}) collective-permute-start(bf16[256,1024]{1,0:T(8,128)(2,1)} %attend.6.refs_1_), channel_id=1, source_target_pairs={{0,4},{4,0},{8,12},{12,8},{1,5},{5,1},{9,13},{13,9},{2,6},{6,2},{1... | collective-permute-start | bytes 1572872 | tf_op jit(solution)/shard_map/ppermute | solution.py:526
  297.8 25.7 %collective-permute-start.37 = (bf16[256,1024]{1,0:T(8,128)(2,1)}, bf16[256,1024]{1,0:T(8,128)(2,1)S(1)}, u32[]{:S(2)}, u32[]{:S(2)}) collective-permute-start(bf16[256,1024]{1,0:T(8,128)(2,1)} %attend.7.refs_1_), channel_id=1, source_target_pairs={{0,8},{4,12},{8,0},{12,4},{1,9},{5,13},{9,1},{13,5},{2,10},{6,14},... | collective-permute-start | bytes 1572872 | tf_op jit(solution)/shard_map/ppermute | solution.py:529
  320.0 27.5 %collective-permute-start.35 = (bf16[256,2048]{1,0:T(8,128)(2,1)}, bf16[256,2048]{1,0:T(8,128)(2,1)S(1)}, u32[]{:S(2)}, u32[]{:S(2)}) collective-permute-start(bf16[256,2048]{1,0:T(8,128)(2,1)} %get-tuple-element.572.b_ref), channel_id=1, source_target_pairs={{0,1},{3,2},{4,5},{7,6},{8,9},{11,10},{12,13},{15,14},{16,17},{19,... | collective-permute-start | bytes 3145736 | tf_op jit(solution)/shard_map/ppermute | solution.py:523
  324.0 45.7 %collective-permute-start.42 = (bf16[256,2048]{1,0:T(8,128)(2,1)}, bf16[256,2048]{1,0:T(8,128)(2,1)S(1)}, u32[]{:S(2)}, u32[]{:S(2)}) collective-permute-start(bf16[256,2048]{1,0:T(8,128)(2,1)} %get-tuple-element.601.b_ref), channel_id=1, source_target_pairs={{0,1},{3,2},{4,5},{7,6},{8,9},{11,10},{12,13},{15,14},{16,17},{19,... | collective-permute-start | bytes 3145736 | tf_op jit(solution)/shard_map/ppermute | solution.py:523
  346.2 45.9 %collective-permute-start.45 = (bf16[256,2048]{1,0:T(8,128)(2,1)}, bf16[256,2048]{1,0:T(8,128)(2,1)S(1)}, u32[]{:S(2)}, u32[]{:S(2)}) collective-permute-start(bf16[256,2048]{1,0:T(8,128)(2,1)} %get-tuple-element.617.b_ref), channel_id=1, source_target_pairs={{0,1},{3,2},{4,5},{7,6},{8,9},{11,10},{12,13},{15,14},{16,17},{19,... | collective-permute-start | bytes 3145736 | tf_op jit(solution)/shard_map/ppermute | solution.py:523
  350.6 25.6 %collective-permute-start.41 = (bf16[256,1024]{1,0:T(8,128)(2,1)}, bf16[256,1024]{1,0:T(8,128)(2,1)S(1)}, u32[]{:S(2)}, u32[]{:S(2)}) collective-permute-start(bf16[256,1024]{1,0:T(8,128)(2,1)} %add.209), channel_id=1, source_target_pairs={{1,2},{2,1},{5,6},{6,5},{9,10},{10,9},{13,14},{14,13},{17,18},{18,... | collective-permute-start | bytes 1572872 | tf_op jit(solution)/shard_map/ppermute | solution.py:523
  353.5 35.3 %collective-permute-start.40 = (bf16[256,1024]{1,0:T(8,128)(2,1)}, bf16[256,1024]{1,0:T(8,128)(2,1)S(1)}, u32[]{:S(2)}, u32[]{:S(2)}) collective-permute-start(bf16[256,1024]{1,0:T(8,128)(2,1)} %add.210), channel_id=1, source_target_pairs={{1,2},{2,1},{5,6},{6,5},{9,10},{10,9},{13,14},{14,13},{17,18},{18,... | collective-permute-start | bytes 1572872 | tf_op jit(solution)/shard_map/ppermute | solution.py:523
  374.9 23.8 %collective-permute-start.48 = (bf16[256,1024]{1,0:T(8,128)(2,1)}, bf16[256,1024]{1,0:T(8,128)(2,1)S(1)}, u32[]{:S(2)}, u32[]{:S(2)}) collective-permute-start(bf16[256,1024]{1,0:T(8,128)(2,1)} %add.212), channel_id=1, source_target_pairs={{1,2},{2,1},{5,6},{6,5},{9,10},{10,9},{13,14},{14,13},{17,18},{18,... | collective-permute-start | bytes 1572872 | tf_op jit(solution)/shard_map/ppermute | solution.py:523
  375.5 23.9 %collective-permute-start.49 = (bf16[256,1024]{1,0:T(8,128)(2,1)}, bf16[256,1024]{1,0:T(8,128)(2,1)S(1)}, u32[]{:S(2)}, u32[]{:S(2)}) collective-permute-start(bf16[256,1024]{1,0:T(8,128)(2,1)} %add.211), channel_id=1, source_target_pairs={{1,2},{2,1},{5,6},{6,5},{9,10},{10,9},{13,14},{14,13},{17,18},{18,... | collective-permute-start | bytes 1572872 | tf_op jit(solution)/shard_map/ppermute | solution.py:523
  376.3 37.2 %collective-permute-start.39 = (bf16[256,2048]{1,0:T(8,128)(2,1)S(1)}, bf16[256,2048]{1,0:T(8,128)(2,1)S(1)}, u32[]{:S(2)}, u32[]{:S(2)}) collective-permute-start(bf16[256,2048]{1,0:T(8,128)(2,1)S(1)} %copy-done.15), channel_id=1, source_target_pairs={{0,1},{3,2},{4,5},{7,6},{8,9},{11,10},{12,13},{15,14},{16,17},{19,... | collective-permute-start | bytes 3145736 | tf_op jit(solution)/shard_map/ppermute | solution.py:523
  395.2 10.0 %collective-permute-start.47 = (bf16[256,1024]{1,0:T(8,128)(2,1)}, bf16[256,1024]{1,0:T(8,128)(2,1)S(1)}, u32[]{:S(2)}, u32[]{:S(2)}) collective-permute-start(bf16[256,1024]{1,0:T(8,128)(2,1)} %add.215), channel_id=1, source_target_pairs={{1,2},{2,1},{5,6},{6,5},{9,10},{10,9},{13,14},{14,13},{17,18},{18,... | collective-permute-start | bytes 1572872 | tf_op jit(solution)/shard_map/ppermute | solution.py:523
  398.0 10.9 %collective-permute-start.46 = (bf16[256,1024]{1,0:T(8,128)(2,1)}, bf16[256,1024]{1,0:T(8,128)(2,1)S(1)}, u32[]{:S(2)}, u32[]{:S(2)}) collective-permute-start(bf16[256,1024]{1,0:T(8,128)(2,1)} %add.216), channel_id=1, source_target_pairs={{1,2},{2,1},{5,6},{6,5},{9,10},{10,9},{13,14},{14,13},{17,18},{18,... | collective-permute-start | bytes 1572872 | tf_op jit(solution)/shard_map/ppermute | solution.py:523
  398.7 13.2 %collective-permute-start.44 = (bf16[256,1024]{1,0:T(8,128)(2,1)S(1)}, bf16[256,1024]{1,0:T(8,128)(2,1)S(1)}, u32[]{:S(2)}, u32[]{:S(2)}) collective-permute-start(bf16[256,1024]{1,0:T(8,128)(2,1)S(1)} %copy-done.56), channel_id=1, source_target_pairs={{1,0},{5,4},{9,8},{13,12},{17,16},{21,20},{25,24},{29,28}} | collective-permute-start | bytes 1572872 | tf_op jit(solution)/shard_map/ppermute | solution.py:523
  399.5 12.4 %collective-permute-start.43 = (bf16[256,1024]{1,0:T(8,128)(2,1)S(1)}, bf16[256,1024]{1,0:T(8,128)(2,1)}, u32[]{:S(2)}, u32[]{:S(2)}) collective-permute-start(bf16[256,1024]{1,0:T(8,128)(2,1)S(1)} %copy-done.57), channel_id=1, source_target_pairs={{1,0},{5,4},{9,8},{13,12},{17,16},{21,20},{25,24},{29,28}} | collective-permute-start | bytes 1572872 | tf_op jit(solution)/shard_map/ppermute | solution.py:523
  405.2 15.6 %collective-permute-start.53 = (bf16[256,1024]{1,0:T(8,128)(2,1)}, bf16[256,1024]{1,0:T(8,128)(2,1)}, u32[]{:S(2)}, u32[]{:S(2)}) collective-permute-start(bf16[256,1024]{1,0:T(8,128)(2,1)} %add.217), channel_id=1, source_target_pairs={{1,0},{5,4},{9,8},{13,12},{17,16},{21,20},{25,24},{29,28}} | collective-permute-start | bytes 1572872 | tf_op jit(solution)/shard_map/ppermute | solution.py:523
  416.6 6.8 %collective-permute-start.52 = (bf16[256,1024]{1,0:T(8,128)(2,1)}, bf16[256,1024]{1,0:T(8,128)(2,1)S(1)}, u32[]{:S(2)}, u32[]{:S(2)}) collective-permute-start(bf16[256,1024]{1,0:T(8,128)(2,1)} %add.221), channel_id=1, source_target_pairs={{1,2},{2,1},{5,6},{6,5},{9,10},{10,9},{13,14},{14,13},{17,18},{18,... | collective-permute-start | bytes 1572872 | tf_op jit(solution)/shard_map/ppermute | solution.py:523
  417.3 9.1 %collective-permute-start.51 = (bf16[256,1024]{1,0:T(8,128)(2,1)S(1)}, bf16[256,1024]{1,0:T(8,128)(2,1)S(1)}, u32[]{:S(2)}, u32[]{:S(2)}) collective-permute-start(bf16[256,1024]{1,0:T(8,128)(2,1)S(1)} %copy-done.55), channel_id=1, source_target_pairs={{1,0},{5,4},{9,8},{13,12},{17,16},{21,20},{25,24},{29,28}} | collective-permute-start | bytes 1572872 | tf_op jit(solution)/shard_map/ppermute | solution.py:523
  420.1 6.2 %collective-permute-start.50 = (bf16[256,1024]{1,0:T(8,128)(2,1)}, bf16[256,1024]{1,0:T(8,128)(2,1)S(1)}, u32[]{:S(2)}, u32[]{:S(2)}) collective-permute-start(bf16[256,1024]{1,0:T(8,128)(2,1)} %add.222), channel_id=1, source_target_pairs={{1,2},{2,1},{5,6},{6,5},{9,10},{10,9},{13,14},{14,13},{17,18},{18,... | collective-permute-start | bytes 1572872 | tf_op jit(solution)/shard_map/ppermute | solution.py:523
  420.8 36.4 %collective-permute-start.54 = (bf16[256,1024]{1,0:T(8,128)(2,1)S(1)}, bf16[256,1024]{1,0:T(8,128)(2,1)}, u32[]{:S(2)}, u32[]{:S(2)}) collective-permute-start(bf16[256,1024]{1,0:T(8,128)(2,1)S(1)} %copy-done.54), channel_id=1, source_target_pairs={{2,3},{6,7},{10,11},{14,15},{18,19},{22,23},{26,27},{30,31}} | collective-permute-start | bytes 1572872 | tf_op jit(solution)/shard_map/ppermute | solution.py:523
  422.1 45.5 %collective-permute-start.55 = (bf16[256,1024]{1,0:T(8,128)(2,1)}, bf16[256,1024]{1,0:T(8,128)(2,1)}, u32[]{:S(2)}, u32[]{:S(2)}) collective-permute-start(bf16[256,1024]{1,0:T(8,128)(2,1)} %add.220), channel_id=1, source_target_pairs={{2,3},{6,7},{10,11},{14,15},{18,19},{22,23},{26,27},{30,31}} | collective-permute-start | bytes 1572872 | tf_op jit(solution)/shard_map/ppermute | solution.py:523
  429.3 49.5 %collective-permute-start.56 = (bf16[256,1024]{1,0:T(8,128)(2,1)}, bf16[256,1024]{1,0:T(8,128)(2,1)}, u32[]{:S(2)}, u32[]{:S(2)}) collective-permute-start(bf16[256,1024]{1,0:T(8,128)(2,1)} %add.223), channel_id=1, source_target_pairs={{2,3},{6,7},{10,11},{14,15},{18,19},{22,23},{26,27},{30,31}} | collective-permute-start | bytes 1572872 | tf_op jit(solution)/shard_map/ppermute | solution.py:523
  430.7 54.5 %collective-permute-start.57 = (bf16[256,1024]{1,0:T(8,128)(2,1)}, bf16[256,1024]{1,0:T(8,128)(2,1)}, u32[]{:S(2)}, u32[]{:S(2)}) collective-permute-start(bf16[256,1024]{1,0:T(8,128)(2,1)} %add.224), channel_id=1, source_target_pairs={{2,3},{6,7},{10,11},{14,15},{18,19},{22,23},{26,27},{30,31}} | collective-permute-start | bytes 1572872 | tf_op jit(solution)/shard_map/ppermute | solution.py:523
  (73 other events, 704.7 us)
